TPU v7x, 32 devices: a whole 2x2x4 slice. The times are simulated.
32 devices in a mesh: dp: 8 (over y, x, core), seq: 4 (over z).
Axes of the slice: x: 2, y: 2, z: 4, core: 2. Of those that a mesh axis runs over, the one named last changes fastest.
Arguments:
- patches: bfloat16 [32, 1024, 768], P('dp', 'seq'), may hold values from -6 to 6
- captions: bfloat16 [32, 64, 768], P('dp', 'seq'), may hold values from -6 to 6
- pairs: int32 [32, 32], replicated, may hold values from 0 to 1, as said below
- image_attend_in: bfloat16 [768, 2304], P(('dp', 'seq')), may hold values from -0.21875 to 0.21875
- image_attend_out: bfloat16 [768, 768], P(('dp', 'seq')), may hold values from -0.875 to 0.875
- image_up_weight: bfloat16 [768, 3072], P(('dp', 'seq')), may hold values from -0.21875 to 0.21875
- image_up_bias: bfloat16 [3072], P(('dp', 'seq')), may hold values from -3 to 3
- image_down_weight: bfloat16 [3072, 768], P(('dp', 'seq')), may hold values from -0.109375 to 0.109375
- image_vectors: bfloat16 [11, 768], P(None, ('dp', 'seq')), may hold values from -3.5 to 3.5, as said below
- probe_query_weight: bfloat16 [768, 768], P(('dp', 'seq')), may hold values from -0.21875 to 0.21875
- probe_pair_weight: bfloat16 [768, 1536], P(('dp', 'seq')), may hold values from -0.21875 to 0.21875
- probe_out_weight: bfloat16 [768, 768], P(('dp', 'seq')), may hold values from -0.21875 to 0.21875
- probe_up_weight: bfloat16 [768, 3072], P(('dp', 'seq')), may hold values from -0.21875 to 0.21875
- probe_up_bias: bfloat16 [3072], P(('dp', 'seq')), may hold values from -3 to 3
- probe_down_weight: bfloat16 [3072, 768], P(('dp', 'seq')), may hold values from -0.109375 to 0.109375
- text_attend_in: bfloat16 [768, 2304], P(('dp', 'seq')), may hold values from -0.21875 to 0.21875
- text_attend_out: bfloat16 [768, 768], P(('dp', 'seq')), may hold values from -0.4375 to 0.4375
- text_up_weight: bfloat16 [768, 3072], P(('dp', 'seq')), may hold values from -0.21875 to 0.21875
- text_up_bias: bfloat16 [3072], P(('dp', 'seq')), may hold values from -3 to 3
- text_down_weight: bfloat16 [3072, 768], P(('dp', 'seq')), may hold values from -0.109375 to 0.109375
- text_vectors: bfloat16 [7, 768], P(None, ('dp', 'seq')), may hold values from -1 to 1.6, as said below
- text_head_weight: bfloat16 [768, 768], P(('dp', 'seq')), may hold values from -0.21875 to 0.21875
- temp_bias: float32 [2], replicated, may hold values from -3 to 2.5, as said below
Outputs:
- loss: float32 [], replicated
- grad_patches: float32 [32, 1024, 768], P('dp', 'seq')
- grad_captions: float32 [32, 64, 768], P('dp', 'seq')
- grad_image_attend_in: float32 [768, 2304], P(('dp', 'seq'))
- grad_image_attend_out: float32 [768, 768], P(('dp', 'seq'))
- grad_image_up_weight: float32 [768, 3072], P(('dp', 'seq'))
- grad_image_up_bias: float32 [3072], P(('dp', 'seq'))
- grad_image_down_weight: float32 [3072, 768], P(('dp', 'seq'))
- grad_image_vectors: float32 [11, 768], P(None, ('dp', 'seq'))
- grad_probe_query_weight: float32 [768, 768], P(('dp', 'seq'))
- grad_probe_pair_weight: float32 [768, 1536], P(('dp', 'seq'))
- grad_probe_out_weight: float32 [768, 768], P(('dp', 'seq'))
- grad_probe_up_weight: float32 [768, 3072], P(('dp', 'seq'))
- grad_probe_up_bias: float32 [3072], P(('dp', 'seq'))
- grad_probe_down_weight: float32 [3072, 768], P(('dp', 'seq'))
- grad_text_attend_in: float32 [768, 2304], P(('dp', 'seq'))
- grad_text_attend_out: float32 [768, 768], P(('dp', 'seq'))
- grad_text_up_weight: float32 [768, 3072], P(('dp', 'seq'))
- grad_text_up_bias: float32 [3072], P(('dp', 'seq'))
- grad_text_down_weight: float32 [3072, 768], P(('dp', 'seq'))
- grad_text_vectors: float32 [7, 768], P(None, ('dp', 'seq'))
- grad_text_head_weight: float32 [768, 768], P(('dp', 'seq'))
- grad_temp_bias: float32 [2], replicated
Inputs may be any that keep to these rules, and one draw needn't show every extreme that they name: `pairs`: each image has between 2 and 5 positive captions; some image has exactly 2 and some exactly 5. `image_vectors`: gain rows lie near 1, shift and bias rows near 0, the probe row is of order one. `text_vectors`: gain rows lie near 1, shift and bias rows near 0. `temp_bias`: t between 1.5 and 2.5, bias between -3 and -1.
All inputs are finite; a program needn't handle non-finite values.
Results may differ from a plain program's by a relative error of at most 0.014.
Values may be sent and summed in bfloat16 or wider, within the bound.
A program may use at most 320 MiB of HBM per device.

v0:
```python
from functools import partial

import jax
import jax.numpy as jnp
from jax import lax
from jax.sharding import PartitionSpec as P

HEADS = 12


exact_mode = lax.Precision.HIGHEST
epsilon = 1e-06


def combined_all(value, axis, join):
    pieces = jax.tree.map(lambda part: lax.all_gather(part, axis), value)
    head = jax.tree.map(lambda part: part[0], pieces)
    tail = jax.tree.map(lambda part: part[1:], pieces)
    running, _ = lax.scan(lambda running, section: (join(running, section), None), head, tail)
    return running


def spread_2(value, axis, source):
    kept = jnp.where(lax.axis_index(axis) == source, value, 0).astype(value.dtype)
    return lax.psum(kept, axis)


def layer_norm(inputs, gain, shift):
    center = inputs - jnp.mean(inputs, -1, keepdims=True)
    spread = jnp.mean(center * center, -1, keepdims=True)
    return center * lax.rsqrt(spread + epsilon) * gain + shift


def norm_back(inputs, gain, shift, upstream):
    unused, pullback = jax.vjp(layer_norm, inputs, gain, shift)
    return pullback(upstream)


def project_rows(left, right):
    return jnp.einsum("...d,de->...e", left, right, preferred_element_type=jnp.float32)


def normalize(rows):
    return rows * lax.rsqrt(jnp.sum(rows * rows, -1, keepdims=True) + epsilon)


def sigmoid_loss(image_rows, text_rows, temp_bias, labels):
    logits = (
        jnp.dot(normalize(image_rows), normalize(text_rows).T, precision=exact_mode)
        * jnp.exp(temp_bias[0])
        + temp_bias[1]
    )
    return -jnp.sum(jax.nn.log_sigmoid(labels * logits)) / image_rows.shape[0]


def attend_forward(queries, keys, values):
    factor = queries.shape[-1] ** (-0.5)
    scores = jnp.einsum("thd,shd->hts", queries, keys, preferred_element_type=jnp.float32) * factor
    highest = jnp.max(scores, -1, keepdims=True)
    weights = jnp.exp(scores - highest)
    totals = jnp.sum(weights, -1, keepdims=True)
    probs = (weights / totals).astype(jnp.bfloat16)
    output = jnp.einsum("hts,shd->thd", probs, values, preferred_element_type=jnp.float32)
    return (output, highest + jnp.log(totals))


def attend_backward(queries, keys, values, logsum, upstream):
    factor = queries.shape[-1] ** (-0.5)
    scores = jnp.einsum("thd,shd->hts", queries, keys, preferred_element_type=jnp.float32) * factor
    probs = jnp.exp(scores - logsum)
    d_values = jnp.einsum(
        "hts,thd->shd", probs.astype(jnp.bfloat16), upstream, preferred_element_type=jnp.float32
    )
    d_probs = jnp.einsum("thd,shd->hts", upstream, values, preferred_element_type=jnp.float32)
    inner = jnp.sum(probs * d_probs, -1, keepdims=True)
    d_scores = (probs * (d_probs - inner)).astype(jnp.bfloat16)
    d_queries = (
        jnp.einsum("hts,shd->thd", d_scores, keys, preferred_element_type=jnp.float32) * factor
    )
    d_keys = (
        jnp.einsum("hts,thd->shd", d_scores, queries, preferred_element_type=jnp.float32) * factor
    )
    return (d_queries, d_keys, d_values)


def block_forward(inputs, weights, gather_pair):
    attend_in, attend_out, up_weight, up_bias, down_weight, vectors = weights
    vec_float = vectors.astype(jnp.float32)
    number, length, features = inputs.shape
    head_width = features // HEADS
    normed = layer_norm(inputs, vec_float[0], vec_float[1]).astype(jnp.bfloat16)
    projected = project_rows(normed, attend_in).astype(jnp.bfloat16)
    queries = projected[..., :features].reshape(number, length, HEADS, head_width)
    gathered = gather_pair(projected[..., features:])
    spread_len = gathered.shape[1]
    keys = gathered[..., :features].reshape(number, spread_len, HEADS, head_width)
    values = gathered[..., features:].reshape(number, spread_len, HEADS, head_width)
    attended, logsum = lax.map(lambda items: attend_forward(*items), (queries, keys, values))
    mixed = attended.reshape(number, length, features).astype(jnp.bfloat16)
    hidden = inputs + project_rows(mixed, attend_out)
    second = layer_norm(hidden, vec_float[2], vec_float[3]).astype(jnp.bfloat16)
    upper = project_rows(second, up_weight) + up_bias.astype(jnp.float32)
    active = jax.nn.gelu(upper, approximate=True).astype(jnp.bfloat16)
    output = hidden + (project_rows(active, down_weight) + vec_float[4])
    saved = (normed, queries, keys, values, logsum, mixed, hidden, second, upper, active)
    return (output, saved)


def block_backward(inputs, weights, saved, upstream, scatter_pair):
    attend_in, attend_out, up_weight, up_bias, down_weight, vectors = weights
    normed, queries, keys, values, logsum, mixed, hidden, second, upper, active = saved
    vec_float = vectors.astype(jnp.float32)
    number, length, features = inputs.shape
    spread_len = keys.shape[1]
    d_branch = upstream.astype(jnp.bfloat16)
    grad_down = jnp.einsum("btf,btd->fd", active, d_branch, preferred_element_type=jnp.float32)
    grad_down_bias = jnp.sum(d_branch.astype(jnp.float32), (0, 1))
    d_active = jnp.einsum("btd,fd->btf", d_branch, down_weight, preferred_element_type=jnp.float32)
    unused, gelu_pull = jax.vjp(partial(jax.nn.gelu, approximate=True), upper)
    d_upper = gelu_pull(d_active)[0].astype(jnp.bfloat16)
    grad_up = jnp.einsum("btd,btf->df", second, d_upper, preferred_element_type=jnp.float32)
    grad_up_bias = jnp.sum(d_upper.astype(jnp.float32), (0, 1))
    d_second = jnp.einsum("btf,df->btd", d_upper, up_weight, preferred_element_type=jnp.float32)
    d_hidden_norm, grad_gain_two, grad_shift_two = norm_back(
        hidden, vec_float[2], vec_float[3], d_second
    )
    d_hidden = upstream + d_hidden_norm
    d_attend = d_hidden.astype(jnp.bfloat16)
    grad_out = jnp.einsum("btd,bte->de", mixed, d_attend, preferred_element_type=jnp.float32)
    d_mixed = jnp.einsum("bte,de->btd", d_attend, attend_out, preferred_element_type=jnp.float32)
    d_mixed = d_mixed.astype(jnp.bfloat16).reshape(queries.shape)
    d_queries, d_keys, d_values = lax.map(
        lambda items: attend_backward(*items), (queries, keys, values, logsum, d_mixed)
    )
    d_pair = jnp.concatenate(
        [
            d_keys.reshape(number, spread_len, features),
            d_values.reshape(number, spread_len, features),
        ],
        -1,
    )
    d_local = scatter_pair(d_pair)
    d_projected = jnp.concatenate(
        [d_queries.reshape(number, length, features), d_local], -1
    ).astype(jnp.bfloat16)
    grad_in = jnp.einsum("btd,bte->de", normed, d_projected, preferred_element_type=jnp.float32)
    d_normed = jnp.einsum("bte,de->btd", d_projected, attend_in, preferred_element_type=jnp.float32)
    d_inputs_norm, grad_gain_one, grad_shift_one = norm_back(
        inputs, vec_float[0], vec_float[1], d_normed
    )
    grad_vectors = jnp.stack(
        [grad_gain_one, grad_shift_one, grad_gain_two, grad_shift_two, grad_down_bias]
    )
    return (
        d_hidden + d_inputs_norm,
        (grad_in, grad_out, grad_up, grad_up_bias, grad_down, grad_vectors),
    )


def head_forward(pooled, out_weight, up_weight, up_bias, down_weight, vec_float):
    start_rows = jnp.dot(pooled, out_weight.astype(jnp.float32), precision=exact_mode)
    head_normed = layer_norm(start_rows, vec_float[8], vec_float[9]).astype(jnp.bfloat16)
    head_upper = jnp.dot(
        head_normed, up_weight, preferred_element_type=jnp.float32
    ) + up_bias.astype(jnp.float32)
    head_active = jax.nn.gelu(head_upper, approximate=True).astype(jnp.bfloat16)
    embed = start_rows + (
        jnp.dot(head_active, down_weight, preferred_element_type=jnp.float32) + vec_float[10]
    )
    return (embed, (start_rows, head_normed, head_upper, head_active))


def head_backward(pooled, out_weight, up_weight, down_weight, vec_float, head_saved, upstream):
    start_rows, head_normed, head_upper, head_active = head_saved
    grad_down = jnp.dot(head_active.astype(jnp.float32).T, upstream, precision=exact_mode)
    grad_down_bias = jnp.sum(upstream, 0)
    d_active = jnp.dot(upstream, down_weight.astype(jnp.float32).T, precision=exact_mode)
    unused, gelu_pull = jax.vjp(partial(jax.nn.gelu, approximate=True), head_upper)
    d_upper = gelu_pull(d_active)[0]
    grad_up = jnp.dot(head_normed.astype(jnp.float32).T, d_upper, precision=exact_mode)
    grad_up_bias = jnp.sum(d_upper, 0)
    d_normed = jnp.dot(d_upper, up_weight.astype(jnp.float32).T, precision=exact_mode)
    d_start_norm, grad_gain, grad_shift = norm_back(
        start_rows, vec_float[8], vec_float[9], d_normed
    )
    d_start = upstream + d_start_norm
    grad_out = jnp.dot(pooled.T, d_start, precision=exact_mode)
    d_pooled = jnp.dot(d_start, out_weight.astype(jnp.float32).T, precision=exact_mode)
    return (
        d_pooled,
        (grad_out, grad_up, grad_up_bias, grad_down, grad_gain, grad_shift, grad_down_bias),
    )


def gather_image_pair(pair):
    return lax.all_gather(pair, "seq", axis=1, tiled=True)


def gather_text_pair(pair):
    return lax.all_gather(pair, "seq", axis=1, tiled=True)


def scatter_image_pair(pair):
    return lax.psum_scatter(
        pair.astype(jnp.bfloat16), "seq", scatter_dimension=1, tiled=True
    ).astype(jnp.float32)


def scatter_text_pair(pair):
    return lax.psum_scatter(
        pair.astype(jnp.bfloat16), "seq", scatter_dimension=1, tiled=True
    ).astype(jnp.float32)


def merge_softmax(first, second):
    highest = jnp.maximum(first[0], second[0])
    left_scale = jnp.exp(first[0] - highest)
    right_scale = jnp.exp(second[0] - highest)
    totals = first[1] * left_scale + second[1] * right_scale
    sums = first[2] * left_scale[..., None] + second[2] * right_scale[..., None]
    return (highest, totals, sums)


def merge_pool(local_top, local_total, local_sums):
    return combined_all((local_top, local_total, local_sums), "seq", merge_softmax)


def per_device(
    patches,
    captions,
    pairs,
    image_attend_in,
    image_attend_out,
    image_up_weight,
    image_up_bias,
    image_down_weight,
    image_vectors,
    probe_query_weight,
    probe_pair_weight,
    probe_out_weight,
    probe_up_weight,
    probe_up_bias,
    probe_down_weight,
    text_attend_in,
    text_attend_out,
    text_up_weight,
    text_up_bias,
    text_down_weight,
    text_vectors,
    text_head_weight,
    temp_bias,
):
    image_full = (
        lax.all_gather(image_attend_in, ("dp", "seq"), axis=0, tiled=True),
        lax.all_gather(image_attend_out, ("dp", "seq"), axis=0, tiled=True),
        lax.all_gather(image_up_weight, ("dp", "seq"), axis=0, tiled=True),
        lax.all_gather(image_up_bias, ("dp", "seq"), axis=0, tiled=True),
        lax.all_gather(image_down_weight, ("dp", "seq"), axis=0, tiled=True),
        lax.all_gather(image_vectors, ("dp", "seq"), axis=1, tiled=True),
        lax.all_gather(probe_query_weight, ("dp", "seq"), axis=0, tiled=True),
        lax.all_gather(probe_pair_weight, ("dp", "seq"), axis=0, tiled=True),
        lax.all_gather(probe_out_weight, ("dp", "seq"), axis=0, tiled=True),
        lax.all_gather(probe_up_weight, ("dp", "seq"), axis=0, tiled=True),
        lax.all_gather(probe_up_bias, ("dp", "seq"), axis=0, tiled=True),
        lax.all_gather(probe_down_weight, ("dp", "seq"), axis=0, tiled=True),
    )
    text_full = (
        lax.all_gather(text_attend_in, ("dp", "seq"), axis=0, tiled=True),
        lax.all_gather(text_attend_out, ("dp", "seq"), axis=0, tiled=True),
        lax.all_gather(text_up_weight, ("dp", "seq"), axis=0, tiled=True),
        lax.all_gather(text_up_bias, ("dp", "seq"), axis=0, tiled=True),
        lax.all_gather(text_down_weight, ("dp", "seq"), axis=0, tiled=True),
        lax.all_gather(text_vectors, ("dp", "seq"), axis=1, tiled=True),
        lax.all_gather(text_head_weight, ("dp", "seq"), axis=0, tiled=True),
    )
    seq_index = lax.axis_index("seq")
    seq_count = lax.axis_size("seq")
    image_in = patches.astype(jnp.float32)
    text_in = captions.astype(jnp.float32)
    head_mask = (seq_index == 0).astype(jnp.float32)
    text_mask = (seq_index == seq_count - 1).astype(jnp.float32)
    number, patch_rows, features = image_in.shape
    text_rows = text_in.shape[1]
    head_width = features // HEADS
    factor = head_width ** (-0.5)
    image_out, image_saved = block_forward(image_in, image_full[0:6], gather_image_pair)
    image_vec = image_full[5].astype(jnp.float32)
    final = layer_norm(image_out, image_vec[5], image_vec[6]).astype(jnp.bfloat16)
    pool_pair = project_rows(final, image_full[7]).astype(jnp.bfloat16)
    pool_keys = (
        pool_pair[..., :features].reshape(number, patch_rows, HEADS, head_width).astype(jnp.float32)
    )
    pool_values = (
        pool_pair[..., features:].reshape(number, patch_rows, HEADS, head_width).astype(jnp.float32)
    )
    probe_query = jnp.dot(image_full[5][7:8], image_full[6], preferred_element_type=jnp.float32)[
        0
    ].reshape(HEADS, head_width)
    pool_scores = jnp.einsum("hd,bthd->bht", probe_query, pool_keys, precision=exact_mode) * factor
    local_top = jnp.max(pool_scores, -1)
    local_weights = jnp.exp(pool_scores - local_top[..., None])
    local_total = jnp.sum(local_weights, -1)
    local_sums = jnp.einsum("bht,bthd->bhd", local_weights, pool_values, precision=exact_mode)
    merged_top, merged_total, merged_sums = merge_pool(local_top, local_total, local_sums)
    pooled_heads = merged_sums / merged_total[..., None]
    pooled = pooled_heads.reshape(number, features)
    image_embed, head_saved = head_forward(
        pooled, image_full[8], image_full[9], image_full[10], image_full[11], image_vec
    )
    text_out, text_saved = block_forward(text_in, text_full[0:6], gather_text_pair)
    text_vec = text_full[5].astype(jnp.float32)
    last_row = text_out[:, -1]
    text_final = layer_norm(last_row, text_vec[5], text_vec[6]).astype(jnp.bfloat16)
    text_local = jnp.dot(text_final, text_full[6], preferred_element_type=jnp.float32)
    text_embed = spread_2(text_local, "seq", seq_count - 1)
    every_image, every_text = (
        lax.all_gather(image_embed, "dp", axis=0, tiled=True),
        lax.all_gather(text_embed, "dp", axis=0, tiled=True),
    )
    start = lax.axis_index("dp") * number
    labels = (2 * pairs - 1).astype(jnp.float32)
    loss, loss_pull = jax.vjp(
        lambda left, right, scalars: sigmoid_loss(left, right, scalars, labels),
        every_image,
        every_text,
        temp_bias,
    )
    d_every_image, d_every_text, grad_temp = loss_pull(jnp.ones_like(loss))
    d_image = lax.dynamic_slice_in_dim(d_every_image, start, number, 0)
    d_text = lax.dynamic_slice_in_dim(d_every_text, start, number, 0)
    image_back = (
        lax.all_gather(image_attend_in, ("dp", "seq"), axis=0, tiled=True),
        lax.all_gather(image_attend_out, ("dp", "seq"), axis=0, tiled=True),
        lax.all_gather(image_up_weight, ("dp", "seq"), axis=0, tiled=True),
        lax.all_gather(image_up_bias, ("dp", "seq"), axis=0, tiled=True),
        lax.all_gather(image_down_weight, ("dp", "seq"), axis=0, tiled=True),
        lax.all_gather(image_vectors, ("dp", "seq"), axis=1, tiled=True),
        lax.all_gather(probe_query_weight, ("dp", "seq"), axis=0, tiled=True),
        lax.all_gather(probe_pair_weight, ("dp", "seq"), axis=0, tiled=True),
        lax.all_gather(probe_out_weight, ("dp", "seq"), axis=0, tiled=True),
        lax.all_gather(probe_up_weight, ("dp", "seq"), axis=0, tiled=True),
        lax.all_gather(probe_up_bias, ("dp", "seq"), axis=0, tiled=True),
        lax.all_gather(probe_down_weight, ("dp", "seq"), axis=0, tiled=True),
    )
    text_back = (
        lax.all_gather(text_attend_in, ("dp", "seq"), axis=0, tiled=True),
        lax.all_gather(text_attend_out, ("dp", "seq"), axis=0, tiled=True),
        lax.all_gather(text_up_weight, ("dp", "seq"), axis=0, tiled=True),
        lax.all_gather(text_up_bias, ("dp", "seq"), axis=0, tiled=True),
        lax.all_gather(text_down_weight, ("dp", "seq"), axis=0, tiled=True),
        lax.all_gather(text_vectors, ("dp", "seq"), axis=1, tiled=True),
        lax.all_gather(text_head_weight, ("dp", "seq"), axis=0, tiled=True),
    )
    d_pooled_rows, head_grads = head_backward(
        pooled, image_back[8], image_back[9], image_back[11], image_vec, head_saved, d_image
    )
    d_pooled = d_pooled_rows.reshape(number, HEADS, head_width)
    pool_probs = jnp.exp(pool_scores - merged_top[..., None]) / merged_total[..., None]
    d_pool_values = jnp.einsum("bht,bhd->bthd", pool_probs, d_pooled)
    d_pool_probs = jnp.einsum("bhd,bthd->bht", d_pooled, pool_values, precision=exact_mode)
    inner = jnp.sum(d_pooled * pooled_heads, -1, keepdims=True)
    d_pool_scores = pool_probs * (d_pool_probs - inner) * factor
    d_pool_keys = jnp.einsum("bht,hd->bthd", d_pool_scores, probe_query)
    d_probe_query = jnp.einsum(
        "bht,bthd->hd", d_pool_scores, pool_keys, precision=exact_mode
    ).reshape(features)
    d_pool_pair = jnp.concatenate(
        [
            d_pool_keys.reshape(number, patch_rows, features),
            d_pool_values.reshape(number, patch_rows, features),
        ],
        -1,
    ).astype(jnp.bfloat16)
    grad_probe_pair = jnp.einsum(
        "btd,bte->de", final, d_pool_pair, preferred_element_type=jnp.float32
    )
    d_final = jnp.einsum(
        "bte,de->btd", d_pool_pair, image_back[7], preferred_element_type=jnp.float32
    )
    d_image_out, grad_gain_final, grad_shift_final = norm_back(
        image_out, image_vec[5], image_vec[6], d_final
    )
    probe_row = image_back[5][7].astype(jnp.float32)
    grad_probe_query = probe_row[:, None] * d_probe_query[None, :]
    d_probe_row = jnp.dot(image_back[6].astype(jnp.float32), d_probe_query, precision=exact_mode)
    d_patches, image_grads = block_backward(
        image_in, image_back[0:6], image_saved, d_image_out, scatter_image_pair
    )
    head_rows = jnp.stack([head_grads[4], head_grads[5], head_grads[6]]) * head_mask
    grad_image_vectors = jnp.concatenate(
        [image_grads[5], jnp.stack([grad_gain_final, grad_shift_final, d_probe_row]), head_rows], 0
    )
    grad_head = jnp.dot(text_final.astype(jnp.float32).T, d_text, precision=exact_mode) * text_mask
    d_text_final = (
        jnp.dot(d_text, text_back[6].astype(jnp.float32).T, precision=exact_mode) * text_mask
    )
    d_last, grad_gain_text, grad_shift_text = norm_back(
        last_row, text_vec[5], text_vec[6], d_text_final
    )
    d_text_out = jnp.concatenate(
        [jnp.zeros((number, text_rows - 1, features), jnp.float32), d_last[:, None, :]], 1
    )
    d_captions, text_grads = block_backward(
        text_in, text_back[0:6], text_saved, d_text_out, scatter_text_pair
    )
    grad_text_vectors = jnp.concatenate(
        [text_grads[5], jnp.stack([grad_gain_text, grad_shift_text])], 0
    )
    image_owned = (
        lax.psum_scatter(image_grads[0], ("dp", "seq"), scatter_dimension=0, tiled=True),
        lax.psum_scatter(image_grads[1], ("dp", "seq"), scatter_dimension=0, tiled=True),
        lax.psum_scatter(image_grads[2], ("dp", "seq"), scatter_dimension=0, tiled=True),
        lax.psum_scatter(image_grads[3], ("dp", "seq"), scatter_dimension=0, tiled=True),
        lax.psum_scatter(image_grads[4], ("dp", "seq"), scatter_dimension=0, tiled=True),
        lax.psum_scatter(grad_image_vectors, ("dp", "seq"), scatter_dimension=1, tiled=True),
        lax.psum_scatter(grad_probe_query, ("dp", "seq"), scatter_dimension=0, tiled=True),
        lax.psum_scatter(grad_probe_pair, ("dp", "seq"), scatter_dimension=0, tiled=True),
        lax.psum_scatter(head_grads[0] * head_mask, ("dp", "seq"), scatter_dimension=0, tiled=True),
        lax.psum_scatter(head_grads[1] * head_mask, ("dp", "seq"), scatter_dimension=0, tiled=True),
        lax.psum_scatter(head_grads[2] * head_mask, ("dp", "seq"), scatter_dimension=0, tiled=True),
        lax.psum_scatter(head_grads[3] * head_mask, ("dp", "seq"), scatter_dimension=0, tiled=True),
    )
    text_owned = (
        lax.psum_scatter(text_grads[0], ("dp", "seq"), scatter_dimension=0, tiled=True),
        lax.psum_scatter(text_grads[1], ("dp", "seq"), scatter_dimension=0, tiled=True),
        lax.psum_scatter(text_grads[2], ("dp", "seq"), scatter_dimension=0, tiled=True),
        lax.psum_scatter(text_grads[3], ("dp", "seq"), scatter_dimension=0, tiled=True),
        lax.psum_scatter(text_grads[4], ("dp", "seq"), scatter_dimension=0, tiled=True),
        lax.psum_scatter(grad_text_vectors, ("dp", "seq"), scatter_dimension=1, tiled=True),
        lax.psum_scatter(grad_head, ("dp", "seq"), scatter_dimension=0, tiled=True),
    )
    return (
        loss,
        d_patches,
        d_captions,
        image_owned[0],
        image_owned[1],
        image_owned[2],
        image_owned[3],
        image_owned[4],
        image_owned[5],
        image_owned[6],
        image_owned[7],
        image_owned[8],
        image_owned[9],
        image_owned[10],
        image_owned[11],
        text_owned[0],
        text_owned[1],
        text_owned[2],
        text_owned[3],
        text_owned[4],
        text_owned[5],
        text_owned[6],
        grad_temp,
    )


def solution(mesh):
    in_specs = (
        P("dp", "seq", None),
        P("dp", "seq", None),
        P(),
        P(("dp", "seq"), None),
        P(("dp", "seq"), None),
        P(("dp", "seq"), None),
        P(("dp", "seq")),
        P(("dp", "seq"), None),
        P(None, ("dp", "seq")),
        P(("dp", "seq"), None),
        P(("dp", "seq"), None),
        P(("dp", "seq"), None),
        P(("dp", "seq"), None),
        P(("dp", "seq")),
        P(("dp", "seq"), None),
        P(("dp", "seq"), None),
        P(("dp", "seq"), None),
        P(("dp", "seq"), None),
        P(("dp", "seq")),
        P(("dp", "seq"), None),
        P(None, ("dp", "seq")),
        P(("dp", "seq"), None),
        P(),
    )
    out_specs = (
        P(),
        P("dp", "seq", None),
        P("dp", "seq", None),
        P(("dp", "seq"), None),
        P(("dp", "seq"), None),
        P(("dp", "seq"), None),
        P(("dp", "seq")),
        P(("dp", "seq"), None),
        P(None, ("dp", "seq")),
        P(("dp", "seq"), None),
        P(("dp", "seq"), None),
        P(("dp", "seq"), None),
        P(("dp", "seq"), None),
        P(("dp", "seq")),
        P(("dp", "seq"), None),
        P(("dp", "seq"), None),
        P(("dp", "seq"), None),
        P(("dp", "seq"), None),
        P(("dp", "seq")),
        P(("dp", "seq"), None),
        P(None, ("dp", "seq")),
        P(("dp", "seq"), None),
        P(),
    )
    return jax.shard_map(
        per_device, mesh=mesh, in_specs=in_specs, out_specs=out_specs, check_vma=False
    )
```

profile of v0, /device:TPU:0, one launch (start us, length us, event | category | flops | bytes accessed | tf_op | source)
XLA Modules:
  0.0 3444.3 jit_solution(6860977977165994664)
XLA Ops:
  12.0 71.3 %all-gather.3 = bf16[32,24,11]{1,2,0:T(8,128)(2,1)S(1)} all-gather(bf16[1,24,11]{1,2,0:T(8,128)(2,1)} %bitcast.520), channel_id=1, replica_groups=mesh['dp'=8,'seq'=4] {'dp','seq'}, dimensions={0}, use_global_device_ids=true | all-gather | bytes 17424 | tf_op jit(solution)/shard_map/all_gather | solution.py:259
  102.6 37.5 %all-reduce.12 = (bf16[3072]{0:T(1024)(128)(2,1)S(1)}, bf16[3072]{0:T(1024)(128)(2,1)S(1)}, bf16[3072]{0:T(1024)(128)(2,1)S(1)}) all-reduce(bf16[3072]{0:T(1024)(128)(2,1)S(1)} %dynamic-update-slice.2, bf16[3072]{0:T(1024)(128)(2,1)S(1)} %dynamic-update-slice, ...), channel_id=1, replica_groups=mesh['dp'=8,'seq'=4] {'dp','seq'}, use_global_device_ids=true, to_apply=%add.5 | all-reduce | flops 9216 | bytes 36864
  142.2 67.0 %all-gather.7 = bf16[32,24,7]{1,2,0:T(8,128)(2,1)S(1)} all-gather(bf16[1,24,7]{1,2,0:T(8,128)(2,1)S(1)} %bitcast.521), channel_id=1, replica_groups=mesh['dp'=8,'seq'=4] {'dp','seq'}, dimensions={0}, use_global_device_ids=true | all-gather | bytes 11088 | tf_op jit(solution)/shard_map/all_gather | solution.py:273
  276.0 37.3 %all-gather.49.cloned.1.call-done = bf16[768,3072]{1,0:T(8,128)(2,1)} async-done(((bf16[24,3072]{1,0:T(8,128)(2,1)}), bf16[768,3072]{1,0:T(8,128)(2,1)}) %all-gather.49.cloned.1.call-update) | async-done | bytes 4718608 | tf_op jit(solution)/shard_map/all_gather | solution.py:270
  317.4 60.9 %all-gather.51.cloned.1.call-done = bf16[3072,768]{1,0:T(8,128)(2,1)} async-done(((bf16[96,768]{1,0:T(8,128)(2,1)}), bf16[3072,768]{1,0:T(8,128)(2,1)}) %all-gather.51.cloned.1.call-update) | async-done | bytes 4718608 | tf_op jit(solution)/shard_map/all_gather | solution.py:272
  382.3 51.8 %all-gather.53.cloned.1.call-done = bf16[768,768]{1,0:T(8,128)(2,1)} async-done(((bf16[24,768]{1,0:T(8,128)(2,1)}), bf16[768,768]{1,0:T(8,128)(2,1)}) %all-gather.53.cloned.1.call-update) | async-done | bytes 1179664 | tf_op jit(solution)/shard_map/all_gather | solution.py:274
  435.7 17.9 psum.7
  463.8 189.7 %all-gather.27.cloned.1.call-done = bf16[4,1024,1536]{2,1,0:T(8,128)(2,1)} async-done(((bf16[4,256,1536]{2,1,0:T(8,128)(2,1)}), bf16[4,1024,1536]{2,1,0:T(8,128)(2,1)}) %all-gather.27.cloned.1.call-update) | async-done | bytes 12582928 | tf_op jit(solution)/shard_map/all_gather | solution.py:196
  682.6 47.0 %while.66 = (s32[]{:T(128)}, bf16[4,256,12,64]{1,3,2,0:T(8,128)(2,1)}, f32[4,12,256,1]{2,1,3,0:T(8,128)}, bf16[4,1024,12,64]{1,3,2,0:T(8,128)(2,1)}, bf16[4,256,...) while((s32[]{:T(128)}, bf16[4,256,12,64]{1,3,2,0:T(8,128)(2,1)}, ...), condition=%wide.region_5.6_spmd, body=%wide.region_2.5_spmd.sunk | while | flops 833614848 | bytes 42179148 | solution.py:98
  735.1 38.7 %all-gather.31.cloned.1.call-done = bf16[768,3072]{1,0:T(8,128)(2,1)} async-done(((bf16[24,3072]{1,0:T(8,128)(2,1)}), bf16[768,3072]{1,0:T(8,128)(2,1)}) %all-gather.31.cloned.1.call-update) | async-done | bytes 4718608 | tf_op jit(solution)/shard_map/all_gather | solution.py:256
  784.8 54.3 %all-gather.33.cloned.1.call-done = bf16[3072,768]{1,0:T(8,128)(2,1)} async-done(((bf16[96,768]{1,0:T(8,128)(2,1)}), bf16[3072,768]{1,0:T(8,128)(2,1)}) %all-gather.33.cloned.1.call-update) | async-done | bytes 4718608 | tf_op jit(solution)/shard_map/all_gather | solution.py:258
  854.5 43.4 %all-gather.35.cloned.1.call-done = bf16[768,1536]{1,0:T(8,128)(2,1)} async-done(((bf16[24,1536]{1,0:T(8,128)(2,1)}), bf16[768,1536]{1,0:T(8,128)(2,1)}) %all-gather.35.cloned.1.call-update) | async-done | bytes 2359312 | tf_op jit(solution)/shard_map/all_gather | solution.py:261
  955.9 63.0 %all-gather.41.cloned.1.call-done = bf16[768,3072]{1,0:T(8,128)(2,1)} async-done(((bf16[24,3072]{1,0:T(8,128)(2,1)}), bf16[768,3072]{1,0:T(8,128)(2,1)}) %all-gather.41.cloned.1.call-update) | async-done | bytes 4718608 | tf_op jit(solution)/shard_map/all_gather | solution.py:263
  1022.1 61.9 %all-gather.43.cloned.1.call-done = bf16[3072,768]{1,0:T(8,128)(2,1)} async-done(((bf16[96,768]{1,0:T(8,128)(2,1)}), bf16[3072,768]{1,0:T(8,128)(2,1)}) %all-gather.43.cloned.1.call-update) | async-done | bytes 4718608 | tf_op jit(solution)/shard_map/all_gather | solution.py:265
  1140.6 19.7 while.70
  1212.6 115.3 %while.69 = (s32[]{:T(128)}, bf16[4,256,12,64]{1,3,2,0:T(8,128)(2,1)}, bf16[4,1024,12,64]{1,3,2,0:T(8,128)(2,1)}, bf16[4,1024,12,64]{1,3,2,0:T(8,128)(2,1)}, bf1...) while((s32[]{:T(128)}, ...), condition=%wide.region_40.41_spmd, body=%wide.region_38.40_spmd.sunk | while | flops 2051994624 | bytes 120423584 | solution.py:132
  1380.3 186.2 %reduce-scatter.19.cloned.1.call-done = bf16[4,256,1536]{2,1,0:T(8,128)(2,1)} async-done(((bf16[4,1024,1536]{2,1,0:T(8,128)(2,1)}), bf16[4,256,1536]{2,1,0:T(8,128)(2,1)}) %reduce-scatter.19.cloned.1.call-update) | async-done | bytes 3145744 | tf_op jit(solution)/shard_map/reduce_scatter | solution.py:204
  1678.3 22.5 all-reduce.15.cloned.1.call-done
  1707.4 99.4 %reduce-scatter.49.cloned.1.call-done = f32[24,768]{1,0:T(8,128)} async-done(((f32[768,768]{1,0:T(8,128)}), f32[24,768]{1,0:T(8,128)}) %reduce-scatter.49.cloned.1.call-update) | async-done | bytes 73744 | tf_op jit(solution)/shard_map/reduce_scatter | solution.py:430
  1806.8 104.6 %reduce-scatter.35.cloned.1.call-done = f32[24,768]{1,0:T(8,128)} async-done(((f32[768,768]{1,0:T(8,128)}), f32[24,768]{1,0:T(8,128)}) %reduce-scatter.35.cloned.1.call-update) | async-done | bytes 73744 | tf_op jit(solution)/shard_map/reduce_scatter | solution.py:418
  1911.4 104.0 %reduce-scatter.43.cloned.1.call-done = f32[24,768]{1,0:T(8,128)} async-done(((f32[768,768]{1,0:T(8,128)}), f32[24,768]{1,0:T(8,128)}) %reduce-scatter.43.cloned.1.call-update) | async-done | bytes 73744 | tf_op jit(solution)/shard_map/reduce_scatter | solution.py:425
  2015.4 104.7 %reduce-scatter.25.cloned.1.call-done = f32[24,768]{1,0:T(8,128)} async-done(((f32[768,768]{1,0:T(8,128)}), f32[24,768]{1,0:T(8,128)}) %reduce-scatter.25.cloned.1.call-update) | async-done | bytes 73744 | tf_op jit(solution)/shard_map/reduce_scatter | solution.py:411
  2120.1 104.0 %reduce-scatter.31.cloned.1.call-done = f32[24,768]{1,0:T(8,128)} async-done(((f32[768,768]{1,0:T(8,128)}), f32[24,768]{1,0:T(8,128)}) %reduce-scatter.31.cloned.1.call-update) | async-done | bytes 73744 | tf_op jit(solution)/shard_map/reduce_scatter | solution.py:416
  2224.2 112.8 %reduce-scatter.33.cloned.1.call-done = f32[24,1536]{1,0:T(8,128)} async-done(((f32[768,1536]{1,0:T(8,128)}), f32[24,1536]{1,0:T(8,128)}) %reduce-scatter.33.cloned.1.call-update) | async-done | bytes 147472 | tf_op jit(solution)/shard_map/reduce_scatter | solution.py:417
  2337.0 124.5 %reduce-scatter.41.cloned.1.call-done = f32[24,2304]{1,0:T(8,128)} async-done(((f32[768,2304]{1,0:T(8,128)}), f32[24,2304]{1,0:T(8,128)}) %reduce-scatter.41.cloned.1.call-update) | async-done | bytes 221200 | tf_op jit(solution)/shard_map/reduce_scatter | solution.py:424
  2461.5 142.2 %reduce-scatter.37.cloned.1.call-done = f32[24,3072]{1,0:T(8,128)} async-done(((f32[768,3072]{1,0:T(8,128)}), f32[24,3072]{1,0:T(8,128)}) %reduce-scatter.37.cloned.1.call-update) | async-done | bytes 294928 | tf_op jit(solution)/shard_map/reduce_scatter | solution.py:419
  2603.7 140.8 %reduce-scatter.27.cloned.1.call-done = f32[24,3072]{1,0:T(8,128)} async-done(((f32[768,3072]{1,0:T(8,128)}), f32[24,3072]{1,0:T(8,128)}) %reduce-scatter.27.cloned.1.call-update) | async-done | bytes 294928 | tf_op jit(solution)/shard_map/reduce_scatter | solution.py:412
  2744.5 142.1 %reduce-scatter.45.cloned.1.call-done = f32[24,3072]{1,0:T(8,128)} async-done(((f32[768,3072]{1,0:T(8,128)}), f32[24,3072]{1,0:T(8,128)}) %reduce-scatter.45.cloned.1.call-update) | async-done | bytes 294928 | tf_op jit(solution)/shard_map/reduce_scatter | solution.py:426
  2886.6 141.1 %reduce-scatter.47.cloned.1.call-done = f32[96,768]{1,0:T(8,128)} async-done(((f32[3072,768]{1,0:T(8,128)}), f32[96,768]{1,0:T(8,128)}) %reduce-scatter.47.cloned.1.call-update) | async-done | bytes 294928 | tf_op jit(solution)/shard_map/reduce_scatter | solution.py:428
  3027.7 142.1 %reduce-scatter.29.cloned.1.call-done = f32[96,768]{1,0:T(8,128)} async-done(((f32[3072,768]{1,0:T(8,128)}), f32[96,768]{1,0:T(8,128)}) %reduce-scatter.29.cloned.1.call-update) | async-done | bytes 294928 | tf_op jit(solution)/shard_map/reduce_scatter | solution.py:414
  3169.8 140.9 %reduce-scatter.39.cloned.1.call-done = f32[96,768]{1,0:T(8,128)} async-done(((f32[3072,768]{1,0:T(8,128)}), f32[96,768]{1,0:T(8,128)}) %reduce-scatter.39.cloned.1.call-update) | async-done | bytes 294928 | tf_op jit(solution)/shard_map/reduce_scatter | solution.py:421
  3310.7 125.5 %reduce-scatter.23.cloned.1.call-done = f32[24,2304]{1,0:T(8,128)} async-done(((f32[768,2304]{1,0:T(8,128)}), f32[24,2304]{1,0:T(8,128)}) %reduce-scatter.23.cloned.1.call-update) | async-done | bytes 221200 | tf_op jit(solution)/shard_map/reduce_scatter | solution.py:410
  (823 shorter events, 706.8 us)
Async XLA Ops:
  7.2 79.3 %all-gather.25.cloned.1.call-start = ((), (), s32[]{:S(2)}) async-start(), calls=%async_computation.16 | async-start | bytes 3649536 | tf_op jit(solution)/shard_map/all_gather | solution.py:254
  7.9 204.4 %all-gather.37.cloned.1.call-start = ((), (), s32[]{:S(2)}) async-start(), calls=%async_computation.22 | async-start | bytes 1216512 | tf_op jit(solution)/shard_map/all_gather | solution.py:260
  8.7 209.1 %all-gather.45.cloned.1.call-start = ((), (), s32[]{:S(2)}) async-start(), calls=%async_computation.26 | async-start | bytes 3649536 | tf_op jit(solution)/shard_map/all_gather | solution.py:268
  9.4 262.4 %all-gather.47.cloned.1.call-start = ((), (), s32[]{:S(2)}) async-start(), calls=%async_computation.27 | async-start | bytes 1216512 | tf_op jit(solution)/shard_map/all_gather | solution.py:269
  10.0 303.3 %all-gather.49.cloned.1.call-start = ((), (), s32[]{:S(2)}) async-start(), calls=%async_computation.28 | async-start | bytes 4866048 | tf_op jit(solution)/shard_map/all_gather | solution.py:270
  10.6 367.7 %all-gather.51.cloned.1.call-start = ((), (), s32[]{:S(2)}) async-start(), calls=%async_computation.29 | async-start | bytes 4866048 | tf_op jit(solution)/shard_map/all_gather | solution.py:272
  11.2 422.9 %all-gather.53.cloned.1.call-start = ((), (), s32[]{:S(2)}) async-start(), calls=%async_computation.30 | async-start | bytes 1216512 | tf_op jit(solution)/shard_map/all_gather | solution.py:274
  11.9 641.5 %all-gather.27.cloned.1.call-start = ((), (), s32[]{:S(2)}) async-start(), calls=%async_computation.17 | async-start | bytes 15728640 | tf_op jit(solution)/shard_map/all_gather | solution.py:196
  97.0 632.6 %all-gather.29.cloned.1.call-start = ((), (), s32[]{:S(2)}) async-start(), calls=%async_computation.18 | async-start | bytes 1216512 | tf_op jit(solution)/shard_map/all_gather | solution.py:255
  97.8 676.1 %all-gather.31.cloned.1.call-start = ((), (), s32[]{:S(2)}) async-start(), calls=%async_computation.19 | async-start | bytes 4866048 | tf_op jit(solution)/shard_map/all_gather | solution.py:256
  98.4 740.7 %all-gather.33.cloned.1.call-start = ((), (), s32[]{:S(2)}) async-start(), calls=%async_computation.20 | async-start | bytes 4866048 | tf_op jit(solution)/shard_map/all_gather | solution.py:258
  99.1 798.8 %all-gather.35.cloned.1.call-start = ((), (), s32[]{:S(2)}) async-start(), calls=%async_computation.21 | async-start | bytes 2433024 | tf_op jit(solution)/shard_map/all_gather | solution.py:261
  99.7 854.0 %all-gather.39.cloned.1.call-start = ((), (), s32[]{:S(2)}) async-start(), calls=%async_computation.23 | async-start | bytes 1216512 | tf_op jit(solution)/shard_map/all_gather | solution.py:262
  100.4 918.5 %all-gather.41.cloned.1.call-start = ((), (), s32[]{:S(2)}) async-start(), calls=%async_computation.24 | async-start | bytes 4866048 | tf_op jit(solution)/shard_map/all_gather | solution.py:263
  101.0 982.9 %all-gather.43.cloned.1.call-start = ((), (), s32[]{:S(2)}) async-start(), calls=%async_computation.25 | async-start | bytes 4866048 | tf_op jit(solution)/shard_map/all_gather | solution.py:265
  101.6 1270.4 %reduce-scatter.21.cloned.1.call-start = ((), (), s32[]{:S(2)}) async-start(), calls=%async_computation.32 | async-start | bytes 983040 | tf_op jit(solution)/shard_map/reduce_scatter | solution.py:210
  1166.0 400.6 %reduce-scatter.19.cloned.1.call-start = ((), (), s32[]{:S(2)}) async-start(), calls=%async_computation.31 | async-start | bytes 15728640 | tf_op jit(solution)/shard_map/reduce_scatter | solution.py:204
  1355.8 345.0 %all-reduce.15.cloned.1.call-start = ((), (), s32[]{:S(2)}) async-start(), calls=%async_computation.47 | async-start | bytes 221184
  1576.9 229.9 %reduce-scatter.49.cloned.1.call-start = ((), (), s32[]{:S(2)}) async-start(), calls=%async_computation.46 | async-start | bytes 2433024 | tf_op jit(solution)/shard_map/reduce_scatter | solution.py:430
  1580.4 331.0 %reduce-scatter.35.cloned.1.call-start = ((), (), s32[]{:S(2)}) async-start(), calls=%async_computation.39 | async-start | bytes 2433024 | tf_op jit(solution)/shard_map/reduce_scatter | solution.py:418
  1584.0 431.4 %reduce-scatter.43.cloned.1.call-start = ((), (), s32[]{:S(2)}) async-start(), calls=%async_computation.43 | async-start | bytes 2433024 | tf_op jit(solution)/shard_map/reduce_scatter | solution.py:425
  1586.0 534.1 %reduce-scatter.25.cloned.1.call-start = ((), (), s32[]{:S(2)}) async-start(), calls=%async_computation.34 | async-start | bytes 2433024 | tf_op jit(solution)/shard_map/reduce_scatter | solution.py:411
  1590.3 633.9 %reduce-scatter.31.cloned.1.call-start = ((), (), s32[]{:S(2)}) async-start(), calls=%async_computation.37 | async-start | bytes 2433024 | tf_op jit(solution)/shard_map/reduce_scatter | solution.py:416
  1593.0 744.0 %reduce-scatter.33.cloned.1.call-start = ((), (), s32[]{:S(2)}) async-start(), calls=%async_computation.38 | async-start | bytes 4866048 | tf_op jit(solution)/shard_map/reduce_scatter | solution.py:417
  1600.3 861.1 %reduce-scatter.41.cloned.1.call-start = ((), (), s32[]{:S(2)}) async-start(), calls=%async_computation.42 | async-start | bytes 7299072 | tf_op jit(solution)/shard_map/reduce_scatter | solution.py:424
  1605.3 998.4 %reduce-scatter.37.cloned.1.call-start = ((), (), s32[]{:S(2)}) async-start(), calls=%async_computation.40 | async-start | bytes 9732096 | tf_op jit(solution)/shard_map/reduce_scatter | solution.py:419
  1612.7 1131.8 %reduce-scatter.27.cloned.1.call-start = ((), (), s32[]{:S(2)}) async-start(), calls=%async_computation.35 | async-start | bytes 9732096 | tf_op jit(solution)/shard_map/reduce_scatter | solution.py:412
  1625.3 1261.3 %reduce-scatter.45.cloned.1.call-start = ((), (), s32[]{:S(2)}) async-start(), calls=%async_computation.44 | async-start | bytes 9732096 | tf_op jit(solution)/shard_map/reduce_scatter | solution.py:426
  1631.2 1396.5 %reduce-scatter.47.cloned.1.call-start = ((), (), s32[]{:S(2)}) async-start(), calls=%async_computation.45 | async-start | bytes 9732096 | tf_op jit(solution)/shard_map/reduce_scatter | solution.py:428
  1637.4 1532.4 %reduce-scatter.29.cloned.1.call-start = ((), (), s32[]{:S(2)}) async-start(), calls=%async_computation.36 | async-start | bytes 9732096 | tf_op jit(solution)/shard_map/reduce_scatter | solution.py:414
  1651.6 1659.1 %reduce-scatter.39.cloned.1.call-start = ((), (), s32[]{:S(2)}) async-start(), calls=%async_computation.41 | async-start | bytes 9732096 | tf_op jit(solution)/shard_map/reduce_scatter | solution.py:421
  1658.7 1777.5 %reduce-scatter.23.cloned.1.call-start = ((), (), s32[]{:S(2)}) async-start(), calls=%async_computation.33 | async-start | bytes 7299072 | tf_op jit(solution)/shard_map/reduce_scatter | solution.py:410
  (207 other events, 7785.7 us)
Sparse Core Ops, SparseCore 0:
  10.8 63.1 all-gather.24
  76.8 52.9 all-gather.36
  132.7 59.1 all-gather.44
  194.5 53.5 all-gather.46
  250.7 62.5 all-gather.48
  315.9 62.3 all-gather.50
  381.1 52.8 all-gather.52
  436.2 217.1 all-gather.26
  656.2 52.3 all-gather.28
  711.3 62.5 all-gather.30
  776.7 62.3 all-gather.32
  841.7 56.1 all-gather.34
  900.7 52.9 all-gather.38
  956.4 62.4 all-gather.40
  1021.6 62.3 all-gather.42
  1166.1 22.1 reduce-scatter.20
  1355.9 210.6 reduce-scatter.18
  1577.0 123.7 all-reduce.14
  1706.7 100.0 reduce-scatter.48
  1813.4 97.9 reduce-scatter.34
  1917.3 98.1 reduce-scatter.42
  2022.1 97.9 reduce-scatter.24
  2126.0 98.1 reduce-scatter.30
  2231.0 105.9 reduce-scatter.32
  2343.2 118.2 reduce-scatter.40
  2468.8 134.8 reduce-scatter.36
  2610.0 134.4 reduce-scatter.26
  2752.0 134.6 reduce-scatter.44
  2893.1 134.5 reduce-scatter.46
  3035.0 134.7 reduce-scatter.28
  3176.3 134.4 reduce-scatter.38
  3317.9 118.2 reduce-scatter.22
where the time goes:
time: 3450 us; the launch traced here: 3440 us
  waiting for transfers between devices  2550 us (74%)
  matrix products  370 us (11%)
  blocking collectives  268 us (8%)
  local copies, waits for them, and re-layouts  144 us (4%)
  other arithmetic  87.8 us (3%)
    all_gather x1, waiting for transfers between devices, gather_image_pair(): return lax.all_gather(pair, 'seq', axis=1, tiled=True)  190 us
    reduce_scatter x1, waiting for transfers between devices, scatter_image_pair(): lax.psum_scatter(pair.astype(jnp.bfloat16), 'seq', scatter_dimension=1, t...  186 us
    reduce_scatter x1, waiting for transfers between devices, per_device(): lax.psum_scatter(head_grads[1] * head_mask, ('dp', 'seq'), scatter_dimens...  142 us
    reduce_scatter x1, waiting for transfers between devices, per_device(): lax.psum_scatter(text_grads[2], ('dp', 'seq'), scatter_dimension=0, tiled...  142 us
    reduce_scatter x1, waiting for transfers between devices, per_device(): lax.psum_scatter(image_grads[4], ('dp', 'seq'), scatter_dimension=0, tile...  142 us
    reduce_scatter x1, waiting for transfers between devices, per_device(): lax.psum_scatter(text_grads[4], ('dp', 'seq'), scatter_dimension=0, tiled...  141 us
    reduce_scatter x1, waiting for transfers between devices, per_device(): lax.psum_scatter(head_grads[3] * head_mask, ('dp', 'seq'), scatter_dimens...  141 us
    reduce_scatter x1, waiting for transfers between devices, per_device(): lax.psum_scatter(image_grads[2], ('dp', 'seq'), scatter_dimension=0, tile...  141 us
  transfers between devices with their start and end apart: 32, of which 26 were waited for; matrix products, arithmetic and copies ran while one was open for 14% of the time, Pallas kernels for 0%

commit v1 on v0

v1 whole, which is shorter than its diff:
```python
from functools import partial

import jax
import jax.numpy as jnp
from jax import lax
from jax.experimental import pallas as pl
from jax.experimental.pallas import tpu as pltpu
from jax.sharding import PartitionSpec as P

HEADS = 12
ALL = ("dp", "seq")
F32, BF = jnp.float32, jnp.bfloat16
HIGH = lax.Precision.HIGHEST
EPS = 1e-06


def mm(a, b, ca=1, cb=0):
    return lax.dot_general(a, b, (((ca,), (cb,)), ((), ())), preferred_element_type=F32)


def mm_exact(a, b, ca=1, cb=0):
    return lax.dot_general(a, b, (((ca,), (cb,)), ((), ())), precision=HIGH, preferred_element_type=F32)


def split_two(a):
    high = a.astype(BF)
    return high, (a - high.astype(F32)).astype(BF)


def layer_norm(x, gain, shift):
    center = x - jnp.mean(x, -1, keepdims=True)
    spread = jnp.mean(center * center, -1, keepdims=True)
    return center * lax.rsqrt(spread + EPS) * gain + shift


def norm_back(x, gain, upstream):
    center = x - jnp.mean(x, -1, keepdims=True)
    inverse = lax.rsqrt(jnp.mean(center * center, -1, keepdims=True) + EPS)
    unit = center * inverse
    scaled = upstream * gain
    d_x = inverse * (
        scaled
        - jnp.mean(scaled, -1, keepdims=True)
        - unit * jnp.mean(scaled * unit, -1, keepdims=True)
    )
    return d_x, jnp.sum(upstream * unit, 0), jnp.sum(upstream, 0)


def norm_back_rows(x, gain, upstream):
    d_x, d_gain, d_shift = norm_back(x, gain, upstream)
    return d_x, d_gain[None], d_shift[None]


def mm_two(a, b, cb=0):
    high, low = split_two(a)
    return mm(high, b, 1, cb) + mm(low, b, 1, cb)


def gelu_pair(u):
    c = 0.7978845608028654
    t = jnp.tanh(c * (u + 0.044715 * u * u * u))
    value = 0.5 * u * (1.0 + t)
    slope = 0.5 * (1.0 + t) + 0.5 * u * (1.0 - t * t) * c * (1.0 + 3 * 0.044715 * u * u)
    return value, slope


def attend_fwd_kernel(q_ref, k_ref, v_ref, o_ref, lse_ref):
    q = q_ref[...] * 0.125
    k = k_ref[...]
    lane = lax.broadcasted_iota(jnp.int32, k.shape, 1)
    v_turned = jnp.transpose(v_ref[...])
    outs = []
    for h in range(2):
        keep = (lane < 64) if h == 0 else (lane >= 64)
        own_k = jnp.where(keep, k, jnp.zeros_like(k))
        s = mm(own_k, q, 1, 1)
        top = jnp.max(s, 0, keepdims=True)
        p = jnp.exp(s - top)
        total = jnp.sum(p, 0, keepdims=True)
        outs.append(mm(v_turned[64 * h : 64 * h + 64], p.astype(BF)) / total)
        lse_ref[0, h : h + 1, :] = top + jnp.log(total)
    o_ref[...] = jnp.transpose(jnp.concatenate(outs, 0)).astype(BF)


def attend_fwd(proj, length):
    rows, width = proj.shape[0], proj.shape[1] // 3
    pairs = width // 128
    block = lambda part: pl.BlockSpec((length, 128), lambda b, h: (b, part * pairs + h))
    return pl.pallas_call(
        attend_fwd_kernel,
        grid=(rows // length, pairs),
        in_specs=[block(0), block(1), block(2)],
        out_specs=[block(0), pl.BlockSpec((1, 2, length), lambda b, h: (h, 0, b))],
        out_shape=[
            jax.ShapeDtypeStruct((rows, width), BF),
            jax.ShapeDtypeStruct((pairs, 2, rows), F32),
        ],
        compiler_params=pltpu.CompilerParams(vmem_limit_bytes=48 << 20),
        cost_estimate=pl.CostEstimate(
            flops=rows * length * width * 8,
            bytes_accessed=rows * width * 8,
            transcendentals=rows * length * HEADS,
        ),
    )(proj, proj, proj)


def attend_bwd_kernel(q_ref, k_ref, v_ref, do_ref, lse_ref, d_ref, dq_ref, dk_ref, dv_ref):
    q = q_ref[...] * 0.125
    k, v, do = k_ref[...], v_ref[...], do_ref[...]
    lane = lax.broadcasted_iota(jnp.int32, k.shape, 1)
    dqs, dks, dvs = [], [], []
    for h in range(2):
        keep = (lane < 64) if h == 0 else (lane >= 64)
        s = mm(jnp.where(keep, k, jnp.zeros_like(k)), q, 1, 1)
        p = jnp.exp(s - lse_ref[0, h : h + 1, :])
        dp = mm(jnp.where(keep, v, jnp.zeros_like(v)), do, 1, 1)
        ds = (p * (dp - d_ref[0, h : h + 1, :])).astype(BF)
        dvs.append(mm(p.astype(BF), do))
        dks.append(mm(ds, q))
        dqs.append(mm(ds, k, 0, 0))
    low = lane < 64
    dq_ref[...] = (jnp.where(low, dqs[0], dqs[1]) * 0.125).astype(BF)
    dk_ref[...] = jnp.where(low, dks[0], dks[1]).astype(BF)
    dv_ref[...] = jnp.where(low, dvs[0], dvs[1]).astype(BF)


def attend_bwd(proj, d_out, lse, inner, length):
    rows, width = proj.shape[0], proj.shape[1] // 3
    pairs = width // 128
    block = lambda part: pl.BlockSpec((length, 128), lambda b, h: (b, part * pairs + h))
    row = pl.BlockSpec((1, 2, length), lambda b, h: (h, 0, b))
    result = jax.ShapeDtypeStruct((rows, width), BF)
    return pl.pallas_call(
        attend_bwd_kernel,
        grid=(rows // length, pairs),
        in_specs=[block(0), block(1), block(2), block(0), row, row],
        out_specs=[block(0)] * 3,
        out_shape=[result] * 3,
        compiler_params=pltpu.CompilerParams(vmem_limit_bytes=56 << 20),
        cost_estimate=pl.CostEstimate(
            flops=rows * length * width * 20,
            bytes_accessed=rows * width * 16,
            transcendentals=rows * length * HEADS,
        ),
    )(proj, proj, proj, d_out, lse, inner)


def head_blocks(width):
    own = jnp.arange(width)[None, :] // (width // HEADS) == jnp.arange(HEADS)[:, None]
    return own.astype(F32)


def spread_heads(rows):
    n, width = rows.shape
    return (rows[:, None, :] * head_blocks(width)[None]).reshape(n * HEADS, width)


def fold_heads(rows):
    total, width = rows.shape
    return jnp.sum(rows.reshape(total // HEADS, HEADS, width) * head_blocks(width)[None], 1)


def device_program(
    patches, captions, pairs,
    image_attend_in, image_attend_out, image_up_weight, image_up_bias, image_down_weight,
    image_vectors, probe_query_weight, probe_pair_weight, probe_out_weight, probe_up_weight,
    probe_up_bias, probe_down_weight, text_attend_in, text_attend_out, text_up_weight,
    text_up_bias, text_down_weight, text_vectors, text_head_weight, temp_bias,
):
    seq = lax.axis_size("seq")
    world = seq * lax.axis_size("dp")
    me = lax.axis_index("dp") * seq + lax.axis_index("seq")
    width = patches.shape[-1]
    head_width = width // HEADS
    factor = head_width ** (-0.5)
    hidden_width = image_up_weight.shape[1]
    part = width // world
    wide_part = hidden_width // world

    def gather(*weights):
        flat = jnp.concatenate([w.reshape(-1, width) for w in weights], 0)
        full = lax.all_gather(flat, ALL, axis=0)
        out, at = [], 0
        for w in weights:
            count = w.size // width
            piece = full[:, at : at + count]
            out.append(piece.reshape(world * w.shape[0], w.shape[1]))
            at += count
        return out

    small = jnp.concatenate(
        [image_vectors.reshape(-1), text_vectors.reshape(-1), image_up_bias, probe_up_bias, text_up_bias]
    )
    small_all = lax.all_gather(small, ALL, axis=0)
    sizes = [image_vectors.size, text_vectors.size, image_up_bias.size, probe_up_bias.size, text_up_bias.size]
    cuts = [sum(sizes[:i]) for i in range(len(sizes) + 1)]
    pieces = [small_all[:, cuts[i] : cuts[i + 1]].astype(F32) for i in range(len(sizes))]
    ivec = pieces[0].reshape(world, -1, part).transpose(1, 0, 2).reshape(-1, width)
    tvec = pieces[1].reshape(world, -1, part).transpose(1, 0, 2).reshape(-1, width)
    i_bias, p_bias, t_bias = (p.reshape(-1) for p in pieces[2:])

    (w_in,) = gather(image_attend_in)
    w_out, w_up, w_down = gather(image_attend_out, image_up_weight, image_down_weight)
    tw_in, tw_out, tw_up, tw_down, tw_head, pw_query, pw_pair, pw_out, pw_up, pw_down = gather(
        text_attend_in, text_attend_out, text_up_weight, text_down_weight, text_head_weight,
        probe_query_weight, probe_pair_weight, probe_out_weight, probe_up_weight, probe_down_weight,
    )

    def to_owner(x):
        return lax.all_to_all(x, "seq", 0, 1, tiled=True)

    x = to_owner(patches)
    own, length = x.shape[0], x.shape[1]
    x = x.reshape(own * length, width).astype(F32)
    captions_own = to_owner(captions)
    text_length = captions_own.shape[1]

    normed = layer_norm(x, ivec[0], ivec[1]).astype(BF)
    proj = mm(normed, w_in).astype(BF)
    mixed, lse = attend_fwd(proj, length)
    hidden = x + mm(mixed, w_out)
    second = layer_norm(hidden, ivec[2], ivec[3]).astype(BF)
    value, slope = gelu_pair(mm(second, w_up) + i_bias)
    active, slope = value.astype(BF), slope.astype(BF)
    block_out = hidden + mm(active, w_down) + ivec[4]
    final = layer_norm(block_out, ivec[5], ivec[6]).astype(BF)

    t_x = captions_own.astype(F32)
    t_normed = layer_norm(t_x, tvec[0], tvec[1]).astype(BF)
    t_last = t_normed[:, -1]
    tw_q, tw_k, tw_v = tw_in[:, :width], tw_in[:, width : 2 * width], tw_in[:, 2 * width :]
    t_q = mm(t_last, tw_q).astype(BF)
    t_keys = mm(spread_heads(t_q.astype(F32)).astype(BF), tw_k, 1, 1) * factor
    t_keys = t_keys.reshape(own, HEADS, width)
    k_high, k_low = split_two(t_keys)
    scores = jnp.einsum("bsd,bhd->bsh", t_normed, k_high, preferred_element_type=F32)
    scores += jnp.einsum("bsd,bhd->bsh", t_normed, k_low, preferred_element_type=F32)
    t_probs = jax.nn.softmax(scores, axis=1)
    t_used = jnp.einsum("bsh,bsd->bhd", t_probs, t_normed.astype(F32), precision=HIGH)
    t_mixed = fold_heads(mm(t_used.reshape(own * HEADS, width).astype(BF), tw_v)).astype(BF)
    t_hidden = t_x[:, -1] + mm(t_mixed, tw_out)
    t_second = layer_norm(t_hidden, tvec[2], tvec[3]).astype(BF)
    t_value, t_slope = gelu_pair(mm(t_second, tw_up) + t_bias)
    t_active = t_value.astype(BF)
    t_out = t_hidden + mm(t_active, tw_down) + tvec[4]
    t_final = layer_norm(t_out, tvec[5], tvec[6]).astype(BF)
    text_embed = mm(t_final, tw_head)

    pw_k, pw_v = pw_pair[:, :width], pw_pair[:, width:]
    probe_query = mm_exact(ivec[7:8], pw_query.astype(F32))
    p_keys = mm_exact(spread_heads(probe_query), pw_k.astype(F32), 1, 1) * factor
    k_high, k_low = split_two(p_keys)
    pool_scores = mm(k_high, final, 1, 1) + mm(k_low, final, 1, 1)
    pool_scores = pool_scores.reshape(HEADS, own, length)
    pool_probs = jax.nn.softmax(pool_scores, axis=-1)
    final_own = final.reshape(own, length, width)
    p_high, p_low = split_two(pool_probs)
    used = jnp.einsum("hbt,btd->bhd", p_high, final_own, preferred_element_type=F32)
    used += jnp.einsum("hbt,btd->bhd", p_low, final_own, preferred_element_type=F32)
    pooled = fold_heads(mm_exact(used.reshape(own * HEADS, width), pw_v.astype(F32)))
    head_start = mm_exact(pooled, pw_out.astype(F32))
    head_normed = layer_norm(head_start, ivec[8], ivec[9]).astype(BF)
    h_value, h_slope = gelu_pair(mm(head_normed, pw_up) + p_bias)
    head_active = h_value.astype(BF)
    image_embed = head_start + mm(head_active, pw_down) + ivec[10]

    embeds = lax.all_gather(jnp.stack([image_embed, text_embed], 1), ALL, axis=0, tiled=True)
    every_image, every_text = embeds[:, 0], embeds[:, 1]
    labels = (2 * pairs - 1).astype(F32)
    total = every_image.shape[0]
    i_scale = lax.rsqrt(jnp.sum(every_image * every_image, -1, keepdims=True) + EPS)
    t_scale = lax.rsqrt(jnp.sum(every_text * every_text, -1, keepdims=True) + EPS)
    z_i, z_t = every_image * i_scale, every_text * t_scale
    cosine = mm_exact(z_i, z_t, 1, 1)
    temper = jnp.exp(temp_bias[0])
    logits = cosine * temper + temp_bias[1]
    loss = -jnp.sum(jax.nn.log_sigmoid(labels * logits)) / total
    g = -labels * jax.nn.sigmoid(-labels * logits) / total
    grad_temp = jnp.stack([temper * jnp.sum(g * cosine), jnp.sum(g)])
    dz_i = temper * mm_exact(g, z_t)
    dz_t = temper * mm_exact(g, z_i, 0, 0)
    all_d_image = (dz_i - z_i * jnp.sum(z_i * dz_i, -1, keepdims=True)) * i_scale
    all_d_text = (dz_t - z_t * jnp.sum(z_t * dz_t, -1, keepdims=True)) * t_scale
    d_image = lax.dynamic_slice_in_dim(all_d_image, me * own, own, 0)
    d_text = lax.dynamic_slice_in_dim(all_d_text, me * own, own, 0)

    h_upper = mm_exact(d_image, pw_down.astype(F32), 1, 1) * h_slope
    h_norm = mm_exact(h_upper, pw_up.astype(F32), 1, 1)
    d_start, dv8, dv9 = norm_back(head_start, ivec[8], h_norm)
    d_start = d_image + d_start
    dv10 = jnp.sum(d_image, 0)
    d_pooled = mm_exact(d_start, pw_out.astype(F32), 1, 1)
    p_values = mm_exact(spread_heads(d_pooled), pw_v.astype(F32), 1, 1).reshape(own, HEADS, width)
    v_high, v_low = split_two(p_values)
    d_probs = jnp.einsum("bhd,btd->hbt", v_high, final_own, preferred_element_type=F32)
    d_probs += jnp.einsum("bhd,btd->hbt", v_low, final_own, preferred_element_type=F32)
    d_scores = pool_probs * (d_probs - jnp.sum(pool_probs * d_probs, -1, keepdims=True))
    s_high, s_low = split_two(d_scores)
    p_used = jnp.einsum("hbt,btd->bhd", s_high, final_own, preferred_element_type=F32)
    p_used += jnp.einsum("hbt,btd->bhd", s_low, final_own, preferred_element_type=F32)
    d_query = jnp.sum(fold_heads(mm_exact(p_used.reshape(own * HEADS, width), pw_k.astype(F32))), 0) * factor
    d_final = jnp.einsum(
        "hbt,bhd->btd",
        jnp.concatenate([s_high, p_high], 0),
        jnp.concatenate([jnp.broadcast_to(k_high[None], (own, HEADS, width)), v_high], 1),
        preferred_element_type=F32,
    ).reshape(own * length, width)
    dy, dv5, dv6 = norm_back(block_out, ivec[5], d_final)

    d_branch = dy.astype(BF)
    g_down = mm(active, d_branch, 0, 0)
    dv4 = jnp.sum(dy, 0)
    d_upper_f = mm(d_branch, w_down, 1, 1) * slope.astype(F32)
    d_upper = d_upper_f.astype(BF)
    g_bias = jnp.sum(d_upper_f, 0)
    g_up = mm(second, d_upper, 0, 0)
    d_hidden, dv2, dv3 = norm_back(hidden, ivec[2], mm(d_upper, w_up, 1, 1))
    d_hidden = dy + d_hidden
    d_attend = d_hidden.astype(BF)
    g_out = mm(mixed, d_attend, 0, 0)
    d_mixed = mm(d_attend, w_out, 1, 1).astype(BF)

    def scatter(*grads):
        flat = jnp.concatenate([g.astype(BF).reshape(world, -1, width) for g in grads], 1)
        mine = lax.psum_scatter(flat, ALL, scatter_dimension=0, tiled=False).astype(F32)
        out, at = [], 0
        for g in grads:
            count = g.size // world // width
            out.append(mine[at : at + count].reshape(g.shape[0] // world, g.shape[1]))
            at += count
        return out

    own_up, own_down, own_out = scatter(g_up, g_down, g_out)
    inner_rows = jnp.sum(
        (d_mixed.astype(F32) * mixed.astype(F32)).reshape(own * length, HEADS, head_width), -1
    ).T.reshape(HEADS // 2, 2, own * length)
    d_q, d_k, d_v = attend_bwd(proj, d_mixed, lse, inner_rows, length)
    g_in = jnp.concatenate([mm(normed, d, 0, 0) for d in (d_q, d_k, d_v)], 1)
    (own_in,) = scatter(g_in)
    d_normed = (
        mm(d_q, w_in[:, :width], 1, 1)
        + mm(d_k, w_in[:, width : 2 * width], 1, 1)
        + mm(d_v, w_in[:, 2 * width :], 1, 1)
    )
    d_x, dv0, dv1 = norm_back(x, ivec[0], d_normed)
    d_x = (d_hidden + d_x).reshape(own, length, width)

    def to_tokens(v):
        return lax.all_to_all(v.astype(BF), "seq", 1, 0, tiled=True).astype(F32)

    grad_patches = to_tokens(d_x)

    dt_final = mm_exact(d_text, tw_head.astype(F32), 1, 1)
    dt_out, tv5, tv6 = norm_back(t_out, tvec[5], dt_final)
    dt_branch = dt_out.astype(BF)
    tv4 = jnp.sum(dt_out, 0)
    dt_upper = (mm(dt_branch, tw_down, 1, 1) * t_slope).astype(BF)
    dt_hidden, tv2, tv3 = norm_back(t_hidden, tvec[2], mm(dt_upper, tw_up, 1, 1))
    dt_hidden = dt_out + dt_hidden
    dt_attend = dt_hidden.astype(BF)
    dt_mixed = mm(dt_attend, tw_out, 1, 1).astype(BF)
    t_values = mm(spread_heads(dt_mixed.astype(F32)).astype(BF), tw_v, 1, 1).reshape(own, HEADS, width)
    tv_high, tv_low = split_two(t_values)
    dt_probs = jnp.einsum("bsd,bhd->bsh", t_normed, tv_high, preferred_element_type=F32)
    dt_probs += jnp.einsum("bsd,bhd->bsh", t_normed, tv_low, preferred_element_type=F32)
    dt_scores = t_probs * (dt_probs - jnp.sum(t_probs * dt_probs, 1, keepdims=True))
    tk_used = jnp.einsum("bsh,bsd->bhd", dt_scores, t_normed.astype(F32), precision=HIGH)
    dt_q = fold_heads(mm(tk_used.reshape(own * HEADS, width).astype(BF), tw_k)) * factor
    dt_q = dt_q.astype(BF)
    dt_normed = jnp.einsum("bsh,bhd->bsd", dt_scores, t_keys, precision=HIGH)
    dt_normed += jnp.einsum("bsh,bhd->bsd", t_probs, t_values, precision=HIGH)
    dt_normed = dt_normed.at[:, -1].add(mm(dt_q, tw_q, 1, 1))
    flat_x = t_x.reshape(own * text_length, width)
    dt_x, tv0, tv1 = norm_back(flat_x, tvec[0], dt_normed.reshape(own * text_length, width))
    dt_x = dt_x.reshape(own, text_length, width).at[:, -1].add(dt_hidden)
    grad_captions = to_tokens(dt_x)

    whole = jnp.concatenate(
        [v.astype(F32) for v in (h_upper, d_start, d_pooled, dt_branch, dt_upper, dt_attend, dt_q, t_q, dt_mixed)], 1
    )
    whole = lax.all_gather(whole, ALL, axis=0, tiled=True)
    at = [0]

    def take(count):
        at[0] += count
        return whole[:, at[0] - count : at[0]]

    a_h_upper, a_start, a_pooled, a_branch, a_upper, a_attend, a_q, a_query, a_mixed = (
        take(c) for c in (hidden_width, width, width, width, hidden_width, width, width, width, width)
    )
    columns = [pooled, head_normed, t_last, t_mixed, t_second, t_final]
    columns += [used, t_used, tk_used * factor]
    columns += [head_active, t_active]
    columns = jnp.concatenate(
        [v.astype(F32).reshape(own, -1, width) for v in columns], 1
    )
    wide = 2 * (hidden_width // width)
    narrow = columns.shape[1] - wide
    cut = jnp.concatenate(
        [
            columns[:, :narrow].reshape(own, narrow, world, part).transpose(2, 0, 1, 3).reshape(world, own, -1),
            columns[:, narrow:].reshape(own, 2, world, wide_part).transpose(2, 0, 1, 3).reshape(world, own, -1),
        ],
        2,
    )
    cut = lax.all_to_all(cut, ALL, 0, 0, tiled=True).reshape(total, -1)
    slim = cut[:, : narrow * part].reshape(total, narrow, part)
    broad = cut[:, narrow * part :].reshape(total, 2, wide_part)

    def outer(rows, cols):
        return mm_exact(rows, cols, 0, 0)

    def outer_heads(rows, cols):
        cols = cols.reshape(total, HEADS, head_width)
        return jnp.einsum("chm,che->mhe", rows, cols, precision=HIGH).reshape(part, width)

    c_pooled, c_head, c_last, c_mixed, c_second, c_final = (slim[:, i] for i in range(6))
    c_used, ct_used, ctk_used = (slim[:, 6 + i * HEADS : 6 + (i + 1) * HEADS] for i in range(3))
    own_t_in = jnp.concatenate(
        [outer(c_last, a_q), outer_heads(ctk_used, a_query), outer_heads(ct_used, a_mixed)], 1
    )
    own_t_out = outer(c_mixed, a_attend)
    own_t_up = outer(c_second, a_upper)
    own_t_down = outer(broad[:, 1], a_branch)
    own_t_head = outer(c_final, all_d_text)
    own_p_out = outer(c_pooled, a_start)
    own_p_up = outer(c_head, a_h_upper)
    own_p_down = outer(broad[:, 0], all_d_image)
    own_p_values = outer_heads(c_used, a_pooled)

    summed = jnp.concatenate(
        [
            jnp.stack([dv0, dv1, dv2, dv3, dv4, dv5, dv6, dv8, dv9, dv10]),
            jnp.stack([tv0, tv1, tv2, tv3, tv4, tv5, tv6]),
            d_query[None],
            jnp.sum(p_used, 0),
            g_bias.reshape(-1, width),
        ],
        0,
    )
    summed = lax.psum(summed, ALL)
    total_query = summed[17]
    mine = lambda v, n: lax.dynamic_slice_in_dim(v, me * n, n, -1)
    own_probe = mine(ivec[7], part)
    own_p_query = own_probe[:, None] * total_query[None, :]
    dv7 = jnp.sum(probe_query_weight.astype(F32) * total_query[None, :], 1)
    pk_used = mine(summed[18 : 18 + HEADS], part)
    own_p_keys = jnp.einsum(
        "hm,he->mhe", pk_used, probe_query.reshape(HEADS, head_width) * factor
    ).reshape(part, width)
    own_p_pair = jnp.concatenate([own_p_keys, own_p_values], 1)
    ten = mine(summed[:10], part)
    own_ivec = jnp.concatenate([ten[:7], dv7[None], ten[7:]], 0)
    own_tvec = mine(summed[10:17], part)
    own_bias = mine(summed[18 + HEADS :].reshape(-1), wide_part)
    own_p_bias = mine(jnp.sum(a_h_upper, 0), wide_part)
    own_t_bias = mine(jnp.sum(a_upper, 0), wide_part)
    return (
        loss, grad_patches, grad_captions,
        own_in, own_out, own_up, own_bias, own_down, own_ivec,
        own_p_query, own_p_pair, own_p_out, own_p_up, own_p_bias, own_p_down,
        own_t_in, own_t_out, own_t_up, own_t_bias, own_t_down, own_tvec, own_t_head,
        grad_temp,
    )


MESH = pl.DeviceIdType.MESH

class Place:
    def __init__(self):
        i = lax.axis_index("dp")
        self.i, self.z = i, lax.axis_index("seq")
        self.y, self.x, self.c = i // 4, (i // 2) % 2, i % 2
        self.at_y = (i + 4 - 8 * self.y, self.z)
        self.at_x = (i + 2 - 4 * self.x, self.z)
        self.at_c = (i + 1 - 2 * self.c, self.z)

    def at_z(self, k):
        return (self.i, (self.z + k) % 4)

def greet(peers):
    barrier = pltpu.get_barrier_semaphore()
    for p in peers:
        pl.semaphore_signal(barrier, inc=1, device_id=p, device_id_type=MESH)
    pl.semaphore_wait(barrier, len(peers))

def gather_kernel(kinds, *refs):
    n = len(kinds)
    srcs, outs = refs[:n], refs[n:2 * n]
    send, recv, local = refs[2 * n:]
    me = Place()
    y, x, c, z = me.y, me.x, me.c, me.z
    greet([me.at_z(1), me.at_z(2), me.at_z(3), me.at_x, me.at_y, me.at_c])
    started = []
    pending = {}

    def push(a, slot, src, dst, dev, arriving):
        copy = pltpu.make_async_remote_copy(src, dst, send.at[a, slot], recv.at[a, slot], device_id=dev, device_id_type=MESH)
        copy.start()
        started.append(copy)
        return pltpu.make_async_remote_copy(arriving, arriving, send.at[a, slot], recv.at[a, slot], device_id=dev, device_id_type=MESH)

    def stage(a, s):
        kind, order = kinds[a]
        src, out = srcs[a], outs[a]
        for w in pending.pop((a, s - 1), []):
            w()
        waits = []
        if s == 0:
            if kind in ("full", "zg"):
                own = src
            elif kind in ("cols", "za"):
                own = src.at[z]
            else:
                own = src
            home = out.at[y, x, c, z] if kind in ("full", "cols") else out.at[z] if kind in ("zg", "za") else out.at[y, x, c]
            cp = pltpu.make_async_copy(own, home, local.at[a])
            cp.start()
            waits.append(cp.wait)
            if kind != "plane":
                for k in (1, 2, 3):
                    to, fro = (z + k) % 4, (z + 4 - k) % 4
                    s_ref = src.at[to] if kind in ("cols", "za") else src
                    if kind in ("full", "cols"):
                        dst, arr = out.at[y, x, c, z], out.at[y, x, c, fro]
                    else:
                        dst, arr = out.at[z], out.at[fro]
                    waits.append(push(a, k - 1, s_ref, dst, me.at_z(k), arr).wait_recv)
        elif kind in ("zg", "za"):
            return
        elif s == 1:
            if order in ("C", "S"):
                cut = (lambda r: r) if order == "C" else (lambda r: r.at[..., 0:r.shape[-1] // 2])
                waits.append(push(a, 3, cut(out.at[y, x, c]), cut(out.at[y, x, c]), me.at_x, cut(out.at[y, 1 - x, c])).wait_recv)
            if order in ("D", "S"):
                cut = (lambda r: r) if order == "D" else (lambda r: r.at[..., r.shape[-1] // 2:])
                waits.append(push(a, 4, cut(out.at[y, x, c]), cut(out.at[y, x, c]), me.at_y, cut(out.at[1 - y, x, c])).wait_recv)
        elif s == 2:
            if order in ("C", "S"):
                cut = (lambda r: r) if order == "C" else (lambda r: r.at[..., 0:r.shape[-1] // 2])
                waits.append(push(a, 5, cut(out.at[y, :, c]), cut(out.at[y, :, c]), me.at_y, cut(out.at[1 - y, :, c])).wait_recv)
            if order in ("D", "S"):
                cut = (lambda r: r) if order == "D" else (lambda r: r.at[..., r.shape[-1] // 2:])
                waits.append(push(a, 6, cut(out.at[:, x, c]), cut(out.at[:, x, c]), me.at_x, cut(out.at[:, 1 - x, c])).wait_recv)
        elif s == 3:
            waits.append(push(a, 7, out.at[:, :, c], out.at[:, :, c], me.at_c, out.at[:, :, 1 - c]).wait_recv)
        pending[(a, s)] = waits

    for t in range(n + 4):
        for a in range(max(0, t - 4), min(n, t + 1)):
            stage(a, t - a)
    for key in list(pending):
        for w in pending.pop(key):
            w()
    for copy in started:
        copy.wait_send()

def gather(ops, kinds, cid):
    shapes = []
    for o, (kind, _) in zip(ops, kinds):
        if kind == "full":
            s = (2, 2, 2, 4) + o.shape
        elif kind == "cols":
            s = (2, 2, 2, 4) + o.shape[1:]
        elif kind == "plane":
            s = (2, 2, 2) + o.shape
        elif kind == "zg":
            s = (4,) + o.shape
        else:
            s = o.shape
        shapes.append(jax.ShapeDtypeStruct(s, o.dtype))
    n = len(ops)
    return pl.pallas_call(
        partial(gather_kernel, kinds),
        out_shape=shapes,
        in_specs=[pl.BlockSpec(memory_space=pl.ANY)] * n,
        out_specs=[pl.BlockSpec(memory_space=pl.ANY)] * n,
        scratch_shapes=[pltpu.SemaphoreType.DMA((n, 8)), pltpu.SemaphoreType.DMA((n, 8)), pltpu.SemaphoreType.DMA((n,))],
        compiler_params=pltpu.CompilerParams(collective_id=cid, has_side_effects=True),
    )(*ops)

def reduce_kernel(g_ref, dx_ref, own_ref, moved_ref, from_c, acc_c, from_1, acc_1, from_2, acc_2, from_z, send, recv, local):
    me = Place()
    y, x, c, z = me.y, me.x, me.c, me.z
    greet([me.at_z(1), me.at_z(2), me.at_z(3), me.at_x, me.at_y, me.at_c])
    half = g_ref.shape[-1] // 2
    started = []

    def push(slot, src, dst, dev, arriving):
        copy = pltpu.make_async_remote_copy(src, dst, send.at[slot], recv.at[slot], device_id=dev, device_id_type=MESH)
        copy.start()
        started.append(copy)
        return pltpu.make_async_remote_copy(src, arriving, send.at[slot], recv.at[slot], device_id=dev, device_id_type=MESH)

    a_c = push(0, g_ref.at[:, :, 1 - c], from_c, me.at_c, from_c)
    home = pltpu.make_async_copy(g_ref.at[:, :, c], acc_c, local.at[0])
    home.start()
    rest = []
    for k in (1, 2, 3):
        to, fro = (z + k) % 4, (z + 4 - k) % 4
        rest.append(push(k, dx_ref.at[to], moved_ref.at[z], me.at_z(k), moved_ref.at[fro]))
    keep = pltpu.make_async_copy(dx_ref.at[z], moved_ref.at[z], local.at[1])
    keep.start()
    home.wait()
    a_c.wait_recv()
    f32 = lambda v: v.astype(jnp.float32)
    for a in range(2):
        for b in range(2):
            for q in range(4):
                acc_c[a, b, q] = (f32(acc_c[a, b, q]) + f32(from_c[a, b, q])).astype(acc_c.dtype)
    left, right = slice(0, half), slice(half, 2 * half)
    a_y = push(4, acc_c.at[1 - y, :, :, :, left], from_1.at[0], me.at_y, from_1.at[0])
    a_x = push(5, acc_c.at[:, 1 - x, :, :, right], from_1.at[1], me.at_x, from_1.at[1])
    a_y.wait_recv()
    for b in range(2):
        for q in range(4):
            acc_1[0, b, q] = (f32(acc_c[y, b, q, :, left]) + f32(from_1[0, b, q])).astype(acc_1.dtype)
    b_x = push(6, acc_1.at[0, 1 - x], from_2.at[0], me.at_x, from_2.at[0])
    a_x.wait_recv()
    for b in range(2):
        for q in range(4):
            acc_1[1, b, q] = (f32(acc_c[b, x, q, :, right]) + f32(from_1[1, b, q])).astype(acc_1.dtype)
    b_y = push(7, acc_1.at[1, 1 - y], from_2.at[1], me.at_y, from_2.at[1])
    b_x.wait_recv()
    for q in range(4):
        acc_2[q, :, left] = (f32(acc_1[0, x, q]) + f32(from_2[0, q])).astype(acc_2.dtype)
    b_y.wait_recv()
    for q in range(4):
        acc_2[q, :, right] = (f32(acc_1[1, y, q]) + f32(from_2[1, q])).astype(acc_2.dtype)
    last = []
    for k in (1, 2, 3):
        to, fro = (z + k) % 4, (z + 4 - k) % 4
        last.append(push(7 + k, acc_2.at[to], from_z.at[k - 1], me.at_z(k), from_z.at[k - 1]))
    total = f32(acc_2[z])
    for k in (1, 2, 3):
        last[k - 1].wait_recv()
        total += f32(from_z[k - 1])
    own_ref[...] = total
    keep.wait()
    for r in rest:
        r.wait_recv()
    for copy in started:
        copy.wait_send()

def reduce_and_move(g, dx, cid):
    rows, n = g.shape[0] // 32, g.shape[1]
    g = g.reshape(2, 2, 2, 4, rows, n)
    dx = dx.reshape(4, dx.shape[0] // 4, dx.shape[1])
    hbm = pl.BlockSpec(memory_space=pl.ANY)
    v = lambda *s: pltpu.VMEM(s, g.dtype)
    return pl.pallas_call(
        reduce_kernel,
        in_specs=[hbm, hbm],
        out_specs=[pl.BlockSpec(memory_space=pltpu.VMEM), hbm],
        out_shape=[jax.ShapeDtypeStruct((rows, n), jnp.float32), jax.ShapeDtypeStruct(dx.shape, dx.dtype)],
        scratch_shapes=[
            v(2, 2, 4, rows, n), v(2, 2, 4, rows, n), v(2, 2, 4, rows, n // 2), v(2, 2, 4, rows, n // 2),
            v(2, 4, rows, n // 2), v(4, rows, n), v(3, rows, n),
            pltpu.SemaphoreType.DMA((11,)), pltpu.SemaphoreType.DMA((11,)), pltpu.SemaphoreType.DMA((2,)),
        ],
        compiler_params=pltpu.CompilerParams(collective_id=cid, has_side_effects=True, vmem_limit_bytes=40 << 20),
    )(g, dx)

ROWS = 80

def middle_kernel(final_ref, block_ref, tokens_ref, tp_ref, outs_ref, ivec_ref, tvec_ref, pbias_ref, tbias_ref,
                  label_ref, temp_ref,
                  dy_ref, branch_ref, rows_ref, sums_ref, dcap_ref, loss_ref, dz_ref,
                  tn_ref, dn_ref, send_a, recv_a, send_l, recv_l, send_t, recv_t, send_sem, recv_sem):
    me = Place()
    z, i = me.z, me.i
    n_dp = recv_l.shape[0]
    plane = [((i + k) % n_dp, z) for k in range(1, n_dp)]
    greet([me.at_z(1), me.at_z(2), me.at_z(3)] + plane)
    width = final_ref.shape[1]
    part = width // 4
    started = []

    def exchange(n, values_for):
        for q in range(4):
            send_a[n, q] = values_for(q)
        recv_a[n, z] = send_a[n, z]
        arrive = []
        for k in (1, 2, 3):
            to, fro = (z + k) % 4, (z + 4 - k) % 4
            copy = pltpu.make_async_remote_copy(send_a.at[n, to], recv_a.at[n, z], send_sem.at[n, k - 1],
                                                recv_sem.at[n, k - 1], device_id=me.at_z(k), device_id_type=MESH)
            copy.start()
            started.append(copy)
            arrive.append(pltpu.make_async_remote_copy(send_a.at[n, to], recv_a.at[n, fro], send_sem.at[n, k - 1],
                                                       recv_sem.at[n, k - 1], device_id=me.at_z(k), device_id_type=MESH))

        def done():
            for a in arrive:
                a.wait_recv()
            return [recv_a[n, q] for q in range(4)]

        return done

    pad4 = jnp.zeros((4, width), F32)
    pad1 = jnp.zeros((1, width), F32)
    ivec, tvec = ivec_ref[...], tvec_ref[...]
    iv = lambda k: ivec[k:k + 1]
    tv = lambda k: tvec[k:k + 1]
    names = ["tq", "tk", "tv", "thead", "pq", "pk", "pv"]
    col = {n: 2 * width + 256 * k for k, n in enumerate(names)}
    small = lambda n: tp_ref[:, col[n]:col[n] + 256]
    p_up = lambda: tp_ref[:, 0:width]
    t_up = lambda: tp_ref[:, width:2 * width]
    base = 2 * width + 256 * 7
    t_down = lambda: tp_ref[:, base:base + width]
    p_down = lambda: tp_ref[:, base + width:base + 2 * width]
    t_out_w = lambda: outs_ref[0:part, 0:width]
    p_out_w = lambda: outs_ref[0:part, width:2 * width]
    lane = lax.broadcasted_iota(jnp.int32, (1, 256), 1)
    own = [((lane >= 64 * h) & (lane < 64 * h + 64)).astype(F32) for h in range(3)]

    def spread(a):
        return jnp.concatenate([a * own[h] for h in range(3)], 0)

    def fold(a):
        n = a.shape[0] // 3
        return sum(a[h * n:(h + 1) * n] * own[h] for h in range(3))

    t_x = tokens_ref[...].astype(F32)
    tn = layer_norm(t_x, tv(0), tv(1)).astype(BF)
    tn_ref[...] = tn.astype(F32)
    last_at = [3 * 64 + 16 * c + 15 for c in range(4)]
    t_last = jnp.concatenate([tn_ref[r:r + 1, :] for r in last_at], 0)
    x_last = jnp.concatenate([tokens_ref[3 * 64 + 16 * c:3 * 64 + 16 * c + 16, :].astype(F32)[15:16] for c in range(4)], 0)
    t_q = mm(t_last.astype(BF), small("tq")).astype(BF).astype(F32)
    t_keys = mm(spread(t_q).astype(BF), small("tk"), 1, 1) * 0.125
    scores = mm_two(t_keys, tn, 1)
    col_id = (lax.broadcasted_iota(jnp.int32, scores.shape, 1) // 16) % 4
    row_id = lax.broadcasted_iota(jnp.int32, scores.shape, 0) % 4
    mine = col_id == row_id
    top = jnp.max(jnp.where(mine, scores, -1e30), -1, keepdims=True)
    e = jnp.where(mine, jnp.exp(jnp.where(mine, scores - top, 0.0)), 0.0)
    t_probs = e / jnp.sum(e, -1, keepdims=True)
    t_used = mm_two(t_probs, tn)
    t_mixed = fold(mm(t_used.astype(BF), small("tv"))).astype(BF)
    t_part = mm(t_mixed[:, 0:part], t_out_w())

    p_q = mm(iv(7).astype(BF), small("pq"))
    p_keys_my = mm_two(spread(p_q), small("pk"), 1) * 0.125
    block = jnp.concatenate([t_part, p_keys_my, pad1], 0)
    x0 = exchange(0, lambda q: block)()
    t_hidden = x_last + (x0[0] + x0[1] + x0[2] + x0[3])[0:4]
    p_keys = jnp.concatenate([x0[q][4:7] for q in range(4)], 0)
    t_second = layer_norm(t_hidden, tv(2), tv(3)).astype(BF)
    t_value, t_slope = gelu_pair(mm(t_second, t_up()) + tbias_ref[...])
    t_active = t_value.astype(BF)
    t_part = mm(t_active, t_down())
    final = final_ref[...]
    p_scores = mm_two(p_keys, final, 1)
    e = jnp.exp(p_scores - jnp.max(p_scores, -1, keepdims=True))
    p_probs = e / jnp.sum(e, -1, keepdims=True)
    used = mm_two(p_probs, final)
    x1 = exchange(1, lambda q: jnp.concatenate([t_part, used[3 * q:3 * q + 3], pad1], 0))()
    t_out = t_hidden + (x1[0] + x1[1] + x1[2] + x1[3])[0:4] + tv(4)
    t_final = layer_norm(t_out, tv(5), tv(6)).astype(BF)
    t_piece = mm(t_final, small("thead"))
    got = jnp.concatenate([x1[q][4 + h:5 + h] for h in range(3) for q in range(4)], 0)
    pooled = fold(mm_two(got, small("pv")))
    h_part = mm_two(pooled[:, 0:part], p_out_w())
    block = jnp.concatenate([h_part, jnp.concatenate([t_piece[:, 0:part], jnp.zeros((4, width - part), F32)], 1)], 0)
    x2 = exchange(2, lambda q: block)()
    h_start = (x2[0] + x2[1] + x2[2] + x2[3])[0:4]
    text_embed = jnp.concatenate([x2[q][4:8, 0:part] for q in range(4)], 1)
    h_normed = layer_norm(h_start, iv(8), iv(9)).astype(BF)
    h_value, h_slope = gelu_pair(mm(h_normed, p_up()) + pbias_ref[...])
    h_active = h_value.astype(BF)
    h_part = mm(h_active, p_down())
    block = jnp.concatenate([h_part, pad4], 0)
    x3 = exchange(3, lambda q: block)()
    image_embed = h_start + ((x3[0] + x3[1] + x3[2] + x3[3])[0:4] + iv(10))
    send_l[...] = jnp.concatenate([image_embed, text_embed], 0)
    recv_l[i] = send_l[...]
    arrive = []
    for k in range(1, n_dp):
        copy = pltpu.make_async_remote_copy(send_l, recv_l.at[i], send_sem.at[8, k], recv_sem.at[8, k],
                                            device_id=plane[k - 1], device_id_type=MESH)
        copy.start()
        started.append(copy)
        arrive.append(pltpu.make_async_remote_copy(send_l, recv_l.at[(i + n_dp - k) % n_dp], send_sem.at[8, k], recv_sem.at[8, k],
                                                   device_id=plane[k - 1], device_id_type=MESH))
    for a in arrive:
        a.wait_recv()
    every = jnp.concatenate([recv_l[k] for k in range(n_dp)], 0)
    scale = lax.rsqrt(jnp.sum(every * every, -1, keepdims=True) + EPS)
    unit = every * scale
    cosine = mm_exact(unit, unit, 1, 1)
    temper = jnp.exp(jnp.full((1, 1), temp_ref[0], F32))
    logits = cosine * temper + temp_ref[1]
    label = label_ref[...]
    valid = label != 0.0
    signed = label * logits
    total = n_dp * 4
    nll = jnp.maximum(-signed, 0.0) + jnp.log(1.0 + jnp.exp(-jnp.abs(signed)))
    add_all = lambda a: jnp.sum(jnp.sum(a, -1, keepdims=True), 0, keepdims=True)
    loss = add_all(jnp.where(valid, nll, 0.0)) / total
    g = jnp.where(valid, -label / (1.0 + jnp.exp(signed)), 0.0) / total
    gt0 = temper * add_all(g * cosine)
    gt1 = add_all(g)
    at = lax.broadcasted_iota(jnp.int32, (8, 128), 1)
    loss_ref[...] = jnp.where(at == 0, loss, jnp.where(at == 1, gt0, gt1))
    dz = temper * mm_exact(g + jnp.transpose(g), unit)
    dz_ref[...] = (dz - unit * jnp.sum(unit * dz, -1, keepdims=True)) * scale
    d_both = dz_ref[pl.ds(pl.multiple_of(8 * i, 8), 8), :]
    d_image, d_text = d_both[0:4], d_both[4:8]

    dh_upper = mm_two(d_image, p_down(), 1) * h_slope
    h_part = mm_two(dh_upper, p_up(), 1)
    d_text_my = sum(jnp.where(z == q, d_text[:, part * q:part * q + part], 0.0) for q in range(4))
    t_part = mm_two(d_text_my, small("thead")[:, 0:part], 1)
    block = jnp.concatenate([h_part, t_part], 0)
    x4 = exchange(4, lambda q: block)()
    both = x4[0] + x4[1] + x4[2] + x4[3]
    d_start, dv8, dv9 = norm_back_rows(h_start, iv(8), both[0:4])
    d_start = d_image + d_start
    dv10 = jnp.sum(d_image, 0, keepdims=True)
    d_pooled = mm_two(d_start, p_out_w(), 1)
    d_pooled = jnp.concatenate([d_pooled, jnp.zeros((4, 256 - part), F32)], 1)
    p_values_my = mm_two(spread(d_pooled), small("pv"), 1)
    dt_out, tv5, tv6 = norm_back_rows(t_out, tv(5), both[4:8])
    tv4 = jnp.sum(dt_out, 0, keepdims=True)
    dt_branch = dt_out.astype(BF)
    dt_upper = (mm(dt_branch, t_down(), 1, 1) * t_slope).astype(BF)
    t_part = mm(dt_upper, t_up(), 1, 1)
    x5 = exchange(5, lambda q: jnp.concatenate(
        [t_part] + [p_values_my[4 * h + q:4 * h + q + 1] for h in range(3)] + [pad1], 0))()
    dt_hidden, tv2, tv3 = norm_back_rows(t_hidden, tv(2), (x5[0] + x5[1] + x5[2] + x5[3])[0:4])
    dt_hidden = dt_out + dt_hidden
    dt_attend = dt_hidden.astype(BF)
    dt_mixed = mm(dt_attend, t_out_w(), 1, 1).astype(BF).astype(F32)
    dt_mixed = jnp.concatenate([dt_mixed, jnp.zeros((4, 256 - part), F32)], 1)
    t_values = mm(spread(dt_mixed).astype(BF), small("tv"), 1, 1)
    dt_probs = mm_two(t_values, tn, 1)
    dt_scores = t_probs * (dt_probs - jnp.sum(t_probs * dt_probs, -1, keepdims=True))
    tk_used = mm_two(dt_scores, tn) * 0.125
    dt_q = fold(mm(tk_used.astype(BF), small("tk"))).astype(BF)
    dn = mm(dt_scores.astype(BF), t_keys.astype(BF), 0, 0) + mm(t_probs.astype(BF), t_values.astype(BF), 0, 0)
    row_at = lax.broadcasted_iota(jnp.int32, dn.shape, 0)
    dq_back = mm(dt_q, small("tq"), 1, 1)
    for c in range(4):
        dn = dn + jnp.where(row_at == last_at[c], dq_back[c:c + 1], 0.0)
    dn_ref[...] = dn.astype(BF)
    p_values = jnp.concatenate([x5[q][4:7] for q in range(4)], 0)
    d_probs = mm_two(p_values, final, 1)
    d_scores = p_probs * (d_probs - jnp.sum(p_probs * d_probs, -1, keepdims=True))
    p_used = mm_two(d_scores, final) * 0.125
    x6 = exchange(6, lambda q: jnp.concatenate([p_used[3 * q:3 * q + 3], pad1, pad4], 0))
    arrive = []
    for k in (1, 2, 3):
        to, fro = (z + k) % 4, (z + 4 - k) % 4
        rows_to = dn_ref.at[pl.ds(pl.multiple_of(64 * to, 64), 64), :]
        copy = pltpu.make_async_remote_copy(rows_to, recv_t.at[z], send_sem.at[7, k], recv_sem.at[7, k],
                                            device_id=me.at_z(k), device_id_type=MESH)
        copy.start()
        started.append(copy)
        arrive.append(pltpu.make_async_remote_copy(rows_to, recv_t.at[fro], send_sem.at[7, k], recv_sem.at[7, k],
                                                   device_id=me.at_z(k), device_id_type=MESH))
    s_high, s_low = split_two(d_scores)
    q_high, q_low = split_two(p_probs)
    k_high, k_low = split_two(p_keys)
    v_high, v_low = split_two(p_values)
    left = jnp.concatenate([s_high.astype(F32), q_high.astype(F32)], 0)
    right = jnp.concatenate([k_high.astype(F32), v_high.astype(F32)], 0).astype(BF)
    send_t[...] = jnp.transpose(jnp.concatenate([left, jnp.zeros((104, left.shape[1]), F32)], 0))
    right = jnp.concatenate([right, jnp.zeros((104, width), BF)], 0)
    sums_ref[...] = jnp.zeros_like(sums_ref)
    tile = 128

    def step(n, carry):
        at_rows = pl.ds(pl.multiple_of(n * tile, tile), tile)
        d_final = mm(send_t[at_rows, :].astype(BF), right)
        d_y, gain, shift = norm_back_rows(block_ref[at_rows, :], iv(5), d_final)
        dy_ref[at_rows, :] = d_y
        branch_ref[at_rows, :] = d_y.astype(BF)
        sums_ref[5:6] += gain
        sums_ref[6:7] += shift
        sums_ref[4:5] += jnp.sum(d_y, 0, keepdims=True)
        return carry

    lax.fori_loop(0, final_ref.shape[0] // tile, step, 0)
    got6 = x6()
    w_got = jnp.concatenate([got6[q][h:h + 1] for h in range(3) for q in range(4)], 0)
    dq_rows = fold(mm_two(w_got, small("pk")))
    dq_my = jnp.sum(dq_rows, 0, keepdims=True)
    recv_t[z] = dn_ref[pl.ds(pl.multiple_of(64 * z, 64), 64), :]
    for a in arrive:
        a.wait_recv()
    dt_normed = sum(recv_t[q].astype(F32) for q in range(4))
    x_mine = tokens_ref[pl.ds(pl.multiple_of(64 * z, 64), 64), :].astype(F32)
    d_cap, tv0, tv1 = norm_back_rows(x_mine, tv(0), dt_normed)
    row_c = lax.broadcasted_iota(jnp.int32, d_cap.shape, 0)
    for c in range(4):
        d_cap = d_cap + jnp.where((row_c == 16 * c + 15) & (z == 3), dt_hidden[c:c + 1], 0.0)
    dcap_ref[...] = d_cap
    first = (z == 0).astype(F32)
    sums_ref[8:9] = dv8 * first
    sums_ref[9:10] = dv9 * first
    sums_ref[10:11] = dv10 * first
    sums_ref[11:12] = tv0
    sums_ref[12:13] = tv1
    sums_ref[13:14] = tv2 * first
    sums_ref[14:15] = tv3 * first
    sums_ref[15:16] = tv4 * first
    sums_ref[16:17] = tv5 * first
    sums_ref[17:18] = tv6 * first
    own_row = lambda a: sum(jnp.where(z == q, a[q:q + 1].astype(F32), 0.0) for q in range(4))
    pick = lambda a: a[:, 0:part].astype(F32)
    wide = jnp.concatenate
    pieces = [
        dh_upper, dt_upper.astype(F32), h_active.astype(F32), t_active.astype(F32),
        wide([pick(d_pooled), pick(pooled), pick(dt_q), pick(t_q)], 1),
        wide([pick(dt_mixed), pick(t_mixed), jnp.broadcast_to(pick(dq_my), (4, part)), jnp.broadcast_to(pick(p_q), (4, part))], 1),
        own_row(h_normed), own_row(d_start), own_row(t_last), own_row(t_second),
        own_row(dt_attend), own_row(dt_branch), own_row(t_final), pad1,
        used, t_used, tk_used, p_used,
    ]
    rows_ref[...] = jnp.concatenate(pieces, 0)
    for copy in started:
        copy.wait_send()

def middle(final, block_out, tokens, tp, outs, ivec, tvec, pbias, tbias, label, temp, cid, n_dp):
    length, width = final.shape
    v = pl.BlockSpec(memory_space=pltpu.VMEM)
    f = lambda *s: jax.ShapeDtypeStruct(s, F32)
    return pl.pallas_call(
        middle_kernel,
        in_specs=[v] * 10 + [pl.BlockSpec(memory_space=pltpu.SMEM)],
        out_specs=[v] * 7,
        out_shape=[f(length, width), jax.ShapeDtypeStruct((length, width), BF), f(ROWS, width), f(24, width), f(64, width), f(8, 128), f(8 * n_dp, width)],
        scratch_shapes=[
            pltpu.VMEM((256, width), F32), pltpu.VMEM((256, width), BF),
            pltpu.VMEM((7, 4, 8, width), F32), pltpu.VMEM((7, 4, 8, width), F32),
            pltpu.VMEM((8, width), F32), pltpu.VMEM((n_dp, 8, width), F32),
            pltpu.VMEM((length, 128), F32), pltpu.VMEM((4, 64, width), BF),
            pltpu.SemaphoreType.DMA((9, 8)), pltpu.SemaphoreType.DMA((9, 8)),
        ],
        compiler_params=pltpu.CompilerParams(collective_id=cid, has_side_effects=True, vmem_limit_bytes=50 << 20),
    )(final, block_out, tokens, tp, outs, ivec, tvec, pbias, tbias, label, temp)


def fast_program(
    patches, captions, pairs,
    image_attend_in, image_attend_out, image_up_weight, image_up_bias, image_down_weight,
    image_vectors, probe_query_weight, probe_pair_weight, probe_out_weight, probe_up_weight,
    probe_up_bias, probe_down_weight, text_attend_in, text_attend_out, text_up_weight,
    text_up_bias, text_down_weight, text_vectors, text_head_weight, temp_bias,
):
    n_dp, n_z = lax.axis_size("dp"), lax.axis_size("seq")
    world = n_dp * n_z
    at_dp, at_z = lax.axis_index("dp"), lax.axis_index("seq")
    me = at_dp * n_z + at_z
    width = patches.shape[-1]
    head_width = width // HEADS
    hidden_width = image_up_weight.shape[1]
    part, quarter = width // world, width // n_z
    wide_part = hidden_width // world
    fold = hidden_width // width
    length = patches.shape[1] * n_z

    small = jnp.concatenate(
        [image_vectors.reshape(-1), text_vectors.reshape(-1), image_up_bias, probe_up_bias, text_up_bias]
    )
    sizes = [image_vectors.size, text_vectors.size, image_up_bias.size, probe_up_bias.size, text_up_bias.size]
    small = jnp.pad(small, (0, 2048 - small.shape[0])).reshape(16, 128)

    def by_units(w):
        return w.reshape(part, n_dp, n_z, wide_part).transpose(2, 0, 1, 3).reshape(n_z, part, width)

    def by_heads(w):
        cut = w.reshape(part, n_z, quarter).transpose(1, 0, 2)
        return jnp.pad(cut, ((0, 0), (0, 0), (0, 256 - quarter)))

    split = [by_units(probe_up_weight), by_units(text_up_weight)]
    split += [by_heads(text_attend_in[:, k * width : (k + 1) * width]) for k in range(3)]
    split += [by_heads(text_head_weight), by_heads(probe_query_weight)]
    split += [by_heads(probe_pair_weight[:, k * width : (k + 1) * width]) for k in range(2)]
    split = jnp.concatenate(split, 2)
    w_in, x, split, tokens, small_all = gather(
        [image_attend_in, patches, split, captions, small],
        [("full", "S"), ("za", None), ("za", None), ("zg", None), ("full", "C")],
        1,
    )
    w_in = w_in.reshape(width, 3 * width)
    x = x.reshape(length, width).astype(F32)
    main = jnp.concatenate(
        [
            image_attend_out,
            image_up_weight.reshape(part, width, fold).transpose(0, 2, 1).reshape(part, hidden_width),
            image_down_weight.reshape(part, hidden_width),
            text_attend_out,
            probe_out_weight,
        ],
        1,
    )
    main = lax.all_gather(main, ALL, axis=0, tiled=True)
    tp = jnp.concatenate(
        [split.reshape(n_z * part, -1), text_down_weight, probe_down_weight], 1
    )
    tp = lax.all_gather(tp, "dp", axis=0, tiled=True)
    w_out = main[:, :width]
    w_up = main[:, width : width + hidden_width]
    w_down = main[:, width + hidden_width : width + 2 * hidden_width]
    w_down = w_down.reshape(width, fold, width).transpose(1, 0, 2).reshape(hidden_width, width)
    outs = lax.dynamic_slice_in_dim(main[:, width + 2 * hidden_width :], at_z * quarter, quarter, 0)

    small_all = small_all.reshape(world, -1)
    cuts = [sum(sizes[:i]) for i in range(len(sizes) + 1)]
    pieces = [small_all[:, cuts[i] : cuts[i + 1]].astype(F32) for i in range(len(sizes))]
    ivec = pieces[0].reshape(world, -1, part).transpose(1, 0, 2).reshape(-1, width)
    tvec = pieces[1].reshape(world, -1, part).transpose(1, 0, 2).reshape(-1, width)
    i_bias = pieces[2].reshape(width, fold).T.reshape(1, hidden_width)

    def own_units(p):
        p = p.reshape(n_dp, n_z, wide_part)
        return lax.dynamic_index_in_dim(p, at_z, 1, False).reshape(1, width)

    p_bias, t_bias = own_units(pieces[3]), own_units(pieces[4])

    normed = layer_norm(x, ivec[0], ivec[1]).astype(BF)
    proj = mm(normed, w_in).astype(BF)
    mixed, lse = attend_fwd(proj, length)
    hidden = x + mm(mixed, w_out)
    second = layer_norm(hidden, ivec[2], ivec[3]).astype(BF)
    value, slope = gelu_pair(mm(second, w_up) + i_bias)
    active, slope = value.astype(BF), slope.astype(BF)
    block_out = hidden + mm(active, w_down) + ivec[4]
    final = layer_norm(block_out, ivec[5], ivec[6]).astype(BF)

    labels = (2 * pairs - 1).astype(F32).reshape(n_dp, n_z, n_dp, n_z)
    labels = jnp.pad(labels, ((0, 0), (0, n_z), (0, 0), (n_z, 0))).reshape(2 * world, 2 * world)
    dy, d_branch, rows, sums, d_captions, loss_row, d_embeds = middle(
        final, block_out, tokens.reshape(-1, width), tp, outs, ivec, tvec, p_bias, t_bias, labels, temp_bias, 2, n_dp
    )
    loss, grad_temp = loss_row[0, 0], loss_row[0, 1:3]
    grad_captions = d_captions.reshape(captions.shape)
    rows = lax.all_gather(rows.astype(BF), ALL, axis=0, tiled=False)

    g_down = mm(active, d_branch, 0, 0)
    d_upper_f = mm(d_branch, w_down, 1, 1) * slope.astype(F32)
    d_upper = d_upper_f.astype(BF)
    g_bias = jnp.sum(d_upper_f, 0)
    g_up = mm(second, d_upper, 0, 0)
    d_hidden, dv2, dv3 = norm_back(hidden, ivec[2], mm(d_upper, w_up, 1, 1))
    d_hidden = dy + d_hidden
    d_attend = d_hidden.astype(BF)
    g_out = mm(mixed, d_attend, 0, 0)
    d_mixed = mm(d_attend, w_out, 1, 1).astype(BF)
    g_main = jnp.concatenate(
        [
            g_out.astype(BF),
            g_up.astype(BF),
            g_down.astype(BF).reshape(fold, width, width).transpose(1, 0, 2).reshape(width, hidden_width),
        ],
        1,
    )
    g_main = lax.psum_scatter(g_main, ALL, scatter_dimension=0, tiled=True).astype(F32)
    own_out = g_main[:, :width]
    own_up = g_main[:, width : width + hidden_width].reshape(part, fold, width)
    own_up = own_up.transpose(0, 2, 1).reshape(part, hidden_width)
    own_down = g_main[:, width + hidden_width :].reshape(wide_part, width)
    inner_rows = jnp.sum(
        (d_mixed.astype(F32) * mixed.astype(F32)).reshape(length, HEADS, head_width), -1
    ).T.reshape(HEADS // 2, 2, length)
    d_q, d_k, d_v = attend_bwd(proj, d_mixed, lse, inner_rows, length)
    d_normed = (
        mm(d_q, w_in[:, :width], 1, 1)
        + mm(d_k, w_in[:, width : 2 * width], 1, 1)
        + mm(d_v, w_in[:, 2 * width :], 1, 1)
    )
    d_x, dv0, dv1 = norm_back(x, ivec[0], d_normed)
    d_x = (d_hidden + d_x).astype(BF)
    sums = jnp.concatenate([jnp.stack([dv0, dv1, dv2, dv3]), sums[4:], g_bias.reshape(fold, width)], 0)
    sums = jnp.pad(sums, ((0, 128 - sums.shape[0]), (0, 0))).T
    g_in = jnp.concatenate(
        [mm(normed, d, 0, 0).astype(BF) for d in (d_q, d_k, d_v)]
        + [sums.astype(BF), jnp.zeros((width, 128), BF)],
        1,
    )
    own_in, moved = reduce_and_move(g_in, d_x, 3)
    grad_patches = moved.astype(F32)
    own_sums = own_in[:, 3 * width : 3 * width + 128].T
    own_in = own_in[:, : 3 * width]

    rows = rows.reshape(n_dp, n_z, ROWS, width)
    column = lax.dynamic_slice_in_dim(rows, me * part, part, 3)
    one = lambda r: column[:, :, r]
    units = lax.dynamic_slice(rows, (0, at_z, 8, at_dp * wide_part), (n_dp, 1, 8, wide_part))[:, 0]
    each = quarter // part
    pooled = lax.dynamic_slice(rows, (0, me // each, 16, quarter + part * (me % each)), (n_dp, 1, 4, part))[:, 0]
    t_mixed = lax.dynamic_slice(rows, (0, me // each, 20, quarter + part * (me % each)), (n_dp, 1, 4, part))[:, 0]

    def ein(spec, a, b):
        return jnp.einsum(spec, a, b, preferred_element_type=F32)

    def wide(g):
        return g.reshape(part, n_z, n_dp, wide_part).transpose(0, 2, 1, 3).reshape(part, hidden_width)

    d_embeds = d_embeds.reshape(n_dp, 2, n_z, width).astype(BF)
    cut = lambda r, k: rows[:, :, r : r + 4, k * quarter : (k + 1) * quarter]
    heads = lambda v: v.reshape(v.shape[:-1] + (HEADS // n_z, head_width))
    per_head = lambda r: column[:, :, r : r + HEADS].reshape(n_dp, n_z, HEADS // n_z, n_z, part)
    own_p_up = wide(ein("icm,izcl->mzl", one(24), rows[:, :, 0:4]))
    own_t_up = wide(ein("icm,izcl->mzl", one(27), rows[:, :, 4:8]))
    own_p_down = ein("icm,icl->ml", units[:, 0:4], d_embeds[:, 0])
    own_t_down = ein("icm,icl->ml", units[:, 4:8], rows[:, :, 29])
    own_p_out = ein("icm,icl->ml", pooled, rows[:, :, 25])
    own_t_out = ein("icm,icl->ml", t_mixed, rows[:, :, 28])
    own_t_head = ein("icm,icl->ml", one(30), d_embeds[:, 1])
    own_t_q = ein("icm,izcl->mzl", one(26), cut(16, 2)).reshape(part, width)
    own_t_k = ein("izhcm,izche->mzhe", per_head(56), heads(cut(16, 3))).reshape(part, width)
    own_t_v = ein("izhcm,izche->mzhe", per_head(44), heads(cut(20, 0))).reshape(part, width)
    own_t_in = jnp.concatenate([own_t_q, own_t_k, own_t_v], 1)
    d_pooled = cut(16, 0).transpose(0, 2, 1, 3).reshape(n_dp, n_z, HEADS, head_width)
    own_p_v = ein("ichm,iche->mhe", column[:, :, 32:44], d_pooled).reshape(part, width)
    p_used = jnp.sum(column[:, :, 68:80].astype(F32), (0, 1))
    probe_query = cut(20, 3)[0, :, 0].reshape(HEADS, head_width).astype(F32)
    own_p_k = (p_used.T[:, :, None] * probe_query[None]).reshape(part, width)
    own_p_pair = jnp.concatenate([own_p_k, own_p_v], 1)
    d_query = jnp.sum(cut(20, 2)[:, :, 0].astype(F32), 0).reshape(width)
    mine = lambda v, n: lax.dynamic_slice_in_dim(v, me * n, n, -1)
    own_p_query = mine(ivec[7], part)[:, None] * d_query[None, :]
    dv7 = jnp.sum(probe_query_weight.astype(F32) * d_query[None, :], 1)
    bias_of = lambda r: jnp.sum(
        lax.dynamic_slice(rows, (0, at_z, r, at_dp * wide_part), (n_dp, 1, 4, wide_part)).astype(F32), (0, 1, 2)
    )
    own_ivec = jnp.concatenate([own_sums[0:7], dv7[None], own_sums[8:11]], 0)
    own_tvec = own_sums[11:18]
    own_bias = own_sums[24 : 24 + fold].T.reshape(wide_part)
    return (
        loss, grad_patches, grad_captions,
        own_in, own_out, own_up, own_bias, own_down, own_ivec,
        own_p_query, own_p_pair, own_p_out, own_p_up, bias_of(0), own_p_down,
        own_t_in, own_t_out, own_t_up, bias_of(4), own_t_down, own_tvec, own_t_head,
        grad_temp,
    )


def solution(mesh):
    tokens, matrix, vector, table = P("dp", "seq", None), P(ALL, None), P(ALL), P(None, ALL)
    weights = (
        (matrix, matrix, matrix, vector, matrix, table, matrix, matrix, matrix, matrix, vector, matrix)
        + (matrix, matrix, matrix, vector, matrix, table, matrix)
    )
    return jax.shard_map(
        fast_program if mesh.shape["dp"] == 8 and mesh.shape["seq"] == 4 else device_program,
        mesh=mesh,
        in_specs=(tokens, tokens, P()) + weights + (P(),),
        out_specs=(P(), tokens, tokens) + weights + (P(),),
        check_vma=False,
    )
```

time: 3450 us -> 564 us (0.16)
  waiting for transfers between devices: 2550 us -> 0.11 us
  Pallas kernels: 0 us -> 325 us
  blocking collectives: 268 us -> 0 us
  matrix products: 370 us -> 113 us
  local copies, waits for them, and re-layouts: 144 us -> 74.9 us
  other arithmetic: 87.8 us -> 30.9 us
    reduce_scatter x16 -> x1, waiting for transfers between devices: 1920 us -> 0.01 us  [fast_program(): lax.psum_scatter(g_main, ALL, scatter_dimension=0, tiled=True).astype(F32)]
    all_gather x15 -> x3, waiting for transfers between devices: 605 us -> 0.04 us  [the longest x1 0.02 us: fast_program(): main = lax.all_gather(main, ALL, axis=0, tiled=True)]
    pallas_call x0 -> x5, Pallas kernels: none -> 325 us  [the longest x1 146 us: gather(): pl.pallas_call(partial(gather_kernel, kinds), out_shape=shapes, in_specs=...]
    dot_general x104 -> x27, matrix products: 370 us -> 113 us  [the longest x16 107 us: mm(): lax.dot_general(a, b, (((ca,), (cb,)), ((), ())), preferred_element_type=...]
    all_gather x8 -> x0, blocking collectives: 213 us -> none  [the longest x1 71.3 us: per_device(): lax.all_gather(image_vectors, ('dp', 'seq'), axis=1, tiled=True)]
    unnamed x1 -> x0, blocking collectives: 37.5 us -> none
  transfers between devices with their start and end apart: 32 -> 4, of which waited for: 26 -> 0; matrix products, arithmetic and copies ran while one was open for 14% -> 34% of each run, Pallas kernels for 0% -> 47%
where the time goes in v1:
time: 564 us; the launch traced here: 560 us
  Pallas kernels  325 us (58%)
  matrix products  113 us (20%)
  local copies, waits for them, and re-layouts  74.9 us (13%)
  other arithmetic  30.9 us (5%)
  between operations  15.6 us (3%)
    pallas_call x1, Pallas kernels, gather(): pl.pallas_call(partial(gather_kernel, kinds), out_shape=shapes, in_specs=...  146 us
    dot_general x16, matrix products, mm(): lax.dot_general(a, b, (((ca,), (cb,)), ((), ())), preferred_element_type=...  107 us
    pallas_call x1, Pallas kernels, middle(): pl.pallas_call(middle_kernel, in_specs=[v] * 10 + [pl.BlockSpec(memory_sp...  60.8 us
    pallas_call x1, Pallas kernels, reduce_and_move(): pl.pallas_call(reduce_kernel, in_specs=[hbm, hbm], out_specs=[pl.BlockSpe...  60.7 us
    pallas_call x1, Pallas kernels, attend_bwd(): pl.pallas_call(attend_bwd_kernel, grid=(rows // length, pairs), in_specs=...  36.8 us
    unnamed x137, local copies, waits for them, and re-layouts  22.6 us
    pallas_call x1, Pallas kernels, attend_fwd(): pl.pallas_call(attend_fwd_kernel, grid=(rows // length, pairs), in_specs=...  21.1 us
  transfers between devices with their start and end apart: 4, of which 0 were waited for; matrix products, arithmetic and copies ran while one was open for 34% of the time, Pallas kernels for 47%

profile of v1, /device:TPU:0, one launch (start us, length us, event | category | flops | bytes accessed | tf_op | source)
XLA Modules:
  0.0 559.7 jit_solution(9749594719391896129)
XLA Ops:
  15.8 145.5 %shard_map.398 = (bf16[2,2,2,4,24,2304]{5,4,3,2,1,0:T(8,128)(2,1)}, bf16[4,256,768]{2,1,0:T(8,128)(2,1)}, bf16[4,24,3328]{2,1,0:T(8,128)(2,1)}, bf16[4,4,16,768]...) custom-call(bf16[24,2304]{1,0:T(8,128)(2,1)} %refs_0_.1, bf16[4,256,768]{2,1,0:T(8,128)(2,1)} %refs_1_.1, ...), custom_call_target="tpu_custom_call" | custom-call | tf_op jit(solution)/shard_map/pallas_call | solution.py:573
  161.4 2.2 pad_maximum_fusion.1
  170.1 5.4 convolution_convert_fusion.q_ref.k_ref.v_ref
  175.5 21.1 %shard_map.399 = (bf16[1024,768]{1,0:T(8,128)(2,1)S(1)}, f32[6,2,1024]{2,1,0:T(2,128)S(1)}) custom-call(bf16[1024,2304]{1,0:T(8,128)(2,1)} %convolution_convert_fusion.q_ref.k_ref.v_ref, bf16[1024,2304]{1,0:T(8,128)(2,1)} %convolution_convert_fusion.q_ref.k_ref.v_ref, bf16[1024,2304]{1,0:T(8,128)(2,1)} %convolution_convert_fusion.q_ref.k_ref.v_ref), custom_call_target="tpu_custom_call" | custom-call | flops 6442450944 | bytes 6291456 | tf_op jit(solution)/shard_map/pallas_call | solution.py:89
  199.0 2.7 copy.299
  201.8 2.8 copy-done.11
  207.3 8.3 %fusion.10 = f32[1024,3072]{1,0:T(8,128)} fusion(bf16[768,8448]{1,0:T(8,128)(2,1)S(1)} %copy-done.11, f32[1024,768]{1,0:T(8,128)S(1)} %get-tuple-element.192, f32[768]{0:T(1024)S(1)} %add.189, f32[768]{0:T(1024)S(1)} %mul.259, f32[1024]{0:T(1024)S(1)} %add_rsqrt_fusion.1, f32[1024]{0:T(1024)S(1)} %broadcast_multiply_fusion.7), kind=kOutput, calls=%fused_computation.19 | convolution fusion | flops 4835770368 | bytes 20463616 | tf_op jit(solution)/shard_map/dot_general | solution.py:18
  215.6 11.1 %fusion.76 = (f32[1024]{0:T(1024)S(1)}, f32[1024,768]{1,0:T(8,128)S(1)}) fusion(f32[768]{0:T(1024)S(1)} %add.199, f32[1024,768]{1,0:T(8,128)S(1)} %get-tuple-element.192, bf16[3072,768]{1,0:T(8,128)(2,1)S(1)} %bitcast.265, f32[1024,3072]{1,0:T(8,128)} %fusion.10, f32[3072]{0:T(1024)S(1)} %reshape.429), kind=kOutput, calls=%fused_computation.199 | convolution fusion | flops 4865653760 | bytes 23612416 | tf_op jit(solution)/shard_map/dot_general | solution.py:18
  227.4 2.2 slice-done.1
  231.4 60.8 %shard_map.400 = (f32[1024,768]{1,0:T(8,128)}, bf16[1024,768]{1,0:T(8,128)(2,1)S(1)}, f32[80,768]{1,0:T(8,128)S(1)}, f32[24,768]{1,0:T(8,128)S(1)}, f32[64,768]{...) custom-call(bf16[1024,768]{1,0:T(8,128)(2,1)} %add_convert_fusion.final_ref, f32[1024,768]{1,0:T(8,128)} %copy-done.6, ...), custom_call_target="tpu_custom_call" | custom-call | tf_op jit(solution)/shard_map/pallas_call | solution.py:930
  294.1 19.3 %fusion.6 = (bf16[3072]{0:T(1024)(128)(2,1)S(1)}, bf16[1024,3072]{1,0:T(8,128)(2,1)}, f32[1024,3072]{1,0:T(8,128)}) fusion(f32[1024,3072]{1,0:T(8,128)} %fusion.10, f32[3072]{0:T(1024)S(1)} %reshape.429, bf16[1024,768]{1,0:T(8,128)(2,1)} %copy-done.3, bf16[3072,768]{1,0:T(8,128)(2,1)} %bitcast.262), kind=kOutput, calls=%fused_computation.11 | convolution fusion | flops 4901041152 | bytes 37767168 | tf_op jit(solution)/shard_map/dot_general | solution.py:18
  313.4 10.9 %convolution_convert_fusion.1 = bf16[3072,768]{1,0:T(8,128)(2,1)S(1)} fusion(bf16[1024,768]{1,0:T(8,128)(2,1)S(1)} %copy-done.4, f32[1024,3072]{1,0:T(8,128)} %fusion.10, f32[3072]{0:T(1024)S(1)} %reshape.429), kind=kOutput, calls=%fused_computation.14 | convolution fusion | flops 4865654784 | bytes 18886656 | tf_op jit(solution)/shard_map/dot_general | solution.py:18
  324.3 3.6 copy.161
  327.9 3.2 copy.237
  331.2 15.6 %multiply_reduce_fusion = (bf16[768]{0:T(1024)(128)(2,1)S(1)}, f32[1024]{0:T(1024)S(1)}, f32[1024]{0:T(1024)S(1)}, bf16[768]{0:T(1024)(128)(2,1)S(1)}, f32[1024,768]{1,0:T(8,128)}) fusion(f32[1024,768]{1,0:T(8,128)S(1)} %copy-done.13, f32[1024]{0:T(1024)S(1)} %add_rsqrt_fusion.1, f32[1024]{0:T(1024)S(1)} %broadcast_multiply_fusion.7, f32[768]{0:T(1024)S(1)} %mul.259, ...), kind=kOutput, calls=%fused_computation.44 | convolution fusion | flops 4848349184 | bytes 29906944 | tf_op jit(solution)/shard_map/dot_general | solution.py:18
  346.8 3.5 multiply_add_fusion.1
  351.9 2.5 convolution_convert_fusion.4
  356.1 11.1 %convolution_convert_fusion.2 = bf16[768,3072]{1,0:T(8,128)(2,1)S(1)} fusion(f32[1024,3072]{1,0:T(8,128)} %get-tuple-element.195, bf16[1024,3072]{1,0:T(8,128)(2,1)} %get-tuple-element.141, f32[1024,768]{1,0:T(8,128)} %copy-done.12, f32[768]{0:T(1024)S(1)} %add.189, f32[768]{0:T(1024)S(1)} %mul.259, f32[1024]{0:T(1024)S(1)} %add_rsqrt_fusion.1, ...), kind=kOutput, calls=%fused_computation.15 | convolution fusion | flops 4847566848 | bytes 26753024 | tf_op jit(solution)/shard_map/dot_general | solution.py:18
  367.2 7.3 %pad_maximum_fusion = bf16[768,6912]{1,0:T(8,128)(2,1)} fusion(bf16[768,3072]{1,0:T(8,128)(2,1)} %bitcast.259, bf16[768,3072]{1,0:T(8,128)(2,1)S(1)} %convolution_convert_fusion.2, bf16[768,768]{1,0:T(8,128)(2,1)S(1)} %copy.162), kind=kLoop, calls=%fused_computation.10 | loop fusion | flops 31850496 | bytes 21233664 | tf_op jit(solution)/shard_map/concatenate | solution.py:1053
  378.9 5.9 %convert_multiply_fusion.1 = (f32[1024,768]{1,0:T(8,128)}, bf16[1024,768]{1,0:T(8,128)(2,1)}) fusion(bf16[1024,768]{1,0:T(8,128)(2,1)S(1)} %get-tuple-element.45, bf16[768,8448]{1,0:T(8,128)(2,1)} %all-gather.5.cloned.1.call-done, f32[1024,768]{1,0:T(8,128)} %copy-done.7), kind=kOutput, calls=%fused_computation.46 | convolution fusion | flops 1211891712 | bytes 10616832 | tf_op jit(solution)/shard_map/dot_general | solution.py:18
  384.8 2.5 copy.159
  388.4 36.8 %shard_map.401 = (bf16[1024,768]{1,0:T(8,128)(2,1)}, bf16[1024,768]{1,0:T(8,128)(2,1)}, bf16[1024,768]{1,0:T(8,128)(2,1)}) custom-call(bf16[1024,2304]{1,0:T(8,128)(2,1)} %convolution_convert_fusion.q_ref.k_ref.v_ref, bf16[1024,2304]{1,0:T(8,128)(2,1)} %convolution_convert_fusion.q_ref.k_ref.v_ref, ...), custom_call_target="tpu_custom_call" | custom-call | flops 16106127360 | bytes 12582912 | tf_op jit(solution)/shard_map/pallas_call | solution.py:133
  425.2 2.9 fusion.37
  430.1 3.6 fusion.26
  434.0 3.7 fusion.30
  437.8 2.5 fusion.33
  440.3 2.5 fusion.32
  442.8 2.5 fusion.31
  446.7 6.2 %copy.160 = bf16[768,2560]{1,0:T(8,128)(2,1)} copy(bf16[768,2560]{0,1:T(8,128)(2,1)} %broadcast_dynamic-update-slice_fusion) | data formatting | bytes 7864320 | tf_op jit(solution)/shard_map/concatenate | solution.py:1079
  452.9 2.1 copy-done
  455.0 60.7 %shard_map.402 = (f32[24,2560]{1,0:T(8,128)S(1)}, bf16[4,256,768]{2,1,0:T(8,128)(2,1)S(1)}) custom-call(bf16[2,2,2,4,24,2560]{5,4,3,2,1,0:T(8,128)(2,1)S(1)} %bitcast.253, bf16[4,256,768]{2,1,0:T(8,128)(2,1)S(1)} %bitcast.254), custom_call_target="tpu_custom_call" | custom-call | tf_op jit(solution)/shard_map/pallas_call | solution.py:651
  518.0 1.9 convert_element_type.163
  (316 shorter events, 70.8 us)
Async XLA Ops:
  7.2 4.0 copy-start.30
  7.2 4.0 copy-start.31
  7.2 4.9 copy-start.41
  7.2 4.9 copy-start.40
  7.2 5.0 copy-start.32
  7.2 5.2 copy-start.18
  7.3 5.3 copy-start.24
  7.3 5.6 copy-start.23
  7.3 6.0 %copy-start.20 = (bf16[24,3072]{1,0:T(8,128)(2,1)S(1)}, bf16[24,3072]{1,0:T(8,128)(2,1)}, u32[]{:S(2)}) copy-start(bf16[24,3072]{1,0:T(8,128)(2,1)} %param.35) | copy-start | bytes 442372
  7.3 189.4 %all-gather.5.cloned.1.call-start = ((), (), s32[]{:S(2)}) async-start(), calls=%async_computation.1 | async-start | bytes 13381632 | tf_op jit(solution)/shard_map/all_gather | solution.py:1000
  8.5 5.2 copy-start.21
  12.0 219.3 %all-gather.7.cloned.1.call-start = ((), (), s32[]{:S(2)}) async-start(), calls=%async_computation.2 | async-start | bytes 8404992 | tf_op jit(solution)/shard_map/all_gather | solution.py:1004
  13.0 148.4 %copy-start.16 = (bf16[96,768]{1,0:T(8,128)(2,1)S(1)}, bf16[96,768]{1,0:T(8,128)(2,1)}, u32[]{:S(2)}) copy-start(bf16[96,768]{1,0:T(8,128)(2,1)} %param.37) | copy-start | bytes 442372
  13.0 148.4 %copy-start.17 = (bf16[96,768]{1,0:T(8,128)(2,1)S(1)}, bf16[96,768]{1,0:T(8,128)(2,1)}, u32[]{:S(2)}) copy-start(bf16[96,768]{1,0:T(8,128)(2,1)} %param.42) | copy-start | bytes 442372
  14.8 149.0 %copy-start.37 = (s32[32,32]{1,0:T(8,128)S(1)}, s32[32,32]{1,0:T(8,128)}, u32[]{:S(2)}) copy-start(s32[32,32]{1,0:T(8,128)} %param.25) | copy-start | bytes 12292
  161.4 6.0 %copy-start.8 = (bf16[4,256,768]{2,1,0:T(8,128)(2,1)S(1)}, bf16[4,256,768]{2,1,0:T(8,128)(2,1)}, u32[]{:S(2)}) copy-start(bf16[4,256,768]{2,1,0:T(8,128)(2,1)} %get-tuple-element.42) | copy-start | bytes 4718596
  163.6 357.0 %all-gather.9.cloned.1.call-start = ((), (), s32[]{:S(2)}) async-start(), calls=%async_computation.4 | async-start | bytes 4055040 | tf_op jit(solution)/shard_map/all_gather | solution.py:1041
  196.7 7.9 %copy-start.11 = (bf16[768,8448]{1,0:T(8,128)(2,1)S(1)}, bf16[768,8448]{1,0:T(8,128)(2,1)}, u32[]{:S(2)}) copy-start(bf16[768,8448]{1,0:T(8,128)(2,1)} %all-gather.5.cloned.1.call-done) | copy-start | bytes 38928388
  206.7 8.9 %copy-start.12 = (f32[1024,768]{1,0:T(8,128)}, f32[1024,768]{1,0:T(8,128)S(1)}, u32[]{:S(2)}) copy-start(f32[1024,768]{1,0:T(8,128)S(1)} %get-tuple-element.192) | copy-start | bytes 9437188
  206.8 8.8 %slice-start.2 = ((s8[4718592]{0:T(1024)(128)(4,1)}), s8[4194304]{0:T(1024)(128)(4,1)S(1)}, s32[]{:S(2)}) async-start(s8[4718592]{0:T(1024)(128)(4,1)} %bitcast.263), calls=%async_computation.7 | async-start | bytes 8388608
  207.3 8.3 %slice-start.3 = ((s8[4718592]{0:T(1024)(128)(4,1)}), s8[524288]{0:T(1024)(128)(4,1)S(1)}, s32[]{:S(2)}) async-start(s8[4718592]{0:T(1024)(128)(4,1)} %bitcast.263), calls=%async_computation.8 | async-start | bytes 1048576
  227.3 4.0 copy-start.1
  227.3 4.0 copy-start.2
  294.0 253.0 %reduce-scatter.2.cloned.1.call-start = ((), (), s32[]{:S(2)}) async-start(), calls=%async_computation.3 | async-start | bytes 10948608 | tf_op jit(solution)/shard_map/reduce_scatter | solution.py:1061
  294.1 19.3 %copy-start.4 = (bf16[1024,768]{1,0:T(8,128)(2,1)S(1)}, bf16[1024,768]{1,0:T(8,128)(2,1)}, u32[]{:S(2)}) copy-start(bf16[1024,768]{1,0:T(8,128)(2,1)} %copy-done.3) | copy-start | bytes 4718596
  388.4 36.8 %copy-start.47 = (bf16[2,2,2,4,24,2304]{5,4,3,2,1,0:T(8,128)(2,1)S(1)}, bf16[2,2,2,4,24,2304]{5,4,3,2,1,0:T(8,128)(2,1)}, u32[]{:S(2)}) copy-start(bf16[2,2,2,4,24,2304]{5,4,3,2,1,0:T(8,128)(2,1)} %get-tuple-element.44) | copy-start | bytes 10616836
  430.1 3.6 copy-start.38
  430.1 3.7 copy-start.39
  430.1 3.9 copy-start.27
  434.0 3.7 copy-start.52
  515.7 6.8 %copy-start.19 = (bf16[24,768]{1,0:T(8,128)(2,1)S(1)}, bf16[24,768]{1,0:T(8,128)(2,1)}, u32[]{:S(2)}) copy-start(bf16[24,768]{1,0:T(8,128)(2,1)} %param.32) | copy-start | bytes 110596
  515.7 6.7 %copy-start.42 = (f32[24]{0:T(128)S(1)}, f32[24]{0:T(128)}, u32[]{:S(2)}) copy-start(f32[24]{0:T(128)} %dynamic_slice.34) | copy-start | bytes 292
  (29 other events, 64.3 us)
Sparse Core Ops, SparseCore 0:
  12.1 138.7 all-gather.4
  163.7 47.1 all-gather.6
  294.2 61.1 all-gather.8
  374.6 156.3 reduce-scatter.1

commit v2 on v1

--- a/solution.py
+++ b/solution.py
@@ -484,100 +484,141 @@
         pl.semaphore_signal(barrier, inc=1, device_id=p, device_id_type=MESH)
     pl.semaphore_wait(barrier, len(peers))
 
-def gather_kernel(kinds, *refs):
+def gather_kernel(kinds, order, *refs):
     n = len(kinds)
-    srcs, outs = refs[:n], refs[n:2 * n]
-    send, recv, local = refs[2 * n:]
+    srcs, outs = refs[:n], refs[n : 2 * n]
+    send, recv, local = refs[2 * n :]
     me = Place()
     y, x, c, z = me.y, me.x, me.c, me.z
     greet([me.at_z(1), me.at_z(2), me.at_z(3), me.at_x, me.at_y, me.at_c])
-    started = []
-    pending = {}
+    ends = []
+
+    def copy_of(a, slot, src, dst, dev):
+        return pltpu.make_async_remote_copy(
+            src, dst, send.at[a, slot], recv.at[a, slot], device_id=dev, device_id_type=MESH
+        )
 
     def push(a, slot, src, dst, dev, arriving):
-        copy = pltpu.make_async_remote_copy(src, dst, send.at[a, slot], recv.at[a, slot], device_id=dev, device_id_type=MESH)
+        copy = copy_of(a, slot, src, dst, dev)
         copy.start()
-        started.append(copy)
-        return pltpu.make_async_remote_copy(arriving, arriving, send.at[a, slot], recv.at[a, slot], device_id=dev, device_id_type=MESH)
+        ends.append(copy.wait_send)
+        return copy_of(a, slot, src, arriving, dev).wait_recv
+
+    def along(a, step, up):
+        home = outs[a].at[y, x, c]
+        if up:
+            slab, go, to = z - step, (z - step >= 0) & (z < 3), me.at_z(1)
+        else:
+            slab, go, to = z + step, (z + step < 4) & (z > 0), me.at_z(3)
+        slab = jnp.clip(slab, 0, 3)
+        src = srcs[a] if step == 0 else home.at[slab]
+        copy = copy_of(a, step + (0 if up else 3), src, home.at[slab], to)
+        pl.when(go)(lambda: copy.start())
+        ends.append(lambda: pl.when(go)(lambda: copy.wait_send()))
+
+    def arrived(a, step, up):
+        home = outs[a].at[y, x, c]
+        if up:
+            slab, come = z - 1 - step, z - 1 - step >= 0
+        else:
+            slab, come = z + 1 + step, z + 1 + step < 4
+        slab = jnp.clip(slab, 0, 3)
+        copy = copy_of(a, step + (0 if up else 3), home.at[slab], home.at[slab], me.at_z(1))
+        pl.when(come)(lambda: copy.wait_recv())
+
+    waits = {}
+
+    def half(r, which, order_):
+        if order_ != "S":
+            return r
+        n_ = r.shape[-1] // 2
+        return r.at[..., 0:n_] if which == "C" else r.at[..., n_ : 2 * n_]
 
     def stage(a, s):
-        kind, order = kinds[a]
+        kind, turn = kinds[a]
         src, out = srcs[a], outs[a]
-        for w in pending.pop((a, s - 1), []):
-            w()
-        waits = []
-        if s == 0:
-            if kind in ("full", "zg"):
-                own = src
-            elif kind in ("cols", "za"):
-                own = src.at[z]
-            else:
-                own = src
-            home = out.at[y, x, c, z] if kind in ("full", "cols") else out.at[z] if kind in ("zg", "za") else out.at[y, x, c]
-            cp = pltpu.make_async_copy(own, home, local.at[a])
-            cp.start()
-            waits.append(cp.wait)
-            if kind != "plane":
-                for k in (1, 2, 3):
-                    to, fro = (z + k) % 4, (z + 4 - k) % 4
-                    s_ref = src.at[to] if kind in ("cols", "za") else src
-                    if kind in ("full", "cols"):
-                        dst, arr = out.at[y, x, c, z], out.at[y, x, c, fro]
-                    else:
-                        dst, arr = out.at[z], out.at[fro]
-                    waits.append(push(a, k - 1, s_ref, dst, me.at_z(k), arr).wait_recv)
-        elif kind in ("zg", "za"):
+        if kind in ("za", "zg"):
+            own = src.at[z] if kind == "za" else src
+            keep = pltpu.make_async_copy(own, out.at[z], local.at[a])
+            keep.start()
+            ends.append(keep.wait)
+            for k in (1, 2, 3):
+                to, fro = (z + k) % 4, (z + 4 - k) % 4
+                s_ref = src.at[to] if kind == "za" else src
+                ends.append(push(a, k - 1, s_ref, out.at[z], me.at_z(k), out.at[fro]))
             return
-        elif s == 1:
-            if order in ("C", "S"):
-                cut = (lambda r: r) if order == "C" else (lambda r: r.at[..., 0:r.shape[-1] // 2])
-                waits.append(push(a, 3, cut(out.at[y, x, c]), cut(out.at[y, x, c]), me.at_x, cut(out.at[y, 1 - x, c])).wait_recv)
-            if order in ("D", "S"):
-                cut = (lambda r: r) if order == "D" else (lambda r: r.at[..., r.shape[-1] // 2:])
-                waits.append(push(a, 4, cut(out.at[y, x, c]), cut(out.at[y, x, c]), me.at_y, cut(out.at[1 - y, x, c])).wait_recv)
-        elif s == 2:
-            if order in ("C", "S"):
-                cut = (lambda r: r) if order == "C" else (lambda r: r.at[..., 0:r.shape[-1] // 2])
-                waits.append(push(a, 5, cut(out.at[y, :, c]), cut(out.at[y, :, c]), me.at_y, cut(out.at[1 - y, :, c])).wait_recv)
-            if order in ("D", "S"):
-                cut = (lambda r: r) if order == "D" else (lambda r: r.at[..., r.shape[-1] // 2:])
-                waits.append(push(a, 6, cut(out.at[:, x, c]), cut(out.at[:, x, c]), me.at_x, cut(out.at[:, 1 - x, c])).wait_recv)
+        turns = "CD" if turn == "S" else turn
+        if kind != "full" and s == 0:
+            own = src.at[z] if kind == "cols" else src
+            keep = pltpu.make_async_copy(own, out.at[y, x, c, z] if kind == "cols" else out.at[y, x, c], local.at[a])
+            keep.start()
+            waits[a] = [keep.wait]
+            for k in (1, 2, 3) if kind == "cols" else ():
+                to, fro = (z + k) % 4, (z + 4 - k) % 4
+                waits[a].append(push(a, k - 1, src.at[to], out.at[y, x, c, z], me.at_z(k), out.at[y, x, c, fro]))
+        elif s == 0:
+            keep = pltpu.make_async_copy(src, out.at[y, x, c, z], local.at[a])
+            keep.start()
+            waits[a] = [keep.wait]
+            along(a, 0, True)
+            along(a, 0, False)
+        elif s in (1, 2):
+            for up in (True, False):
+                arrived(a, s - 1, up)
+                along(a, s, up)
         elif s == 3:
-            waits.append(push(a, 7, out.at[:, :, c], out.at[:, :, c], me.at_c, out.at[:, :, 1 - c]).wait_recv)
-        pending[(a, s)] = waits
-
-    for t in range(n + 4):
-        for a in range(max(0, t - 4), min(n, t + 1)):
-            stage(a, t - a)
-    for key in list(pending):
-        for w in pending.pop(key):
-            w()
-    for copy in started:
-        copy.wait_send()
-
-def gather(ops, kinds, cid):
+            for up in (True, False) if kind == "full" else ():
+                arrived(a, 2, up)
+            for w in waits.pop(a):
+                w()
+            waits[a] = []
+            for t in turns:
+                cut = lambda r: half(r, t, turn)
+                to, fro = (me.at_x, (y, 1 - x)) if t == "C" else (me.at_y, (1 - y, x))
+                mine = cut(out.at[y, x, c])
+                waits[a].append(push(a, 6 + (t == "D"), mine, mine, to, cut(out.at[fro[0], fro[1], c])))
+        elif s == 4:
+            for w in waits.pop(a):
+                w()
+            waits[a] = []
+            for t in turns:
+                cut = lambda r: half(r, t, turn)
+                if t == "C":
+                    mine, come, to = cut(out.at[y, :, c]), cut(out.at[1 - y, :, c]), me.at_y
+                else:
+                    mine, come, to = cut(out.at[:, x, c]), cut(out.at[:, 1 - x, c]), me.at_x
+                waits[a].append(push(a, 8 + (t == "D"), mine, mine, to, come))
+        elif s == 5:
+            for w in waits.pop(a):
+                w()
+            mine = out.at[:, :, c]
+            ends.append(push(a, 10, mine, mine, me.at_c, out.at[:, :, 1 - c]))
+
+    for a, s in order:
+        stage(a, s)
+    for e in ends:
+        e()
+
+
+def gather(ops, kinds, order, cid):
     shapes = []
     for o, (kind, _) in zip(ops, kinds):
-        if kind == "full":
-            s = (2, 2, 2, 4) + o.shape
-        elif kind == "cols":
-            s = (2, 2, 2, 4) + o.shape[1:]
-        elif kind == "plane":
-            s = (2, 2, 2) + o.shape
-        elif kind == "zg":
-            s = (4,) + o.shape
-        else:
-            s = o.shape
+        s = {"full": (2, 2, 2, 4) + o.shape, "zg": (4,) + o.shape, "za": o.shape, "cols": (2, 2, 2) + o.shape, "plane": (2, 2, 2) + o.shape}[kind]
         shapes.append(jax.ShapeDtypeStruct(s, o.dtype))
     n = len(ops)
     return pl.pallas_call(
-        partial(gather_kernel, kinds),
+        partial(gather_kernel, kinds, order),
         out_shape=shapes,
         in_specs=[pl.BlockSpec(memory_space=pl.ANY)] * n,
         out_specs=[pl.BlockSpec(memory_space=pl.ANY)] * n,
-        scratch_shapes=[pltpu.SemaphoreType.DMA((n, 8)), pltpu.SemaphoreType.DMA((n, 8)), pltpu.SemaphoreType.DMA((n,))],
+        scratch_shapes=[
+            pltpu.SemaphoreType.DMA((n, 11)),
+            pltpu.SemaphoreType.DMA((n, 11)),
+            pltpu.SemaphoreType.DMA((n,)),
+        ],
         compiler_params=pltpu.CompilerParams(collective_id=cid, has_side_effects=True),
     )(*ops)
+
 
 def reduce_kernel(g_ref, dx_ref, own_ref, moved_ref, from_c, acc_c, from_1, acc_1, from_2, acc_2, from_z, send, recv, local):
     me = Place()
@@ -663,7 +704,7 @@
 
 ROWS = 80
 
-def middle_kernel(final_ref, block_ref, tokens_ref, tp_ref, outs_ref, ivec_ref, tvec_ref, pbias_ref, tbias_ref,
+def middle_kernel(final_ref, block_ref, tokens_ref, tp_ref, downs_ref, outs_ref, ivec_ref, tvec_ref, pbias_ref, tbias_ref,
                   label_ref, temp_ref,
                   dy_ref, branch_ref, rows_ref, sums_ref, dcap_ref, loss_ref, dz_ref,
                   tn_ref, dn_ref, send_a, recv_a, send_l, recv_l, send_t, recv_t, send_sem, recv_sem):
@@ -707,9 +748,8 @@
     small = lambda n: tp_ref[:, col[n]:col[n] + 256]
     p_up = lambda: tp_ref[:, 0:width]
     t_up = lambda: tp_ref[:, width:2 * width]
-    base = 2 * width + 256 * 7
-    t_down = lambda: tp_ref[:, base:base + width]
-    p_down = lambda: tp_ref[:, base + width:base + 2 * width]
+    t_down = lambda: downs_ref[:, 0:width]
+    p_down = lambda: downs_ref[:, width:2 * width]
     t_out_w = lambda: outs_ref[0:part, 0:width]
     p_out_w = lambda: outs_ref[0:part, width:2 * width]
     lane = lax.broadcasted_iota(jnp.int32, (1, 256), 1)
@@ -923,13 +963,13 @@
     for copy in started:
         copy.wait_send()
 
-def middle(final, block_out, tokens, tp, outs, ivec, tvec, pbias, tbias, label, temp, cid, n_dp):
+def middle(final, block_out, tokens, tp, downs, outs, ivec, tvec, pbias, tbias, label, temp, cid, n_dp):
     length, width = final.shape
     v = pl.BlockSpec(memory_space=pltpu.VMEM)
     f = lambda *s: jax.ShapeDtypeStruct(s, F32)
     return pl.pallas_call(
         middle_kernel,
-        in_specs=[v] * 10 + [pl.BlockSpec(memory_space=pltpu.SMEM)],
+        in_specs=[v] * 11 + [pl.BlockSpec(memory_space=pltpu.SMEM)],
         out_specs=[v] * 7,
         out_shape=[f(length, width), jax.ShapeDtypeStruct((length, width), BF), f(ROWS, width), f(24, width), f(64, width), f(8, 128), f(8 * n_dp, width)],
         scratch_shapes=[
@@ -940,7 +980,238 @@
             pltpu.SemaphoreType.DMA((9, 8)), pltpu.SemaphoreType.DMA((9, 8)),
         ],
         compiler_params=pltpu.CompilerParams(collective_id=cid, has_side_effects=True, vmem_limit_bytes=50 << 20),
-    )(final, block_out, tokens, tp, outs, ivec, tvec, pbias, tbias, label, temp)
+    )(final, block_out, tokens, tp, downs, outs, ivec, tvec, pbias, tbias, label, temp)
+
+
+def mlp_fwd_kernel(x_ref, mixed_ref, wo_ref, wu_ref, wd_ref, bias_ref, vec_ref,
+                   hidden_ref, second_ref, active_ref, slope_ref, block_ref, final_ref, total):
+    k = pl.program_id(0)
+    vec = vec_ref[...]
+
+    @pl.when(k == 0)
+    def _():
+        hidden = x_ref[...].astype(F32) + mm(mixed_ref[...], wo_ref[...])
+        hidden_ref[...] = hidden
+        second_ref[...] = layer_norm(hidden, vec[2:3], vec[3:4]).astype(BF)
+        total[...] = hidden + vec[4:5]
+
+    value, slope = gelu_pair(mm(second_ref[...], wu_ref[...]) + bias_ref[0])
+    active = value.astype(BF)
+    active_ref[...] = active
+    slope_ref[...] = slope.astype(BF)
+    total[...] += mm(active, wd_ref[...])
+
+    @pl.when(k == pl.num_programs(0) - 1)
+    def _():
+        block_ref[...] = total[...]
+        final_ref[...] = layer_norm(total[...], vec[5:6], vec[6:7]).astype(BF)
+
+
+def mlp_fwd(x, mixed, main, bias, vec, fold):
+    rows, width = mixed.shape
+    whole = pl.BlockSpec((rows, width), lambda k: (0, 0))
+    tile = pl.BlockSpec((rows, width), lambda k: (0, k))
+    at = lambda f: pl.BlockSpec((width, width), lambda k: (0, f(k)))
+    s = lambda n, t: jax.ShapeDtypeStruct((rows, n * width), t)
+    return pl.pallas_call(
+        mlp_fwd_kernel,
+        grid=(fold,),
+        in_specs=[whole, whole, at(lambda k: 0), at(lambda k: 1 + k), at(lambda k: 1 + fold + k),
+                  pl.BlockSpec((1, 1, width), lambda k: (k, 0, 0)), pl.BlockSpec(vec.shape, lambda k: (0, 0))],
+        out_specs=[whole, whole, tile, tile, whole, whole],
+        out_shape=[s(1, F32), s(1, BF), s(fold, BF), s(fold, BF), s(1, F32), s(1, BF)],
+        scratch_shapes=[pltpu.VMEM((rows, width), F32)],
+        compiler_params=pltpu.CompilerParams(vmem_limit_bytes=56 << 20),
+    )(x, mixed, main, main, main, bias.reshape(fold, 1, width), vec)
+
+
+def mlp_bwd_kernel(dy_ref, branch_ref, active_ref, slope_ref, second_ref, hidden_ref, mixed_ref,
+                   wo_ref, wu_ref, wd_ref, vec_ref,
+                   g_ref, dhid_ref, dmix_ref, inner_ref, bias_ref, dvec_ref, total):
+    k = pl.program_id(0)
+    fold = pl.num_programs(0)
+    width = mixed_ref.shape[1]
+    branch = branch_ref[...]
+    columns = lambda n: pl.ds(pl.multiple_of(n * width, width), width)
+    g_ref[:, columns(1 + fold + k)] = mm(active_ref[...], branch, 0, 0).astype(BF)
+    d_upper_f = mm(branch, wd_ref[...], 1, 1) * slope_ref[...].astype(F32)
+    bias_ref[0] = jnp.sum(d_upper_f, 0, keepdims=True)
+    d_upper = d_upper_f.astype(BF)
+    g_ref[:, columns(1 + k)] = mm(second_ref[...], d_upper, 0, 0).astype(BF)
+    back = mm(d_upper, wu_ref[...], 1, 1)
+
+    @pl.when(k == 0)
+    def _():
+        total[...] = back
+
+    @pl.when(k > 0)
+    def _():
+        total[...] += back
+
+    @pl.when(k == fold - 1)
+    def _():
+        vec = vec_ref[...]
+        d_hidden, gain, shift = norm_back_rows(hidden_ref[...], vec[2:3], total[...])
+        dvec_ref[0:1] = gain
+        dvec_ref[1:2] = shift
+        d_hidden = dy_ref[...] + d_hidden
+        dhid_ref[...] = d_hidden
+        d_attend = d_hidden.astype(BF)
+        mixed = mixed_ref[...]
+        g_ref[:, 0:width] = mm(mixed, d_attend, 0, 0).astype(BF)
+        d_mixed = mm(d_attend, wo_ref[...], 1, 1).astype(BF)
+        dmix_ref[...] = d_mixed
+        head = lax.broadcasted_iota(jnp.int32, (16, width), 0)
+        lane = lax.broadcasted_iota(jnp.int32, (16, width), 1)
+        own = (lane // (width // HEADS) == head).astype(BF)
+        high, low = split_two(d_mixed.astype(F32) * mixed.astype(F32))
+        sums = mm(own, high, 1, 1) + mm(own, low, 1, 1)
+        for h in range(HEADS // 2):
+            inner_ref[h] = sums[2 * h : 2 * h + 2]
+
+
+def mlp_bwd(dy, branch, active, slope, second, hidden, mixed, main, vec, fold):
+    rows, width = mixed.shape
+    whole = pl.BlockSpec((rows, width), lambda k: (0, 0))
+    tile = pl.BlockSpec((rows, width), lambda k: (0, k))
+    at = lambda f: pl.BlockSpec((width, width), lambda k: (0, f(k)))
+    f = lambda *s: jax.ShapeDtypeStruct(s, F32)
+    return pl.pallas_call(
+        mlp_bwd_kernel,
+        grid=(fold,),
+        in_specs=[whole, whole, tile, tile, whole, whole, whole,
+                  at(lambda k: 0), at(lambda k: 1 + k), at(lambda k: 1 + fold + k), pl.BlockSpec(vec.shape, lambda k: (0, 0))],
+        out_specs=[pl.BlockSpec((width, (1 + 2 * fold) * width), lambda k: (0, 0)), whole, whole,
+                   pl.BlockSpec((HEADS // 2, 2, rows), lambda k: (0, 0, 0)),
+                   pl.BlockSpec((1, 1, width), lambda k: (k, 0, 0)), pl.BlockSpec((8, width), lambda k: (0, 0))],
+        out_shape=[jax.ShapeDtypeStruct((width, (1 + 2 * fold) * width), BF), f(rows, width),
+                   jax.ShapeDtypeStruct((rows, width), BF), f(HEADS // 2, 2, rows), f(fold, 1, width), f(8, width)],
+        scratch_shapes=[pltpu.VMEM((rows, width), F32)],
+        compiler_params=pltpu.CompilerParams(vmem_limit_bytes=60 << 20),
+    )(dy, branch, active, slope, second, hidden, mixed, main, main, main, vec)
+
+
+def project_bwd_kernel(dq_ref, dk_ref, dv_ref, normed_ref, w_ref, x_ref, dhid_ref, sums_ref, vec_ref, g_ref, dx_ref):
+    width = dq_ref.shape[1]
+    normed = normed_ref[...]
+    back = None
+    for n, ref in enumerate((dq_ref, dk_ref, dv_ref)):
+        d = ref[...]
+        g_ref[:, n * width : (n + 1) * width] = mm(normed, d, 0, 0).astype(BF)
+        part = mm(d, w_ref[:, n * width : (n + 1) * width], 1, 1)
+        back = part if back is None else back + part
+    d_x, gain, shift = norm_back_rows(x_ref[...].astype(F32), vec_ref[0:1], back)
+    dx_ref[...] = (dhid_ref[...] + d_x).astype(BF)
+    sums = jnp.concatenate([gain, shift, sums_ref[2:, :]], 0)
+    sums = jnp.concatenate([sums, jnp.zeros((128 - sums.shape[0], width), F32)], 0)
+    g_ref[:, 3 * width : 3 * width + 128] = jnp.transpose(sums).astype(BF)
+    g_ref[:, 3 * width + 128 : 3 * width + 256] = jnp.zeros((width, 128), BF)
+
+
+def project_bwd(dq, dk, dv, normed, w_in, x, d_hidden, sums, vec):
+    rows, width = dq.shape
+    v = pl.BlockSpec(memory_space=pltpu.VMEM)
+    return pl.pallas_call(
+        project_bwd_kernel,
+        in_specs=[v] * 9,
+        out_specs=[v] * 2,
+        out_shape=[jax.ShapeDtypeStruct((width, 3 * width + 256), BF), jax.ShapeDtypeStruct((rows, width), BF)],
+        compiler_params=pltpu.CompilerParams(vmem_limit_bytes=56 << 20),
+    )(dq, dk, dv, normed, w_in, x, d_hidden, sums, vec)
+
+
+def outer_kernel(rows_ref, dimage_ref, dtext_ref,
+                 pup_ref, tup_ref, pdown_ref, tdown_ref, pout_ref, tout_ref, thead_ref,
+                 tq_ref, tk_ref, tv_ref, pv_ref, pk_ref, bias_ref):
+    at_dp, z = lax.axis_index("dp"), lax.axis_index("seq")
+    n_dp, n_z = 8, 4
+    me = at_dp * n_z + z
+    width = rows_ref.shape[2]
+    part, quarter = width // 32, width // n_z
+    wide_part = 4 * part
+    n = n_dp * n_z
+    each = quarter // part
+
+    def iota(shape, d):
+        return lax.broadcasted_iota(jnp.int32, shape, d)
+
+    def selector(count, first):
+        return (iota((count, width), 1) == iota((count, width), 0) + first).astype(BF)
+
+    def group(r):
+        return jnp.concatenate([rows_ref[r + c] for c in range(4)], 0)
+
+    cols = jnp.concatenate(
+        [mm(selector(part, part * me), rows_ref[r], 1, 1) for r in range(24, 80)], 1
+    ).astype(BF)
+    get = lambda r, count=1: cols[:, n * (r - 24) : n * (r - 24 + count)]
+    a, b = iota((4 * n, n), 0), iota((4 * n, n), 1)
+    same = ((a % n) // n_z == b // n_z) & (a // n == b % n_z)
+    keep = lambda which: (same & (a % n_z == which)).astype(BF)
+    units = selector(wide_part, wide_part * at_dp)
+    heads = selector(part, quarter + part * (me % each))
+    to_mine, to_head = keep(z), keep(me // each)
+    chosen = lambda sel, r, perm: mm(mm(sel, group(r), 1, 1).astype(BF), perm).astype(BF)
+    pdown_ref[...] = mm(chosen(units, 8, to_mine), dimage_ref[...])
+    tdown_ref[...] = mm(chosen(units, 12, to_mine), rows_ref[29])
+    pout_ref[...] = mm(chosen(heads, 16, to_head), rows_ref[25])
+    tout_ref[...] = mm(chosen(heads, 20, to_head), rows_ref[28])
+    thead_ref[...] = mm(get(30), dtext_ref[...])
+    ones = jnp.ones((n, 128), BF)
+    bias_ref[0] = mm(chosen(units, 0, to_mine), ones)
+    bias_ref[1] = mm(chosen(units, 4, to_mine), ones)
+    a, b = iota((n, 4 * n), 0), iota((n, 4 * n), 1)
+    spread = ((b % n) // n_z == a // n_z) & (b // n == a % n_z)
+    spread = spread.astype(BF)
+    lane_z = iota((1, 4 * n), 1) % n_z
+    masks = [(lane_z == q).astype(BF) for q in range(n_z)]
+
+    def blocks(values):
+        return jnp.concatenate([v * m for v, m in zip(values, masks)], 0)
+
+    by_image = lambda r: mm(get(r), spread).astype(BF)
+    g16, g20 = group(16), group(20)
+
+    def put(ref, value, first):
+        for q in range(n_z):
+            ref[q] = value[q * part : (q + 1) * part, first : first + ref.shape[2]]
+
+    put(pup_ref, mm(blocks([by_image(24)] * 4), group(0)), 0)
+    put(tup_ref, mm(blocks([by_image(27)] * 4), group(4)), 0)
+    put(tq_ref, mm(blocks([by_image(26)] * 4), g16), 2 * quarter)
+    lane = iota((1, width), 1)
+    count = HEADS // n_z
+    hw = quarter // count
+
+    def by_head(values_of, rhs, first):
+        total = None
+        for h in range(count):
+            own = ((lane >= first + hw * h) & (lane < first + hw * h + hw)).astype(F32)
+            one = mm(blocks(values_of(h)), rhs) * own
+            total = one if total is None else total + one
+        return total
+
+    put(tk_ref, by_head(lambda h: [get(56 + 4 * h, 4)] * 4, g16, 3 * quarter), 3 * quarter)
+    put(tv_ref, by_head(lambda h: [get(44 + 4 * h, 4)] * 4, g20, 0), 0)
+    put(pv_ref, by_head(lambda h: [by_image(32 + count * q + h) for q in range(n_z)], g16, 0), 0)
+    a, b = iota((HEADS * n, 128), 0), iota((HEADS * n, 128), 1)
+    pk_ref[...] = mm(get(68, HEADS), (a // n == b).astype(BF))
+
+
+def outer_grads(rows, d_image, d_text):
+    width = rows.shape[2]
+    part, quarter = width // 32, width // 4
+    v = pl.BlockSpec(memory_space=pltpu.VMEM)
+    f = lambda *s: jax.ShapeDtypeStruct(s, F32)
+    return pl.pallas_call(
+        outer_kernel,
+        in_specs=[v] * 3,
+        out_specs=[v] * 13,
+        out_shape=[f(4, part, width), f(4, part, width), f(4 * part, width), f(4 * part, width), f(part, width), f(part, width),
+                   f(part, width), f(4, part, quarter), f(4, part, quarter), f(4, part, quarter), f(4, part, quarter),
+                   f(part, 128), f(2, 4 * part, 128)],
+        compiler_params=pltpu.CompilerParams(vmem_limit_bytes=48 << 20),
+    )(rows, d_image, d_text)
 
 
 def fast_program(
@@ -980,13 +1251,17 @@
     split += [by_heads(text_head_weight), by_heads(probe_query_weight)]
     split += [by_heads(probe_pair_weight[:, k * width : (k + 1) * width]) for k in range(2)]
     split = jnp.concatenate(split, 2)
-    w_in, x, split, tokens, small_all = gather(
-        [image_attend_in, patches, split, captions, small],
-        [("full", "S"), ("za", None), ("za", None), ("zg", None), ("full", "C")],
+    downs = jnp.concatenate([text_down_weight, probe_down_weight], 1)
+    w_in, tp, downs, small_all, x, tokens = gather(
+        [image_attend_in, split, downs, small, patches, captions],
+        [("full", "S"), ("cols", "S"), ("plane", "S"), ("full", "C"), ("za", None), ("zg", None)],
+        [(0, 0), (2, 0), (2, 3), (3, 0), (0, 1), (3, 1), (1, 0), (0, 2), (3, 2), (0, 3), (4, 0), (5, 0), (3, 3)]
+        + [(1, 3), (0, 4), (2, 4), (3, 4), (1, 4), (0, 5), (2, 5), (3, 5), (1, 5)],
         1,
     )
+    tp, downs = tp.reshape(width, -1), downs.reshape(width, -1)
     w_in = w_in.reshape(width, 3 * width)
-    x = x.reshape(length, width).astype(F32)
+    x = x.reshape(length, width)
     main = jnp.concatenate(
         [
             image_attend_out,
@@ -998,14 +1273,6 @@
         1,
     )
     main = lax.all_gather(main, ALL, axis=0, tiled=True)
-    tp = jnp.concatenate(
-        [split.reshape(n_z * part, -1), text_down_weight, probe_down_weight], 1
-    )
-    tp = lax.all_gather(tp, "dp", axis=0, tiled=True)
-    w_out = main[:, :width]
-    w_up = main[:, width : width + hidden_width]
-    w_down = main[:, width + hidden_width : width + 2 * hidden_width]
-    w_down = w_down.reshape(width, fold, width).transpose(1, 0, 2).reshape(hidden_width, width)
     outs = lax.dynamic_slice_in_dim(main[:, width + 2 * hidden_width :], at_z * quarter, quarter, 0)
 
     small_all = small_all.reshape(world, -1)
@@ -1021,121 +1288,62 @@
 
     p_bias, t_bias = own_units(pieces[3]), own_units(pieces[4])
 
-    normed = layer_norm(x, ivec[0], ivec[1]).astype(BF)
+    normed = layer_norm(x.astype(F32), ivec[0], ivec[1]).astype(BF)
     proj = mm(normed, w_in).astype(BF)
     mixed, lse = attend_fwd(proj, length)
-    hidden = x + mm(mixed, w_out)
-    second = layer_norm(hidden, ivec[2], ivec[3]).astype(BF)
-    value, slope = gelu_pair(mm(second, w_up) + i_bias)
-    active, slope = value.astype(BF), slope.astype(BF)
-    block_out = hidden + mm(active, w_down) + ivec[4]
-    final = layer_norm(block_out, ivec[5], ivec[6]).astype(BF)
+    hidden, second, active, slope, block_out, final = mlp_fwd(x, mixed, main, i_bias, ivec, fold)
 
     labels = (2 * pairs - 1).astype(F32).reshape(n_dp, n_z, n_dp, n_z)
     labels = jnp.pad(labels, ((0, 0), (0, n_z), (0, 0), (n_z, 0))).reshape(2 * world, 2 * world)
     dy, d_branch, rows, sums, d_captions, loss_row, d_embeds = middle(
-        final, block_out, tokens.reshape(-1, width), tp, outs, ivec, tvec, p_bias, t_bias, labels, temp_bias, 2, n_dp
+        final, block_out, tokens.reshape(-1, width), tp, downs, outs, ivec, tvec, p_bias, t_bias, labels, temp_bias, 2, n_dp
     )
     loss, grad_temp = loss_row[0, 0], loss_row[0, 1:3]
     grad_captions = d_captions.reshape(captions.shape)
-    rows = lax.all_gather(rows.astype(BF), ALL, axis=0, tiled=False)
-
-    g_down = mm(active, d_branch, 0, 0)
-    d_upper_f = mm(d_branch, w_down, 1, 1) * slope.astype(F32)
-    d_upper = d_upper_f.astype(BF)
-    g_bias = jnp.sum(d_upper_f, 0)
-    g_up = mm(second, d_upper, 0, 0)
-    d_hidden, dv2, dv3 = norm_back(hidden, ivec[2], mm(d_upper, w_up, 1, 1))
-    d_hidden = dy + d_hidden
-    d_attend = d_hidden.astype(BF)
-    g_out = mm(mixed, d_attend, 0, 0)
-    d_mixed = mm(d_attend, w_out, 1, 1).astype(BF)
-    g_main = jnp.concatenate(
-        [
-            g_out.astype(BF),
-            g_up.astype(BF),
-            g_down.astype(BF).reshape(fold, width, width).transpose(1, 0, 2).reshape(width, hidden_width),
-        ],
-        1,
+    rows = lax.all_gather(rows.astype(BF), ALL, axis=1, tiled=False)
+
+    g_main, d_hidden, d_mixed, inner, g_bias, dvec = mlp_bwd(
+        dy, d_branch, active, slope, second, hidden, mixed, main, ivec, fold
     )
     g_main = lax.psum_scatter(g_main, ALL, scatter_dimension=0, tiled=True).astype(F32)
     own_out = g_main[:, :width]
     own_up = g_main[:, width : width + hidden_width].reshape(part, fold, width)
     own_up = own_up.transpose(0, 2, 1).reshape(part, hidden_width)
     own_down = g_main[:, width + hidden_width :].reshape(wide_part, width)
-    inner_rows = jnp.sum(
-        (d_mixed.astype(F32) * mixed.astype(F32)).reshape(length, HEADS, head_width), -1
-    ).T.reshape(HEADS // 2, 2, length)
-    d_q, d_k, d_v = attend_bwd(proj, d_mixed, lse, inner_rows, length)
-    d_normed = (
-        mm(d_q, w_in[:, :width], 1, 1)
-        + mm(d_k, w_in[:, width : 2 * width], 1, 1)
-        + mm(d_v, w_in[:, 2 * width :], 1, 1)
-    )
-    d_x, dv0, dv1 = norm_back(x, ivec[0], d_normed)
-    d_x = (d_hidden + d_x).astype(BF)
-    sums = jnp.concatenate([jnp.stack([dv0, dv1, dv2, dv3]), sums[4:], g_bias.reshape(fold, width)], 0)
-    sums = jnp.pad(sums, ((0, 128 - sums.shape[0]), (0, 0))).T
-    g_in = jnp.concatenate(
-        [mm(normed, d, 0, 0).astype(BF) for d in (d_q, d_k, d_v)]
-        + [sums.astype(BF), jnp.zeros((width, 128), BF)],
-        1,
-    )
+    d_q, d_k, d_v = attend_bwd(proj, d_mixed, lse, inner, length)
+    sums = jnp.concatenate([dvec[0:2], dvec[0:2], sums[4:], g_bias.reshape(fold, width)], 0)
+    g_in, d_x = project_bwd(d_q, d_k, d_v, normed, w_in, x, d_hidden, sums, ivec)
     own_in, moved = reduce_and_move(g_in, d_x, 3)
     grad_patches = moved.astype(F32)
     own_sums = own_in[:, 3 * width : 3 * width + 128].T
     own_in = own_in[:, : 3 * width]
 
-    rows = rows.reshape(n_dp, n_z, ROWS, width)
-    column = lax.dynamic_slice_in_dim(rows, me * part, part, 3)
-    one = lambda r: column[:, :, r]
-    units = lax.dynamic_slice(rows, (0, at_z, 8, at_dp * wide_part), (n_dp, 1, 8, wide_part))[:, 0]
-    each = quarter // part
-    pooled = lax.dynamic_slice(rows, (0, me // each, 16, quarter + part * (me % each)), (n_dp, 1, 4, part))[:, 0]
-    t_mixed = lax.dynamic_slice(rows, (0, me // each, 20, quarter + part * (me % each)), (n_dp, 1, 4, part))[:, 0]
-
-    def ein(spec, a, b):
-        return jnp.einsum(spec, a, b, preferred_element_type=F32)
+    d_embeds = d_embeds.reshape(n_dp, 2, n_z, width).astype(BF)
+    pup, tup, own_p_down, own_t_down, own_p_out, own_t_out, own_t_head, tq, tk, tv, pv, pk, biases = outer_grads(
+        rows, d_embeds[:, 0].reshape(world, width), d_embeds[:, 1].reshape(world, width)
+    )
 
     def wide(g):
-        return g.reshape(part, n_z, n_dp, wide_part).transpose(0, 2, 1, 3).reshape(part, hidden_width)
-
-    d_embeds = d_embeds.reshape(n_dp, 2, n_z, width).astype(BF)
-    cut = lambda r, k: rows[:, :, r : r + 4, k * quarter : (k + 1) * quarter]
-    heads = lambda v: v.reshape(v.shape[:-1] + (HEADS // n_z, head_width))
-    per_head = lambda r: column[:, :, r : r + HEADS].reshape(n_dp, n_z, HEADS // n_z, n_z, part)
-    own_p_up = wide(ein("icm,izcl->mzl", one(24), rows[:, :, 0:4]))
-    own_t_up = wide(ein("icm,izcl->mzl", one(27), rows[:, :, 4:8]))
-    own_p_down = ein("icm,icl->ml", units[:, 0:4], d_embeds[:, 0])
-    own_t_down = ein("icm,icl->ml", units[:, 4:8], rows[:, :, 29])
-    own_p_out = ein("icm,icl->ml", pooled, rows[:, :, 25])
-    own_t_out = ein("icm,icl->ml", t_mixed, rows[:, :, 28])
-    own_t_head = ein("icm,icl->ml", one(30), d_embeds[:, 1])
-    own_t_q = ein("icm,izcl->mzl", one(26), cut(16, 2)).reshape(part, width)
-    own_t_k = ein("izhcm,izche->mzhe", per_head(56), heads(cut(16, 3))).reshape(part, width)
-    own_t_v = ein("izhcm,izche->mzhe", per_head(44), heads(cut(20, 0))).reshape(part, width)
-    own_t_in = jnp.concatenate([own_t_q, own_t_k, own_t_v], 1)
-    d_pooled = cut(16, 0).transpose(0, 2, 1, 3).reshape(n_dp, n_z, HEADS, head_width)
-    own_p_v = ein("ichm,iche->mhe", column[:, :, 32:44], d_pooled).reshape(part, width)
-    p_used = jnp.sum(column[:, :, 68:80].astype(F32), (0, 1))
-    probe_query = cut(20, 3)[0, :, 0].reshape(HEADS, head_width).astype(F32)
-    own_p_k = (p_used.T[:, :, None] * probe_query[None]).reshape(part, width)
-    own_p_pair = jnp.concatenate([own_p_k, own_p_v], 1)
-    d_query = jnp.sum(cut(20, 2)[:, :, 0].astype(F32), 0).reshape(width)
+        return g.reshape(n_z, part, n_dp, wide_part).transpose(1, 2, 0, 3).reshape(part, hidden_width)
+
+    own_p_up, own_t_up = wide(pup), wide(tup)
+    own_t_in = jnp.stack([tq, tk, tv]).transpose(2, 0, 1, 3).reshape(part, 3 * width)
+    row20 = rows[20].reshape(n_dp, n_z, n_z, quarter).astype(F32)
+    probe_query = row20[0, :, 3].reshape(HEADS, head_width)
+    own_p_k = (pk[:, :HEADS, None] * probe_query[None]).reshape(part, width)
+    own_p_pair = jnp.concatenate([own_p_k, pv.transpose(1, 0, 2).reshape(part, width)], 1)
+    d_query = jnp.sum(row20[:, :, 2], 0).reshape(width)
     mine = lambda v, n: lax.dynamic_slice_in_dim(v, me * n, n, -1)
     own_p_query = mine(ivec[7], part)[:, None] * d_query[None, :]
     dv7 = jnp.sum(probe_query_weight.astype(F32) * d_query[None, :], 1)
-    bias_of = lambda r: jnp.sum(
-        lax.dynamic_slice(rows, (0, at_z, r, at_dp * wide_part), (n_dp, 1, 4, wide_part)).astype(F32), (0, 1, 2)
-    )
     own_ivec = jnp.concatenate([own_sums[0:7], dv7[None], own_sums[8:11]], 0)
     own_tvec = own_sums[11:18]
     own_bias = own_sums[24 : 24 + fold].T.reshape(wide_part)
     return (
         loss, grad_patches, grad_captions,
         own_in, own_out, own_up, own_bias, own_down, own_ivec,
-        own_p_query, own_p_pair, own_p_out, own_p_up, bias_of(0), own_p_down,
-        own_t_in, own_t_out, own_t_up, bias_of(4), own_t_down, own_tvec, own_t_head,
+        own_p_query, own_p_pair, own_p_out, own_p_up, biases[0, :, 0], own_p_down,
+        own_t_in, own_t_out, own_t_up, biases[1, :, 0], own_t_down, own_tvec, own_t_head,
         grad_temp,
     )
 

time: 564 us -> 532 us (0.943)
  matrix products: 113 us -> 5.55 us
  Pallas kernels: 325 us -> 417 us
  waiting for transfers between devices: 0.11 us -> 38.9 us
  local copies, waits for them, and re-layouts: 74.9 us -> 40.2 us
  other arithmetic: 30.9 us -> 10.5 us
    dot_general x16 -> x1, matrix products: 107 us -> 5.55 us  [mm(): lax.dot_general(a, b, (((ca,), (cb,)), ((), ())), preferred_element_type=...]
    pallas_call x2 -> x6, Pallas kernels: 206 us -> 284 us  [the longest x1 120 us: gather(): pl.pallas_call(partial(gather_kernel, kinds, order), out_shape=shapes, in...]
    reduce_scatter x1, waiting for transfers between devices: 0.01 us -> 38.8 us  [fast_program(): lax.psum_scatter(g_main, ALL, scatter_dimension=0, tiled=True).astype(F32)]
    pallas_call x1, Pallas kernels: 60.7 us -> 75.5 us  [reduce_and_move(): pl.pallas_call(reduce_kernel, in_specs=[hbm, hbm], out_specs=[pl.BlockSpe...]
    concatenate x4 -> x3, other arithmetic: 10.8 us -> 2.11 us  [the longest x1 0.78 us: fast_program(): downs = jnp.concatenate([text_down_weight, probe_down_weight], 1)]
    concatenate x3 -> x0, local copies, waits for them, and re-layouts: 7.08 us -> none  [the longest x2 6.88 us: fast_program(): jnp.concatenate([mm(normed, d, 0, 0).astype(BF) for d in (d_q, d_k, d_v)]...]
    slice x14 -> x5, local copies, waits for them, and re-layouts: 8.55 us -> 1.54 us  [the longest x1 0.74 us: fast_program(): dvec[0:2]]
    reshape x14 -> x6, local copies, waits for them, and re-layouts: 10 us -> 3.49 us  [the longest x4 2.52 us: wide(): g.reshape(n_z, part, n_dp, wide_part).transpose(1, 2, 0, 3)]
  transfers between devices with their start and end apart: 4 -> 3, of which waited for: 0 -> 1; matrix products, arithmetic and copies ran while one was open for 34% -> 7% of each run, Pallas kernels for 47% -> 60%
where the time goes in v2:
time: 532 us; the launch traced here: 527 us
  Pallas kernels  417 us (78%)
  local copies, waits for them, and re-layouts  40.2 us (8%)
  waiting for transfers between devices  38.9 us (7%)
  between operations  15 us (3%)
  other arithmetic  10.5 us (2%)
  matrix products  5.55 us (1%)
    pallas_call x1, Pallas kernels, gather(): pl.pallas_call(partial(gather_kernel, kinds, order), out_shape=shapes, in...  120 us
    pallas_call x1, Pallas kernels, reduce_and_move(): pl.pallas_call(reduce_kernel, in_specs=[hbm, hbm], out_specs=[pl.BlockSpe...  75.5 us
    pallas_call x1, Pallas kernels, middle(): pl.pallas_call(middle_kernel, in_specs=[v] * 11 + [pl.BlockSpec(memory_sp...  74.6 us
    pallas_call x1, Pallas kernels, mlp_bwd(): pl.pallas_call(mlp_bwd_kernel, grid=(fold,), in_specs=[whole, whole, tile...  39.8 us
    reduce_scatter x1, waiting for transfers between devices, fast_program(): lax.psum_scatter(g_main, ALL, scatter_dimension=0, tiled=True).astype(F32)  38.8 us
    pallas_call x1, Pallas kernels, attend_bwd(): pl.pallas_call(attend_bwd_kernel, grid=(rows // length, pairs), in_specs=...  36.3 us
    pallas_call x1, Pallas kernels, mlp_fwd(): pl.pallas_call(mlp_fwd_kernel, grid=(fold,), in_specs=[whole, whole, at(l...  28 us
    pallas_call x1, Pallas kernels, attend_fwd(): pl.pallas_call(attend_fwd_kernel, grid=(rows // length, pairs), in_specs=...  21.1 us
  transfers between devices with their start and end apart: 3, of which 1 were waited for; matrix products, arithmetic and copies ran while one was open for 7% of the time, Pallas kernels for 60%

profile of v2, /device:TPU:0, one launch (start us, length us, event | category | flops | bytes accessed | tf_op | source)
XLA Modules:
  0.0 527.1 jit_solution(8735415482879833040)
XLA Ops:
  7.3 0.9 constant_dynamic-update-slice_fusion.6
  8.2 1.3 copy.69
  10.1 1.0 reshape.294
  15.9 119.8 %shard_map.398 = (bf16[2,2,2,4,24,2304]{5,4,3,2,1,0:T(8,128)(2,1)}, bf16[2,2,2,4,24,3328]{5,4,3,2,1,0:T(8,128)(2,1)}, bf16[2,2,2,96,1536]{4,3,2,1,0:T(8,128)(2,1...) custom-call(bf16[24,2304]{1,0:T(8,128)(2,1)} %refs_0_.1, ...), custom_call_target="tpu_custom_call" | custom-call | tf_op jit(solution)/shard_map/pallas_call | solution.py:609
  135.7 1.1 copy.108
  142.2 5.5 %convolution_convert_fusion.q_ref.k_ref.v_ref = bf16[1024,2304]{1,0:T(8,128)(2,1)} fusion(bf16[1024,768]{1,0:T(8,128)(2,1)S(1)} %bitcast.125, bf16[768,2304]{1,0:T(8,128)(2,1)S(1)} %bitcast.122), kind=kOutput, calls=%fused_computation | convolution fusion | flops 3626237952 | bytes 9830400 | tf_op jit(solution)/shard_map/dot_general | solution.py:18
  147.7 21.1 %shard_map.399 = (bf16[1024,768]{1,0:T(8,128)(2,1)S(1)}, f32[6,2,1024]{2,1,0:T(2,128)S(1)}) custom-call(bf16[1024,2304]{1,0:T(8,128)(2,1)} %convolution_convert_fusion.q_ref.k_ref.v_ref, bf16[1024,2304]{1,0:T(8,128)(2,1)} %convolution_convert_fusion.q_ref.k_ref.v_ref, bf16[1024,2304]{1,0:T(8,128)(2,1)} %convolution_convert_fusion.q_ref.k_ref.v_ref), custom_call_target="tpu_custom_call" | custom-call | flops 6442450944 | bytes 6291456 | tf_op jit(solution)/shard_map/pallas_call | solution.py:89
  168.8 1.1 copy-done
  170.0 1.7 slice-done
  171.7 28.0 %shard_map.400 = (f32[1024,768]{1,0:T(8,128)}, bf16[1024,768]{1,0:T(8,128)(2,1)}, bf16[1024,3072]{1,0:T(8,128)(2,1)}, bf16[1024,3072]{1,0:T(8,128)(2,1)}, f32[10...) custom-call(bf16[1024,768]{1,0:T(8,128)(2,1)} %bitcast.116, bf16[1024,768]{1,0:T(8,128)(2,1)} %copy-done, ...), custom_call_target="tpu_custom_call" | custom-call | tf_op jit(solution)/shard_map/pallas_call | solution.py:1016
  199.8 74.6 %shard_map.401 = (f32[1024,768]{1,0:T(8,128)}, bf16[1024,768]{1,0:T(8,128)(2,1)S(1)}, f32[80,768]{1,0:T(8,128)S(1)}, f32[24,768]{1,0:T(8,128)S(1)}, f32[64,768]{...) custom-call(bf16[1024,768]{1,0:T(8,128)(2,1)} %get-tuple-element.74.final_ref, ...), custom_call_target="tpu_custom_call" | custom-call | tf_op jit(solution)/shard_map/pallas_call | solution.py:970
  274.4 1.1 copy-done.3
  276.3 39.8 %shard_map.402 = (bf16[768,6912]{1,0:T(8,128)(2,1)}, f32[1024,768]{1,0:T(8,128)}, bf16[1024,768]{1,0:T(8,128)(2,1)}, f32[6,2,1024]{2,1,0:T(2,128)}, f32[4,1,768]{2,1,0:T(1,128)}, /*index=5*/f32[8,768]{1,0:T(8,128)}) custom-call(f32[1024,768]{1,0:T(8,128)} %get-tuple-element.80.dy_ref, bf16[1024,768]{1,0:T(8,128)(2,1)} %copy-done.3, ...), custom_call_target="tpu_custom_call" | custom-call | tf_op jit(solution)/shard_map/pallas_call | solution.py:1079
  316.5 1.1 copy-done.9
  317.5 1.8 add_convert_fusion.normed_ref
  321.3 36.3 %shard_map.403 = (bf16[1024,768]{1,0:T(8,128)(2,1)}, bf16[1024,768]{1,0:T(8,128)(2,1)}, bf16[1024,768]{1,0:T(8,128)(2,1)}) custom-call(bf16[1024,2304]{1,0:T(8,128)(2,1)} %convolution_convert_fusion.q_ref.k_ref.v_ref, bf16[1024,2304]{1,0:T(8,128)(2,1)} %convolution_convert_fusion.q_ref.k_ref.v_ref, ...), custom_call_target="tpu_custom_call" | custom-call | flops 16106127360 | bytes 12582912 | tf_op jit(solution)/shard_map/pallas_call | solution.py:133
  357.6 17.4 %shard_map.404 = (bf16[768,2560]{1,0:T(8,128)(2,1)}, bf16[1024,768]{1,0:T(8,128)(2,1)}) custom-call(bf16[1024,768]{1,0:T(8,128)(2,1)} %get-tuple-element.89.dq_ref, bf16[1024,768]{1,0:T(8,128)(2,1)} %get-tuple-element.90.dk_ref, bf16[1024,768]{1,0:T(8,128)(2,1)} %get-tuple-element.91.dv_ref, bf16[1024,768]{1,0:T(8,128)(2,1)} %add_convert_fusion.normed_ref, ...), custom_call_target="tpu_custom_call" | custom-call | tf_op jit(solution)/shard_map/pallas_call | solution.py:1114
  374.9 2.3 copy-done.1
  377.2 1.5 copy-done.2
  378.7 75.5 %shard_map.405 = (f32[24,2560]{1,0:T(8,128)S(1)}, bf16[4,256,768]{2,1,0:T(8,128)(2,1)S(1)}) custom-call(bf16[2,2,2,4,24,2560]{5,4,3,2,1,0:T(8,128)(2,1)S(1)} %bitcast.107, bf16[4,256,768]{2,1,0:T(8,128)(2,1)S(1)} %bitcast.108), custom_call_target="tpu_custom_call" | custom-call | tf_op jit(solution)/shard_map/pallas_call | solution.py:692
  454.2 1.9 convert_element_type.69
  459.1 1.3 fusion.6
  460.6 0.8 broadcast_multiply_fusion.1
  462.3 3.1 copy.94
  465.4 4.4 shard_map.406
  470.7 1.1 reshape.321
  471.9 0.9 reshape.322
  473.2 1.1 reshape.324
  475.6 38.8 %reduce-scatter.2.cloned.1.call-done = bf16[24,6912]{1,0:T(8,128)(2,1)} async-done(((bf16[768,6912]{1,0:T(8,128)(2,1)}), bf16[24,6912]{1,0:T(8,128)(2,1)}) %reduce-scatter.2.cloned.1.call-update) | async-done | bytes 331792 | tf_op jit(solution)/shard_map/reduce_scatter | solution.py:1308
  514.4 1.0 fusion.11
  516.3 1.2 copy.83
  518.3 1.4 slice.153
  (186 shorter events, 22.3 us)
Async XLA Ops:
  7.2 4.0 copy-start.20
  7.2 4.0 copy-start.21
  7.2 4.9 copy-start.14
  7.2 5.3 %copy-start.15 = (bf16[24,3072]{1,0:T(8,128)(2,1)S(1)}, bf16[24,3072]{1,0:T(8,128)(2,1)}, u32[]{:S(2)}) copy-start(bf16[24,3072]{1,0:T(8,128)(2,1)} %param.40) | copy-start | bytes 442372
  7.2 5.7 %copy-start.18 = (bf16[24,2304]{1,0:T(8,128)(2,1)S(1)}, bf16[24,2304]{1,0:T(8,128)(2,1)}, u32[]{:S(2)}) copy-start(bf16[24,2304]{1,0:T(8,128)(2,1)} %param.38) | copy-start | bytes 331780
  7.2 162.7 %all-gather.4.cloned.1.call-start = ((), (), s32[]{:S(2)}) async-start(), calls=%async_computation.1 | async-start | bytes 13381632 | tf_op jit(solution)/shard_map/all_gather | solution.py:1275
  8.2 5.1 copy-start.22
  8.2 5.3 %copy-start.13 = (bf16[24,768]{1,0:T(8,128)(2,1)S(1)}, bf16[24,768]{1,0:T(8,128)(2,1)}, u32[]{:S(2)}) copy-start(bf16[24,768]{1,0:T(8,128)(2,1)} %param.32) | copy-start | bytes 110596
  9.5 4.1 copy-start.19
  9.5 4.4 copy-start.25
  9.5 4.5 copy-start.26
  9.5 4.6 copy-start.27
  9.5 4.6 copy-start.28
  9.5 4.5 copy-start.29
  11.1 3.8 copy-start.16
  11.1 3.8 copy-start.17
  12.0 447.0 %all-gather.6.cloned.1.call-start = ((), (), s32[]{:S(2)}) async-start(), calls=%async_computation.3 | async-start | bytes 4055040 | tf_op jit(solution)/shard_map/all_gather | solution.py:1303
  14.9 124.8 %copy-start.23 = (s32[32,32]{1,0:T(8,128)S(1)}, s32[32,32]{1,0:T(8,128)}, u32[]{:S(2)}) copy-start(s32[32,32]{1,0:T(8,128)} %param.25) | copy-start | bytes 12292
  135.7 4.3 copy-start.8
  140.1 2.1 copy-start.10
  168.8 1.1 copy-start
  170.0 29.8 %copy-start.7 = (f32[6,2,1024]{2,1,0:T(2,128)}, f32[6,2,1024]{2,1,0:T(2,128)S(1)}, u32[]{:S(2)}) copy-start(f32[6,2,1024]{2,1,0:T(2,128)S(1)} %get-tuple-element.87.lse_ref) | copy-start | bytes 147460
  170.0 1.7 slice-start
  171.7 28.1 %copy-start.4 = (f32[11,768]{1,0:T(8,128)S(1)}, f32[11,768]{1,0:T(8,128)}, u32[]{:S(2)}) copy-start(f32[11,768]{1,0:T(8,128)} %reshape.296.vec_ref.ivec_ref) | copy-start | bytes 101380
  171.7 28.1 %copy-start.5 = (bf16[4,4,16,768]{3,2,1,0:T(8,128)(2,1)S(1)}, bf16[4,4,16,768]{3,2,1,0:T(8,128)(2,1)}, u32[]{:S(2)}) copy-start(bf16[4,4,16,768]{3,2,1,0:T(8,128)(2,1)} %get-tuple-element.76) | copy-start | bytes 1179652
  171.7 28.1 %copy-start.6 = (f32[2]{0:T(128)S(1)}, f32[2]{0:T(128)}, u32[]{:S(2)}) copy-start(f32[2]{0:T(128)} %temp_ref.1) | copy-start | bytes 28
  274.4 1.1 copy-start.3
  276.2 238.2 %reduce-scatter.2.cloned.1.call-start = ((), (), s32[]{:S(2)}) async-start(), calls=%async_computation.2 | async-start | bytes 10948608 | tf_op jit(solution)/shard_map/reduce_scatter | solution.py:1308
  316.1 1.4 copy-start.9
  316.2 3.7 copy-start.24
  374.9 2.3 copy-start.1
  377.2 1.5 copy-start.2
  (2 other events, 1.7 us)
Sparse Core Ops, SparseCore 0:
  12.1 144.1 all-gather.3
  276.4 61.4 all-gather.5
  343.9 170.4 reduce-scatter.1

commit v3 on v2

--- a/solution.py
+++ b/solution.py
@@ -959,7 +959,7 @@
         own_row(dt_attend), own_row(dt_branch), own_row(t_final), pad1,
         used, t_used, tk_used, p_used,
     ]
-    rows_ref[...] = jnp.concatenate(pieces, 0)
+    rows_ref[...] = jnp.concatenate(pieces, 0).astype(BF)
     for copy in started:
         copy.wait_send()
 
@@ -971,7 +971,7 @@
         middle_kernel,
         in_specs=[v] * 11 + [pl.BlockSpec(memory_space=pltpu.SMEM)],
         out_specs=[v] * 7,
-        out_shape=[f(length, width), jax.ShapeDtypeStruct((length, width), BF), f(ROWS, width), f(24, width), f(64, width), f(8, 128), f(8 * n_dp, width)],
+        out_shape=[f(length, width), jax.ShapeDtypeStruct((length, width), BF), jax.ShapeDtypeStruct((ROWS, width), BF), f(24, width), f(64, width), f(8, 128), f(8 * n_dp, width)],
         scratch_shapes=[
             pltpu.VMEM((256, width), F32), pltpu.VMEM((256, width), BF),
             pltpu.VMEM((7, 4, 8, width), F32), pltpu.VMEM((7, 4, 8, width), F32),
@@ -981,6 +981,124 @@
         ],
         compiler_params=pltpu.CompilerParams(collective_id=cid, has_side_effects=True, vmem_limit_bytes=50 << 20),
     )(final, block_out, tokens, tp, downs, outs, ivec, tvec, pbias, tbias, label, temp)
+
+
+class Spread:
+    stages = 6
+
+    def __init__(self, me, src, out, send, recv, local):
+        self.me, self.src, self.out, self.send, self.recv, self.local = me, src, out, send, recv, local
+
+    def moves(self, s):
+        me, out = self.me, self.out
+        y, x, c, z = me.y, me.x, me.c, me.z
+        if s < 3:
+            home = out.at[y, x, c]
+            for up in (True, False):
+                step = -s if up else s
+                slab, come = z + step, z + step + (-1 if up else 1)
+                go = ((slab >= 0) & (z < 3)) if up else ((slab < 4) & (z > 0))
+                arrives = (come >= 0) & (come < 4)
+                slab, come = jnp.clip(slab, 0, 3), jnp.clip(come, 0, 3)
+                src = self.src if s == 0 else home.at[slab]
+                yield s + (0 if up else 3), src, home.at[slab], me.at_z(1 if up else 3), go, home.at[come], arrives
+        elif s == 5:
+            mine = out.at[:, :, c]
+            yield 10, mine, mine, me.at_c, None, out.at[:, :, 1 - c], None
+        else:
+            n = out.shape[-1] // 2
+            left, right = (lambda r: r.at[..., 0:n]), (lambda r: r.at[..., n : 2 * n])
+            if s == 3:
+                own = out.at[y, x, c]
+                yield 6, left(own), left(own), me.at_x, None, left(out.at[y, 1 - x, c]), None
+                yield 7, right(own), right(own), me.at_y, None, right(out.at[1 - y, x, c]), None
+            else:
+                own = out.at[y, :, c]
+                yield 8, left(own), left(own), me.at_y, None, left(out.at[1 - y, :, c]), None
+                own = out.at[:, x, c]
+                yield 9, right(own), right(own), me.at_x, None, right(out.at[:, 1 - x, c]), None
+
+    def each(self, s, act):
+        for slot, src, dst, dev, go, come, arrives in self.moves(s):
+            make = lambda a, b: pltpu.make_async_remote_copy(
+                a, b, self.send.at[slot], self.recv.at[slot], device_id=dev, device_id_type=MESH
+            )
+            if act == "arrived":
+                copy, when = make(src, come).wait_recv, arrives
+            else:
+                copy, when = getattr(make(src, dst), "start" if act == "start" else "wait_send"), go
+            if when is None:
+                copy()
+            else:
+                pl.when(when)(lambda: copy())
+
+    def keep(self):
+        me = self.me
+        return pltpu.make_async_copy(self.src, self.out.at[me.y, me.x, me.c, me.z], self.local)
+
+    def begin(self, s):
+        if s == 0:
+            self.keep().start()
+        else:
+            self.each(s - 1, "arrived")
+        if s == 3:
+            self.keep().wait()
+        self.each(s, "start")
+
+    def finish(self):
+        self.each(5, "arrived")
+        for s in range(6):
+            self.each(s, "sent")
+
+
+def attend_bwd_kernel_hosting(q_ref, k_ref, v_ref, do_ref, lse_ref, d_ref, rows_ref, dq_ref, dk_ref, dv_ref, all_ref, send, recv, local):
+    h_at = pl.program_id(0)
+    me = Place()
+    spread = Spread(me, rows_ref, all_ref, send, recv, local)
+
+    def first():
+        greet([me.at_z(1), me.at_z(2), me.at_z(3), me.at_x, me.at_y, me.at_c])
+        spread.begin(0)
+
+    pl.when(h_at == 0)(first)
+    for s in range(1, 6):
+        pl.when(h_at == s)(partial(spread.begin, s))
+    q = q_ref[...] * 0.125
+    k, v, do = k_ref[...], v_ref[...], do_ref[...]
+    lane = lax.broadcasted_iota(jnp.int32, k.shape, 1)
+    dqs, dks, dvs = [], [], []
+    for h in range(2):
+        keep = (lane < 64) if h == 0 else (lane >= 64)
+        s = mm(jnp.where(keep, k, jnp.zeros_like(k)), q, 1, 1)
+        p = jnp.exp(s - lse_ref[0, h : h + 1, :])
+        dp = mm(jnp.where(keep, v, jnp.zeros_like(v)), do, 1, 1)
+        ds = (p * (dp - d_ref[0, h : h + 1, :])).astype(BF)
+        dvs.append(mm(p.astype(BF), do))
+        dks.append(mm(ds, q))
+        dqs.append(mm(ds, k, 0, 0))
+    low = lane < 64
+    dq_ref[...] = (jnp.where(low, dqs[0], dqs[1]) * 0.125).astype(BF)
+    dk_ref[...] = jnp.where(low, dks[0], dks[1]).astype(BF)
+    dv_ref[...] = jnp.where(low, dvs[0], dvs[1]).astype(BF)
+    pl.when(h_at == 5)(spread.finish)
+
+
+def attend_bwd_and_spread(proj, d_out, lse, inner, rows, cid):
+    length, width = proj.shape[0], proj.shape[1] // 3
+    pairs = width // 128
+    block = lambda part: pl.BlockSpec((length, 128), lambda h: (0, part * pairs + h))
+    row = pl.BlockSpec((1, 2, length), lambda h: (h, 0, 0))
+    hbm = pl.BlockSpec(memory_space=pl.ANY)
+    result = jax.ShapeDtypeStruct((length, width), BF)
+    return pl.pallas_call(
+        attend_bwd_kernel_hosting,
+        grid=(pairs,),
+        in_specs=[block(0), block(1), block(2), block(0), row, row, hbm],
+        out_specs=[block(0)] * 3 + [hbm],
+        out_shape=[result] * 3 + [jax.ShapeDtypeStruct((2, 2, 2, 4) + rows.shape, rows.dtype)],
+        scratch_shapes=[pltpu.SemaphoreType.DMA((11,)), pltpu.SemaphoreType.DMA((11,)), pltpu.SemaphoreType.DMA],
+        compiler_params=pltpu.CompilerParams(collective_id=cid, has_side_effects=True, vmem_limit_bytes=56 << 20),
+    )(proj, proj, proj, d_out, lse, inner, rows)
 
 
 def mlp_fwd_kernel(x_ref, mixed_ref, wo_ref, wu_ref, wd_ref, bias_ref, vec_ref,
@@ -1300,7 +1418,6 @@
     )
     loss, grad_temp = loss_row[0, 0], loss_row[0, 1:3]
     grad_captions = d_captions.reshape(captions.shape)
-    rows = lax.all_gather(rows.astype(BF), ALL, axis=1, tiled=False)
 
     g_main, d_hidden, d_mixed, inner, g_bias, dvec = mlp_bwd(
         dy, d_branch, active, slope, second, hidden, mixed, main, ivec, fold
@@ -1310,7 +1427,8 @@
     own_up = g_main[:, width : width + hidden_width].reshape(part, fold, width)
     own_up = own_up.transpose(0, 2, 1).reshape(part, hidden_width)
     own_down = g_main[:, width + hidden_width :].reshape(wide_part, width)
-    d_q, d_k, d_v = attend_bwd(proj, d_mixed, lse, inner, length)
+    d_q, d_k, d_v, rows = attend_bwd_and_spread(proj, d_mixed, lse, inner, rows, 4)
+    rows = rows.reshape(world, ROWS, width).transpose(1, 0, 2)
     sums = jnp.concatenate([dvec[0:2], dvec[0:2], sums[4:], g_bias.reshape(fold, width)], 0)
     g_in, d_x = project_bwd(d_q, d_k, d_v, normed, w_in, x, d_hidden, sums, ivec)
     own_in, moved = reduce_and_move(g_in, d_x, 3)

time: 532 us -> 500 us (0.940)
  waiting for transfers between devices: 38.9 us -> 8.18 us
  Pallas kernels: 417 us -> 411 us
    reduce_scatter x1, waiting for transfers between devices: 38.8 us -> 8.14 us  [fast_program(): lax.psum_scatter(g_main, ALL, scatter_dimension=0, tiled=True).astype(F32)]
    pallas_call x1, Pallas kernels: 75.5 us -> 60.3 us  [reduce_and_move(): pl.pallas_call(reduce_kernel, in_specs=[hbm, hbm], out_specs=[pl.BlockSpe...]
    pallas_call x1, Pallas kernels: 36.3 us -> 46.3 us  [attend_bwd_and_spread(): pl.pallas_call(attend_bwd_kernel_hosting, grid=(pairs,), in_specs=[block(...]
    unnamed x85 -> x88, local copies, waits for them, and re-layouts: 18.6 us -> 18.1 us
  transfers between devices with their start and end apart: 3 -> 2, of which waited for: 1 -> 1; matrix products, arithmetic and copies ran while one was open for 7% -> 8% of each run, Pallas kernels for 60% -> 54%
where the time goes in v3:
time: 500 us; the launch traced here: 495 us
  Pallas kernels  411 us (82%)
  local copies, waits for them, and re-layouts  45 us (9%)
  between operations  15.3 us (3%)
  other arithmetic  9.37 us (2%)
  waiting for transfers between devices  8.18 us (2%)
  matrix products  5.91 us (1%)
    pallas_call x1, Pallas kernels, gather(): pl.pallas_call(partial(gather_kernel, kinds, order), out_shape=shapes, in...  120 us
    pallas_call x1, Pallas kernels, middle(): pl.pallas_call(middle_kernel, in_specs=[v] * 11 + [pl.BlockSpec(memory_sp...  74.6 us
    pallas_call x1, Pallas kernels, reduce_and_move(): pl.pallas_call(reduce_kernel, in_specs=[hbm, hbm], out_specs=[pl.BlockSpe...  60.3 us
    pallas_call x1, Pallas kernels, attend_bwd_and_spread(): pl.pallas_call(attend_bwd_kernel_hosting, grid=(pairs,), in_specs=[block(...  46.3 us
    pallas_call x1, Pallas kernels, mlp_bwd(): pl.pallas_call(mlp_bwd_kernel, grid=(fold,), in_specs=[whole, whole, tile...  39.7 us
    pallas_call x1, Pallas kernels, mlp_fwd(): pl.pallas_call(mlp_fwd_kernel, grid=(fold,), in_specs=[whole, whole, at(l...  28 us
    pallas_call x1, Pallas kernels, attend_fwd(): pl.pallas_call(attend_fwd_kernel, grid=(rows // length, pairs), in_specs=...  21.1 us
    unnamed x88, local copies, waits for them, and re-layouts  18.1 us
  transfers between devices with their start and end apart: 2, of which 1 were waited for; matrix products, arithmetic and copies ran while one was open for 8% of the time, Pallas kernels for 54%

profile of v3, /device:TPU:0, one launch (start us, length us, event | category | flops | bytes accessed | tf_op | source)
XLA Modules:
  0.0 495.0 jit_solution(2403131154875195552)
XLA Ops:
  7.3 1.4 copy.70
  10.1 1.0 reshape.297
  15.9 119.8 %shard_map.398 = (bf16[2,2,2,4,24,2304]{5,4,3,2,1,0:T(8,128)(2,1)}, bf16[2,2,2,4,24,3328]{5,4,3,2,1,0:T(8,128)(2,1)}, bf16[2,2,2,96,1536]{4,3,2,1,0:T(8,128)(2,1...) custom-call(bf16[24,2304]{1,0:T(8,128)(2,1)} %refs_0_.1, ...), custom_call_target="tpu_custom_call" | custom-call | tf_op jit(solution)/shard_map/pallas_call | solution.py:609
  135.8 1.1 copy.112
  142.2 5.9 %convolution_convert_fusion.q_ref.k_ref.v_ref = bf16[1024,2304]{1,0:T(8,128)(2,1)} fusion(bf16[1024,768]{1,0:T(8,128)(2,1)S(1)} %bitcast.128, bf16[768,2304]{1,0:T(8,128)(2,1)S(1)} %bitcast.125), kind=kOutput, calls=%fused_computation | convolution fusion | flops 3626237952 | bytes 9830400 | tf_op jit(solution)/shard_map/dot_general | solution.py:18
  148.1 21.1 %shard_map.399 = (bf16[1024,768]{1,0:T(8,128)(2,1)S(1)}, f32[6,2,1024]{2,1,0:T(2,128)S(1)}) custom-call(bf16[1024,2304]{1,0:T(8,128)(2,1)} %convolution_convert_fusion.q_ref.k_ref.v_ref, bf16[1024,2304]{1,0:T(8,128)(2,1)} %convolution_convert_fusion.q_ref.k_ref.v_ref, bf16[1024,2304]{1,0:T(8,128)(2,1)} %convolution_convert_fusion.q_ref.k_ref.v_ref), custom_call_target="tpu_custom_call" | custom-call | flops 6442450944 | bytes 6291456 | tf_op jit(solution)/shard_map/pallas_call | solution.py:89
  169.2 1.2 copy-done.1
  170.4 1.7 slice-done
  172.2 28.0 %shard_map.400 = (f32[1024,768]{1,0:T(8,128)}, bf16[1024,768]{1,0:T(8,128)(2,1)}, bf16[1024,3072]{1,0:T(8,128)(2,1)}, bf16[1024,3072]{1,0:T(8,128)(2,1)}, f32[10...) custom-call(bf16[1024,768]{1,0:T(8,128)(2,1)} %bitcast.119, bf16[1024,768]{1,0:T(8,128)(2,1)} %copy-done.1, ...), custom_call_target="tpu_custom_call" | custom-call | tf_op jit(solution)/shard_map/pallas_call | solution.py:1134
  200.2 74.6 %shard_map.401 = (f32[1024,768]{1,0:T(8,128)}, bf16[1024,768]{1,0:T(8,128)(2,1)S(1)}, bf16[80,768]{1,0:T(8,128)(2,1)S(1)}, f32[24,768]{1,0:T(8,128)S(1)}, f32[64...) custom-call(bf16[1024,768]{1,0:T(8,128)(2,1)} %get-tuple-element.75.final_ref, ...), custom_call_target="tpu_custom_call" | custom-call | tf_op jit(solution)/shard_map/pallas_call | solution.py:970
  274.8 1.2 copy-done.4
  276.0 39.7 %shard_map.402 = (bf16[768,6912]{1,0:T(8,128)(2,1)}, f32[1024,768]{1,0:T(8,128)}, bf16[1024,768]{1,0:T(8,128)(2,1)}, f32[6,2,1024]{2,1,0:T(2,128)}, f32[4,1,768]{2,1,0:T(1,128)}, /*index=5*/f32[8,768]{1,0:T(8,128)}) custom-call(f32[1024,768]{1,0:T(8,128)} %get-tuple-element.81.dy_ref, bf16[1024,768]{1,0:T(8,128)(2,1)} %copy-done.4, ...), custom_call_target="tpu_custom_call" | custom-call | tf_op jit(solution)/shard_map/pallas_call | solution.py:1197
  316.0 1.1 copy-done.11
  317.1 1.8 add_convert_fusion.normed_ref
  318.9 46.3 %shard_map.403 = (bf16[1024,768]{1,0:T(8,128)(2,1)}, bf16[1024,768]{1,0:T(8,128)(2,1)}, bf16[1024,768]{1,0:T(8,128)(2,1)}, bf16[2,2,2,4,80,768]{5,4,3,2,1,0:T(8,128)(2,1)}) custom-call(bf16[1024,2304]{1,0:T(8,128)(2,1)} %convolution_convert_fusion.q_ref.k_ref.v_ref, bf16[1024,2304]{1,0:T(8,128)(2,1)} %convolution_convert_fusion.q_ref.k_ref.v_ref, ...), custom_call_target="tpu_custom_call" | custom-call | tf_op jit(solution)/shard_map/pallas_call | solution.py:1093
  365.2 5.3 %copy.109 = bf16[32,80,768]{2,0,1:T(8,128)(2,1)} copy(bf16[32,80,768]{2,1,0:T(8,128)(2,1)} %bitcast.123) | data formatting | bytes 7864320 | tf_op jit(solution)/shard_map/reshape | solution.py:1431
  370.7 2.6 copy-done
  373.3 4.4 shard_map.406
  377.8 0.9 reshape.326
  379.1 1.1 reshape.325
  380.7 1.1 reshape.328
  381.9 0.8 slice_convert_fusion
  383.3 0.8 broadcast_multiply_fusion.1
  385.6 17.0 %shard_map.404 = (bf16[768,2560]{1,0:T(8,128)(2,1)}, bf16[1024,768]{1,0:T(8,128)(2,1)}) custom-call(bf16[1024,768]{1,0:T(8,128)(2,1)} %get-tuple-element.91.dq_ref, bf16[1024,768]{1,0:T(8,128)(2,1)} %get-tuple-element.92.dk_ref, bf16[1024,768]{1,0:T(8,128)(2,1)} %get-tuple-element.93.dv_ref, bf16[1024,768]{1,0:T(8,128)(2,1)} %add_convert_fusion.normed_ref, ...), custom_call_target="tpu_custom_call" | custom-call | tf_op jit(solution)/shard_map/pallas_call | solution.py:1232
  402.6 2.3 copy-done.2
  404.9 1.4 copy-done.3
  406.3 60.3 %shard_map.405 = (f32[24,2560]{1,0:T(8,128)S(1)}, bf16[4,256,768]{2,1,0:T(8,128)(2,1)S(1)}) custom-call(bf16[2,2,2,4,24,2560]{5,4,3,2,1,0:T(8,128)(2,1)S(1)} %bitcast.110, bf16[4,256,768]{2,1,0:T(8,128)(2,1)S(1)} %bitcast.111), custom_call_target="tpu_custom_call" | custom-call | tf_op jit(solution)/shard_map/pallas_call | solution.py:692
  468.3 1.9 convert_element_type.66
  473.9 8.1 %reduce-scatter.2.cloned.1.call-done = bf16[24,6912]{1,0:T(8,128)(2,1)} async-done(((bf16[768,6912]{1,0:T(8,128)(2,1)}), bf16[24,6912]{1,0:T(8,128)(2,1)}) %reduce-scatter.2.cloned.1.call-update) | async-done | bytes 331792 | tf_op jit(solution)/shard_map/reduce_scatter | solution.py:1425
  482.1 1.0 fusion.10
  484.0 1.2 copy.85
  485.9 1.4 slice.152
  (186 shorter events, 22.4 us)
Async XLA Ops:
  7.2 4.0 copy-start.22
  7.2 4.0 copy-start.23
  7.2 4.9 copy-start.20
  7.2 5.0 %copy-start.16 = (bf16[24,3072]{1,0:T(8,128)(2,1)S(1)}, bf16[24,3072]{1,0:T(8,128)(2,1)}, u32[]{:S(2)}) copy-start(bf16[24,3072]{1,0:T(8,128)(2,1)} %param.35) | copy-start | bytes 442372
  7.2 5.4 %copy-start.17 = (bf16[24,3072]{1,0:T(8,128)(2,1)S(1)}, bf16[24,3072]{1,0:T(8,128)(2,1)}, u32[]{:S(2)}) copy-start(bf16[24,3072]{1,0:T(8,128)(2,1)} %param.40) | copy-start | bytes 442372
  7.2 6.1 %copy-start.24 = (bf16[24,768]{1,0:T(8,128)(2,1)S(1)}, bf16[24,768]{1,0:T(8,128)(2,1)}, u32[]{:S(2)}) copy-start(bf16[24,768]{1,0:T(8,128)(2,1)} %param.44) | copy-start | bytes 110596
  7.3 163.2 %all-gather.2.cloned.1.call-start = ((), (), s32[]{:S(2)}) async-start(), calls=%async_computation.1 | async-start | bytes 13381632 | tf_op jit(solution)/shard_map/all_gather | solution.py:1393
  8.7 4.7 copy-start.15
  8.7 4.9 copy-start.21
  8.7 5.1 %copy-start.27 = (bf16[11,24]{1,0:T(8,128)(2,1)S(1)}, bf16[11,24]{1,0:T(8,128)(2,1)}, u32[]{:S(2)}) copy-start(bf16[11,24]{1,0:T(8,128)(2,1)} %param.31) | copy-start | bytes 1588
  8.8 5.2 %copy-start.28 = (bf16[7,24]{1,0:T(8,128)(2,1)S(1)}, bf16[7,24]{1,0:T(8,128)(2,1)}, u32[]{:S(2)}) copy-start(bf16[7,24]{1,0:T(8,128)(2,1)} %param.43) | copy-start | bytes 1012
  8.8 5.3 %copy-start.29 = (bf16[96]{0:T(256)(128)(2,1)S(1)}, bf16[96]{0:T(256)(128)(2,1)}, u32[]{:S(2)}) copy-start(bf16[96]{0:T(256)(128)(2,1)} %param.29) | copy-start | bytes 580
  8.8 5.3 %copy-start.30 = (bf16[96]{0:T(256)(128)(2,1)S(1)}, bf16[96]{0:T(256)(128)(2,1)}, u32[]{:S(2)}) copy-start(bf16[96]{0:T(256)(128)(2,1)} %param.36) | copy-start | bytes 580
  8.8 5.3 %copy-start.31 = (bf16[96]{0:T(256)(128)(2,1)S(1)}, bf16[96]{0:T(256)(128)(2,1)}, u32[]{:S(2)}) copy-start(bf16[96]{0:T(256)(128)(2,1)} %param.41) | copy-start | bytes 580
  11.1 3.8 copy-start.18
  11.2 3.8 copy-start.19
  12.0 470.1 %reduce-scatter.2.cloned.1.call-start = ((), (), s32[]{:S(2)}) async-start(), calls=%async_computation.2 | async-start | bytes 10948608 | tf_op jit(solution)/shard_map/reduce_scatter | solution.py:1425
  14.9 124.8 %copy-start.25 = (s32[32,32]{1,0:T(8,128)S(1)}, s32[32,32]{1,0:T(8,128)}, u32[]{:S(2)}) copy-start(s32[32,32]{1,0:T(8,128)} %param.25) | copy-start | bytes 12292
  135.8 4.3 copy-start.10
  140.1 2.1 copy-start.12
  170.4 29.8 %copy-start.8 = (f32[6,2,1024]{2,1,0:T(2,128)}, f32[6,2,1024]{2,1,0:T(2,128)S(1)}, u32[]{:S(2)}) copy-start(f32[6,2,1024]{2,1,0:T(2,128)S(1)} %get-tuple-element.88.lse_ref) | copy-start | bytes 147460
  170.4 1.7 slice-start
  172.1 28.0 %copy-start.5 = (f32[11,768]{1,0:T(8,128)S(1)}, f32[11,768]{1,0:T(8,128)}, u32[]{:S(2)}) copy-start(f32[11,768]{1,0:T(8,128)} %reshape.299.vec_ref.ivec_ref) | copy-start | bytes 101380
  172.1 28.0 %copy-start.6 = (bf16[4,4,16,768]{3,2,1,0:T(8,128)(2,1)S(1)}, bf16[4,4,16,768]{3,2,1,0:T(8,128)(2,1)}, u32[]{:S(2)}) copy-start(bf16[4,4,16,768]{3,2,1,0:T(8,128)(2,1)} %get-tuple-element.77) | copy-start | bytes 1179652
  172.2 28.0 %copy-start.9 = (f32[2]{0:T(128)S(1)}, f32[2]{0:T(128)}, u32[]{:S(2)}) copy-start(f32[2]{0:T(128)} %temp_ref.1) | copy-start | bytes 28
  274.8 1.2 copy-start.4
  276.0 39.7 %copy-start.7 = (bf16[80,768]{1,0:T(8,128)(2,1)}, bf16[80,768]{1,0:T(8,128)(2,1)S(1)}, u32[]{:S(2)}) copy-start(bf16[80,768]{1,0:T(8,128)(2,1)S(1)} %get-tuple-element.90.rows_ref) | copy-start | bytes 368644
  315.7 1.4 copy-start.11
  370.7 2.6 copy-start
  377.8 6.4 %copy-start.26 = (f32[4,1,768]{2,1,0:T(1,128)S(1)}, f32[4,1,768]{2,1,0:T(1,128)}, u32[]{:S(2)}) copy-start(f32[4,1,768]{2,1,0:T(1,128)} %get-tuple-element.97) | copy-start | bytes 36868
  402.6 2.3 copy-start.2
  404.9 1.4 copy-start.3
  (3 other events, 2.9 us)
Sparse Core Ops, SparseCore 0:
  12.1 144.1 all-gather.1
  315.9 166.1 reduce-scatter.1

commit v4 on v3

--- a/solution.py
+++ b/solution.py
@@ -52,8 +52,10 @@
 
 
 def mm_two(a, b, cb=0):
-    high, low = split_two(a)
-    return mm(high, b, 1, cb) + mm(low, b, 1, cb)
+    n = a.shape[0]
+    high = a.astype(BF).astype(F32)
+    both = mm(jnp.concatenate([high, a - high], 0).astype(BF), b, 1, cb)
+    return both[0:n] + both[n : 2 * n]
 
 
 def gelu_pair(u):
@@ -717,28 +719,31 @@
     part = width // 4
     started = []
 
-    def exchange(n, values_for):
+    def exchange(n, values, rows=4):
+        if not isinstance(values, list):
+            values = [values] * 4
         for q in range(4):
-            send_a[n, q] = values_for(q)
+            send_a[n, q, 0:rows] = values[q]
         recv_a[n, z] = send_a[n, z]
-        arrive = []
-        for k in (1, 2, 3):
+        copies = []
+        for k in (3, 2, 1):
             to, fro = (z + k) % 4, (z + 4 - k) % 4
-            copy = pltpu.make_async_remote_copy(send_a.at[n, to], recv_a.at[n, z], send_sem.at[n, k - 1],
-                                                recv_sem.at[n, k - 1], device_id=me.at_z(k), device_id_type=MESH)
+            make = lambda dst: pltpu.make_async_remote_copy(
+                send_a.at[n, to], dst, send_sem.at[n, k], recv_sem.at[n, k], device_id=me.at_z(k), device_id_type=MESH)
+            copy = make(recv_a.at[n, z])
             copy.start()
             started.append(copy)
-            arrive.append(pltpu.make_async_remote_copy(send_a.at[n, to], recv_a.at[n, fro], send_sem.at[n, k - 1],
-                                                       recv_sem.at[n, k - 1], device_id=me.at_z(k), device_id_type=MESH))
+            copies.append(make(recv_a.at[n, fro]))
 
         def done():
-            for a in arrive:
+            for a in copies:
                 a.wait_recv()
-            return [recv_a[n, q] for q in range(4)]
+            return [recv_a[n, q, 0:rows] for q in range(4)]
 
         return done
 
-    pad4 = jnp.zeros((4, width), F32)
+    total = lambda blocks: (blocks[0] + blocks[1]) + (blocks[2] + blocks[3])
+    by_head = lambda blocks, n=3: jnp.concatenate([blocks[q][h : h + 1] for h in range(n) for q in range(4)], 0)
     pad1 = jnp.zeros((1, width), F32)
     ivec, tvec = ivec_ref[...], tvec_ref[...]
     iv = lambda k: ivec[k:k + 1]
@@ -762,6 +767,8 @@
         n = a.shape[0] // 3
         return sum(a[h * n:(h + 1) * n] * own[h] for h in range(3))
 
+    p_q = mm(iv(7).astype(BF), small("pq"))
+    get_keys = exchange(0, mm_two(spread(p_q), small("pk"), 1) * 0.125, 3)
     t_x = tokens_ref[...].astype(F32)
     tn = layer_norm(t_x, tv(0), tv(1)).astype(BF)
     tn_ref[...] = tn.astype(F32)
@@ -779,50 +786,41 @@
     t_probs = e / jnp.sum(e, -1, keepdims=True)
     t_used = mm_two(t_probs, tn)
     t_mixed = fold(mm(t_used.astype(BF), small("tv"))).astype(BF)
-    t_part = mm(t_mixed[:, 0:part], t_out_w())
-
-    p_q = mm(iv(7).astype(BF), small("pq"))
-    p_keys_my = mm_two(spread(p_q), small("pk"), 1) * 0.125
-    block = jnp.concatenate([t_part, p_keys_my, pad1], 0)
-    x0 = exchange(0, lambda q: block)()
-    t_hidden = x_last + (x0[0] + x0[1] + x0[2] + x0[3])[0:4]
-    p_keys = jnp.concatenate([x0[q][4:7] for q in range(4)], 0)
-    t_second = layer_norm(t_hidden, tv(2), tv(3)).astype(BF)
-    t_value, t_slope = gelu_pair(mm(t_second, t_up()) + tbias_ref[...])
-    t_active = t_value.astype(BF)
-    t_part = mm(t_active, t_down())
+    get_t = exchange(1, mm(t_mixed[:, 0:part], t_out_w()), 4)
     final = final_ref[...]
+    p_keys = jnp.concatenate(get_keys(), 0)
     p_scores = mm_two(p_keys, final, 1)
     e = jnp.exp(p_scores - jnp.max(p_scores, -1, keepdims=True))
     p_probs = e / jnp.sum(e, -1, keepdims=True)
     used = mm_two(p_probs, final)
-    x1 = exchange(1, lambda q: jnp.concatenate([t_part, used[3 * q:3 * q + 3], pad1], 0))()
-    t_out = t_hidden + (x1[0] + x1[1] + x1[2] + x1[3])[0:4] + tv(4)
+    get_p = exchange(2, [used[3 * q:3 * q + 3] for q in range(4)], 3)
+    t_hidden = x_last + total(get_t())
+    t_second = layer_norm(t_hidden, tv(2), tv(3)).astype(BF)
+    t_value, t_slope = gelu_pair(mm(t_second, t_up()) + tbias_ref[...])
+    t_active = t_value.astype(BF)
+    get_t = exchange(3, mm(t_active, t_down()), 4)
+    pooled = fold(mm_two(by_head(get_p()), small("pv")))
+    get_p = exchange(4, mm_two(pooled[:, 0:part], p_out_w()), 4)
+    t_out = t_hidden + total(get_t()) + tv(4)
     t_final = layer_norm(t_out, tv(5), tv(6)).astype(BF)
     t_piece = mm(t_final, small("thead"))
-    got = jnp.concatenate([x1[q][4 + h:5 + h] for h in range(3) for q in range(4)], 0)
-    pooled = fold(mm_two(got, small("pv")))
-    h_part = mm_two(pooled[:, 0:part], p_out_w())
-    block = jnp.concatenate([h_part, jnp.concatenate([t_piece[:, 0:part], jnp.zeros((4, width - part), F32)], 1)], 0)
-    x2 = exchange(2, lambda q: block)()
-    h_start = (x2[0] + x2[1] + x2[2] + x2[3])[0:4]
-    text_embed = jnp.concatenate([x2[q][4:8, 0:part] for q in range(4)], 1)
+    get_t = exchange(5, jnp.concatenate([t_piece[:, 0:part], jnp.zeros((4, width - part), F32)], 1), 4)
+    h_start = total(get_p())
     h_normed = layer_norm(h_start, iv(8), iv(9)).astype(BF)
     h_value, h_slope = gelu_pair(mm(h_normed, p_up()) + pbias_ref[...])
     h_active = h_value.astype(BF)
-    h_part = mm(h_active, p_down())
-    block = jnp.concatenate([h_part, pad4], 0)
-    x3 = exchange(3, lambda q: block)()
-    image_embed = h_start + ((x3[0] + x3[1] + x3[2] + x3[3])[0:4] + iv(10))
+    get_p = exchange(6, mm(h_active, p_down()), 4)
+    text_embed = jnp.concatenate([blk[:, 0:part] for blk in get_t()], 1)
+    image_embed = h_start + (total(get_p()) + iv(10))
     send_l[...] = jnp.concatenate([image_embed, text_embed], 0)
     recv_l[i] = send_l[...]
     arrive = []
     for k in range(1, n_dp):
-        copy = pltpu.make_async_remote_copy(send_l, recv_l.at[i], send_sem.at[8, k], recv_sem.at[8, k],
+        copy = pltpu.make_async_remote_copy(send_l, recv_l.at[i], send_sem.at[15, k], recv_sem.at[15, k],
                                             device_id=plane[k - 1], device_id_type=MESH)
         copy.start()
         started.append(copy)
-        arrive.append(pltpu.make_async_remote_copy(send_l, recv_l.at[(i + n_dp - k) % n_dp], send_sem.at[8, k], recv_sem.at[8, k],
+        arrive.append(pltpu.make_async_remote_copy(send_l, recv_l.at[(i + n_dp - k) % n_dp], send_sem.at[15, k], recv_sem.at[15, k],
                                                    device_id=plane[k - 1], device_id_type=MESH))
     for a in arrive:
         a.wait_recv()
@@ -835,11 +833,11 @@
     label = label_ref[...]
     valid = label != 0.0
     signed = label * logits
-    total = n_dp * 4
+    n_all = n_dp * 4
     nll = jnp.maximum(-signed, 0.0) + jnp.log(1.0 + jnp.exp(-jnp.abs(signed)))
     add_all = lambda a: jnp.sum(jnp.sum(a, -1, keepdims=True), 0, keepdims=True)
-    loss = add_all(jnp.where(valid, nll, 0.0)) / total
-    g = jnp.where(valid, -label / (1.0 + jnp.exp(signed)), 0.0) / total
+    loss = add_all(jnp.where(valid, nll, 0.0)) / n_all
+    g = jnp.where(valid, -label / (1.0 + jnp.exp(signed)), 0.0) / n_all
     gt0 = temper * add_all(g * cosine)
     gt1 = add_all(g)
     at = lax.broadcasted_iota(jnp.int32, (8, 128), 1)
@@ -850,26 +848,27 @@
     d_image, d_text = d_both[0:4], d_both[4:8]
 
     dh_upper = mm_two(d_image, p_down(), 1) * h_slope
-    h_part = mm_two(dh_upper, p_up(), 1)
+    get_p = exchange(7, mm_two(dh_upper, p_up(), 1), 4)
     d_text_my = sum(jnp.where(z == q, d_text[:, part * q:part * q + part], 0.0) for q in range(4))
-    t_part = mm_two(d_text_my, small("thead")[:, 0:part], 1)
-    block = jnp.concatenate([h_part, t_part], 0)
-    x4 = exchange(4, lambda q: block)()
-    both = x4[0] + x4[1] + x4[2] + x4[3]
-    d_start, dv8, dv9 = norm_back_rows(h_start, iv(8), both[0:4])
+    get_t = exchange(8, mm_two(d_text_my, small("thead")[:, 0:part], 1), 4)
+    d_start, dv8, dv9 = norm_back_rows(h_start, iv(8), total(get_p()))
     d_start = d_image + d_start
     dv10 = jnp.sum(d_image, 0, keepdims=True)
     d_pooled = mm_two(d_start, p_out_w(), 1)
     d_pooled = jnp.concatenate([d_pooled, jnp.zeros((4, 256 - part), F32)], 1)
     p_values_my = mm_two(spread(d_pooled), small("pv"), 1)
-    dt_out, tv5, tv6 = norm_back_rows(t_out, tv(5), both[4:8])
+    get_p = exchange(9, [jnp.concatenate([p_values_my[4 * h + q:4 * h + q + 1] for h in range(3)], 0) for q in range(4)], 3)
+    dt_out, tv5, tv6 = norm_back_rows(t_out, tv(5), total(get_t()))
     tv4 = jnp.sum(dt_out, 0, keepdims=True)
     dt_branch = dt_out.astype(BF)
     dt_upper = (mm(dt_branch, t_down(), 1, 1) * t_slope).astype(BF)
-    t_part = mm(dt_upper, t_up(), 1, 1)
-    x5 = exchange(5, lambda q: jnp.concatenate(
-        [t_part] + [p_values_my[4 * h + q:4 * h + q + 1] for h in range(3)] + [pad1], 0))()
-    dt_hidden, tv2, tv3 = norm_back_rows(t_hidden, tv(2), (x5[0] + x5[1] + x5[2] + x5[3])[0:4])
+    get_t = exchange(10, mm(dt_upper, t_up(), 1, 1), 4)
+    p_values = jnp.concatenate(get_p(), 0)
+    d_probs = mm_two(p_values, final, 1)
+    d_scores = p_probs * (d_probs - jnp.sum(p_probs * d_probs, -1, keepdims=True))
+    p_used = mm_two(d_scores, final) * 0.125
+    get_p = exchange(11, [p_used[3 * q:3 * q + 3] for q in range(4)], 3)
+    dt_hidden, tv2, tv3 = norm_back_rows(t_hidden, tv(2), total(get_t()))
     dt_hidden = dt_out + dt_hidden
     dt_attend = dt_hidden.astype(BF)
     dt_mixed = mm(dt_attend, t_out_w(), 1, 1).astype(BF).astype(F32)
@@ -885,20 +884,15 @@
     for c in range(4):
         dn = dn + jnp.where(row_at == last_at[c], dq_back[c:c + 1], 0.0)
     dn_ref[...] = dn.astype(BF)
-    p_values = jnp.concatenate([x5[q][4:7] for q in range(4)], 0)
-    d_probs = mm_two(p_values, final, 1)
-    d_scores = p_probs * (d_probs - jnp.sum(p_probs * d_probs, -1, keepdims=True))
-    p_used = mm_two(d_scores, final) * 0.125
-    x6 = exchange(6, lambda q: jnp.concatenate([p_used[3 * q:3 * q + 3], pad1, pad4], 0))
     arrive = []
     for k in (1, 2, 3):
         to, fro = (z + k) % 4, (z + 4 - k) % 4
         rows_to = dn_ref.at[pl.ds(pl.multiple_of(64 * to, 64), 64), :]
-        copy = pltpu.make_async_remote_copy(rows_to, recv_t.at[z], send_sem.at[7, k], recv_sem.at[7, k],
+        copy = pltpu.make_async_remote_copy(rows_to, recv_t.at[z], send_sem.at[14, k], recv_sem.at[14, k],
                                             device_id=me.at_z(k), device_id_type=MESH)
         copy.start()
         started.append(copy)
-        arrive.append(pltpu.make_async_remote_copy(rows_to, recv_t.at[fro], send_sem.at[7, k], recv_sem.at[7, k],
+        arrive.append(pltpu.make_async_remote_copy(rows_to, recv_t.at[fro], send_sem.at[14, k], recv_sem.at[14, k],
                                                    device_id=me.at_z(k), device_id_type=MESH))
     s_high, s_low = split_two(d_scores)
     q_high, q_low = split_two(p_probs)
@@ -923,8 +917,7 @@
         return carry
 
     lax.fori_loop(0, final_ref.shape[0] // tile, step, 0)
-    got6 = x6()
-    w_got = jnp.concatenate([got6[q][h:h + 1] for h in range(3) for q in range(4)], 0)
+    w_got = by_head(get_p())
     dq_rows = fold(mm_two(w_got, small("pk")))
     dq_my = jnp.sum(dq_rows, 0, keepdims=True)
     recv_t[z] = dn_ref[pl.ds(pl.multiple_of(64 * z, 64), 64), :]
@@ -974,13 +967,53 @@
         out_shape=[f(length, width), jax.ShapeDtypeStruct((length, width), BF), jax.ShapeDtypeStruct((ROWS, width), BF), f(24, width), f(64, width), f(8, 128), f(8 * n_dp, width)],
         scratch_shapes=[
             pltpu.VMEM((256, width), F32), pltpu.VMEM((256, width), BF),
-            pltpu.VMEM((7, 4, 8, width), F32), pltpu.VMEM((7, 4, 8, width), F32),
+            pltpu.VMEM((12, 4, 4, width), F32), pltpu.VMEM((12, 4, 4, width), F32),
             pltpu.VMEM((8, width), F32), pltpu.VMEM((n_dp, 8, width), F32),
             pltpu.VMEM((length, 128), F32), pltpu.VMEM((4, 64, width), BF),
-            pltpu.SemaphoreType.DMA((9, 8)), pltpu.SemaphoreType.DMA((9, 8)),
+            pltpu.SemaphoreType.DMA((16, 8)), pltpu.SemaphoreType.DMA((16, 8)),
         ],
         compiler_params=pltpu.CompilerParams(collective_id=cid, has_side_effects=True, vmem_limit_bytes=50 << 20),
     )(final, block_out, tokens, tp, downs, outs, ivec, tvec, pbias, tbias, label, temp)
+
+
+def plane_moves(me, out, s):
+    y, x, c = me.y, me.x, me.c
+    n = out.shape[-1] // 2
+    left, right = (lambda r: r.at[..., 0:n]), (lambda r: r.at[..., n : 2 * n])
+    if s == 3:
+        own = out.at[y, x, c]
+        yield 6, left(own), left(own), me.at_x, None, left(out.at[y, 1 - x, c]), None
+        yield 7, right(own), right(own), me.at_y, None, right(out.at[1 - y, x, c]), None
+    elif s == 4:
+        own = out.at[y, :, c]
+        yield 8, left(own), left(own), me.at_y, None, left(out.at[1 - y, :, c]), None
+        own = out.at[:, x, c]
+        yield 9, right(own), right(own), me.at_x, None, right(out.at[:, 1 - x, c]), None
+    else:
+        mine = out.at[:, :, c]
+        yield 10, mine, mine, me.at_c, None, out.at[:, :, 1 - c], None
+
+
+def turn_moves(me, src, home, split):
+    z = me.z
+    for k in (3, 2, 1):
+        to, fro = (z + k) % 4, (z + 4 - k) % 4
+        yield k - 1, src.at[to] if split else src, home.at[z], me.at_z(k), None, home.at[fro], None
+
+
+def run_moves(moves, act, send, recv):
+    for slot, src, dst, dev, go, come, arrives in moves:
+        make = lambda a, b: pltpu.make_async_remote_copy(
+            a, b, send.at[slot], recv.at[slot], device_id=dev, device_id_type=MESH
+        )
+        if act == "arrived":
+            copy, when = make(src, come).wait_recv, arrives
+        else:
+            copy, when = getattr(make(src, dst), "start" if act == "start" else "wait_send"), go
+        if when is None:
+            copy()
+        else:
+            pl.when(when)(lambda: copy())
 
 
 class Spread:
@@ -1002,35 +1035,11 @@
                 slab, come = jnp.clip(slab, 0, 3), jnp.clip(come, 0, 3)
                 src = self.src if s == 0 else home.at[slab]
                 yield s + (0 if up else 3), src, home.at[slab], me.at_z(1 if up else 3), go, home.at[come], arrives
-        elif s == 5:
-            mine = out.at[:, :, c]
-            yield 10, mine, mine, me.at_c, None, out.at[:, :, 1 - c], None
         else:
-            n = out.shape[-1] // 2
-            left, right = (lambda r: r.at[..., 0:n]), (lambda r: r.at[..., n : 2 * n])
-            if s == 3:
-                own = out.at[y, x, c]
-                yield 6, left(own), left(own), me.at_x, None, left(out.at[y, 1 - x, c]), None
-                yield 7, right(own), right(own), me.at_y, None, right(out.at[1 - y, x, c]), None
-            else:
-                own = out.at[y, :, c]
-                yield 8, left(own), left(own), me.at_y, None, left(out.at[1 - y, :, c]), None
-                own = out.at[:, x, c]
-                yield 9, right(own), right(own), me.at_x, None, right(out.at[:, 1 - x, c]), None
+            yield from plane_moves(me, out, s)
 
     def each(self, s, act):
-        for slot, src, dst, dev, go, come, arrives in self.moves(s):
-            make = lambda a, b: pltpu.make_async_remote_copy(
-                a, b, self.send.at[slot], self.recv.at[slot], device_id=dev, device_id_type=MESH
-            )
-            if act == "arrived":
-                copy, when = make(src, come).wait_recv, arrives
-            else:
-                copy, when = getattr(make(src, dst), "start" if act == "start" else "wait_send"), go
-            if when is None:
-                copy()
-            else:
-                pl.when(when)(lambda: copy())
+        run_moves(self.moves(s), act, self.send, self.recv)
 
     def keep(self):
         me = self.me
@@ -1101,9 +1110,97 @@
     )(proj, proj, proj, d_out, lse, inner, rows)
 
 
-def mlp_fwd_kernel(x_ref, mixed_ref, wo_ref, wu_ref, wd_ref, bias_ref, vec_ref,
-                   hidden_ref, second_ref, active_ref, slope_ref, block_ref, final_ref, total):
+def attend_fwd_kernel_hosting(q_ref, k_ref, v_ref, split_ref, downs_ref, tokens_ref,
+                              o_ref, lse_ref, tp_ref, down_ref, token_ref, send, recv, local):
+    h_at = pl.program_id(0)
+    me = Place()
+    home = tp_ref.at[me.y, me.x, me.c]
+    down_home = down_ref.at[me.y, me.x, me.c]
+    keeps = [
+        pltpu.make_async_copy(split_ref.at[me.z], home.at[me.z], local.at[0]),
+        pltpu.make_async_copy(downs_ref, down_home, local.at[1]),
+        pltpu.make_async_copy(tokens_ref, token_ref.at[me.z], local.at[2]),
+    ]
+    groups = {
+        "split": (lambda: turn_moves(me, split_ref, home, True), 0),
+        "tokens": (lambda: turn_moves(me, tokens_ref, token_ref, False), 2),
+        "split_xy": (lambda: plane_moves(me, tp_ref, 3), 0),
+        "down_xy": (lambda: plane_moves(me, down_ref, 3), 1),
+    }
+
+    def act(name, what):
+        moves, a = groups[name]
+        run_moves(moves(), what, send.at[a], recv.at[a])
+
+    def first():
+        greet([me.at_z(1), me.at_z(2), me.at_z(3), me.at_x, me.at_y])
+        for keep in keeps:
+            keep.start()
+        act("split", "start")
+        keeps[1].wait()
+        act("down_xy", "start")
+
+    def middle_step():
+        act("split", "arrived")
+        keeps[0].wait()
+        act("split_xy", "start")
+        act("tokens", "start")
+
+    def last():
+        for name in ("split_xy", "down_xy", "tokens"):
+            act(name, "arrived")
+        keeps[2].wait()
+        for name in groups:
+            act(name, "sent")
+
+    pl.when(h_at == 0)(first)
+    pl.when(h_at == 3)(middle_step)
+    attend_fwd_kernel(q_ref, k_ref, v_ref, o_ref, lse_ref)
+    pl.when(h_at == pl.num_programs(0) - 1)(last)
+
+
+def attend_fwd_and_gather(proj, split, downs, tokens, cid):
+    length, width = proj.shape[0], proj.shape[1] // 3
+    pairs = width // 128
+    block = lambda part: pl.BlockSpec((length, 128), lambda h: (0, part * pairs + h))
+    hbm = pl.BlockSpec(memory_space=pl.ANY)
+    s = jax.ShapeDtypeStruct
+    return pl.pallas_call(
+        attend_fwd_kernel_hosting,
+        grid=(pairs,),
+        in_specs=[block(0), block(1), block(2), hbm, hbm, hbm],
+        out_specs=[block(0), pl.BlockSpec((1, 2, length), lambda h: (h, 0, 0)), hbm, hbm, hbm],
+        out_shape=[
+            s((length, width), BF),
+            s((pairs, 2, length), F32),
+            s((2, 2, 2) + split.shape, BF),
+            s((2, 2, 2) + downs.shape, BF),
+            s((4,) + tokens.shape, BF),
+        ],
+        scratch_shapes=[pltpu.SemaphoreType.DMA((3, 11)), pltpu.SemaphoreType.DMA((3, 11)), pltpu.SemaphoreType.DMA((3,))],
+        compiler_params=pltpu.CompilerParams(collective_id=cid, has_side_effects=True, vmem_limit_bytes=48 << 20),
+    )(proj, proj, proj, split, downs, tokens)
+
+
+def mlp_fwd_kernel(x_ref, mixed_ref, wo_ref, wu_ref, wd_ref, bias_ref, vec_ref, tp_in, down_in,
+                   hidden_ref, second_ref, active_ref, slope_ref, block_ref, final_ref, tp_ref, down_ref, total, send, recv):
     k = pl.program_id(0)
+    me = Place()
+
+    def act(s, what):
+        for a, ref in enumerate((tp_ref, down_ref)):
+            run_moves(plane_moves(me, ref, s), what, send.at[a], recv.at[a])
+
+    def first():
+        greet([me.at_x, me.at_y, me.at_c])
+        act(4, "start")
+
+    def then():
+        act(4, "arrived")
+        act(5, "start")
+
+    pl.when(k == 0)(first)
+    pl.when(k == pl.num_programs(0) - 1)(then)
     vec = vec_ref[...]
 
     @pl.when(k == 0)
@@ -1123,24 +1220,30 @@
     def _():
         block_ref[...] = total[...]
         final_ref[...] = layer_norm(total[...], vec[5:6], vec[6:7]).astype(BF)
-
-
-def mlp_fwd(x, mixed, main, bias, vec, fold):
+        act(5, "arrived")
+        act(4, "sent")
+        act(5, "sent")
+
+
+def mlp_fwd(x, mixed, main, bias, vec, fold, tp, downs, cid):
     rows, width = mixed.shape
     whole = pl.BlockSpec((rows, width), lambda k: (0, 0))
     tile = pl.BlockSpec((rows, width), lambda k: (0, k))
     at = lambda f: pl.BlockSpec((width, width), lambda k: (0, f(k)))
     s = lambda n, t: jax.ShapeDtypeStruct((rows, n * width), t)
+    hbm = pl.BlockSpec(memory_space=pl.ANY)
     return pl.pallas_call(
         mlp_fwd_kernel,
         grid=(fold,),
         in_specs=[whole, whole, at(lambda k: 0), at(lambda k: 1 + k), at(lambda k: 1 + fold + k),
-                  pl.BlockSpec((1, 1, width), lambda k: (k, 0, 0)), pl.BlockSpec(vec.shape, lambda k: (0, 0))],
-        out_specs=[whole, whole, tile, tile, whole, whole],
-        out_shape=[s(1, F32), s(1, BF), s(fold, BF), s(fold, BF), s(1, F32), s(1, BF)],
-        scratch_shapes=[pltpu.VMEM((rows, width), F32)],
-        compiler_params=pltpu.CompilerParams(vmem_limit_bytes=56 << 20),
-    )(x, mixed, main, main, main, bias.reshape(fold, 1, width), vec)
+                  pl.BlockSpec((1, 1, width), lambda k: (k, 0, 0)), pl.BlockSpec(vec.shape, lambda k: (0, 0)), hbm, hbm],
+        out_specs=[whole, whole, tile, tile, whole, whole, hbm, hbm],
+        out_shape=[s(1, F32), s(1, BF), s(fold, BF), s(fold, BF), s(1, F32), s(1, BF),
+                   jax.ShapeDtypeStruct(tp.shape, BF), jax.ShapeDtypeStruct(downs.shape, BF)],
+        scratch_shapes=[pltpu.VMEM((rows, width), F32), pltpu.SemaphoreType.DMA((2, 11)), pltpu.SemaphoreType.DMA((2, 11))],
+        input_output_aliases={7: 6, 8: 7},
+        compiler_params=pltpu.CompilerParams(collective_id=cid, has_side_effects=True, vmem_limit_bytes=56 << 20),
+    )(x, mixed, main, main, main, bias.reshape(fold, 1, width), vec, tp, downs)
 
 
 def mlp_bwd_kernel(dy_ref, branch_ref, active_ref, slope_ref, second_ref, hidden_ref, mixed_ref,
@@ -1370,14 +1473,12 @@
     split += [by_heads(probe_pair_weight[:, k * width : (k + 1) * width]) for k in range(2)]
     split = jnp.concatenate(split, 2)
     downs = jnp.concatenate([text_down_weight, probe_down_weight], 1)
-    w_in, tp, downs, small_all, x, tokens = gather(
-        [image_attend_in, split, downs, small, patches, captions],
-        [("full", "S"), ("cols", "S"), ("plane", "S"), ("full", "C"), ("za", None), ("zg", None)],
-        [(0, 0), (2, 0), (2, 3), (3, 0), (0, 1), (3, 1), (1, 0), (0, 2), (3, 2), (0, 3), (4, 0), (5, 0), (3, 3)]
-        + [(1, 3), (0, 4), (2, 4), (3, 4), (1, 4), (0, 5), (2, 5), (3, 5), (1, 5)],
+    w_in, small_all, x = gather(
+        [image_attend_in, small, patches],
+        [("full", "S"), ("full", "C"), ("za", None)],
+        [(0, 0), (1, 0), (0, 1), (1, 1), (0, 2), (1, 2), (0, 3), (2, 0), (1, 3), (0, 4), (1, 4), (0, 5), (1, 5)],
         1,
     )
-    tp, downs = tp.reshape(width, -1), downs.reshape(width, -1)
     w_in = w_in.reshape(width, 3 * width)
     x = x.reshape(length, width)
     main = jnp.concatenate(
@@ -1408,8 +1509,11 @@
 
     normed = layer_norm(x.astype(F32), ivec[0], ivec[1]).astype(BF)
     proj = mm(normed, w_in).astype(BF)
-    mixed, lse = attend_fwd(proj, length)
-    hidden, second, active, slope, block_out, final = mlp_fwd(x, mixed, main, i_bias, ivec, fold)
+    mixed, lse, tp, downs, tokens = attend_fwd_and_gather(proj, split, downs, captions, 5)
+    hidden, second, active, slope, block_out, final, tp, downs = mlp_fwd(
+        x, mixed, main, i_bias, ivec, fold, tp, downs, 6
+    )
+    tp, downs = tp.reshape(width, -1), downs.reshape(width, -1)
 
     labels = (2 * pairs - 1).astype(F32).reshape(n_dp, n_z, n_dp, n_z)
     labels = jnp.pad(labels, ((0, 0), (0, n_z), (0, 0), (n_z, 0))).reshape(2 * world, 2 * world)

time: 500 us -> 485 us (0.970)
  the two profiles are of different devices: /device:TPU:0 before, /device:TPU:8 now
where the time goes in v4:
time: 485 us; the launch traced here: 477 us
  Pallas kernels  401 us (83%)
  local copies, waits for them, and re-layouts  47 us (10%)
  between operations  15.3 us (3%)
  other arithmetic  8.65 us (2%)
  matrix products  5.38 us (1%)
    pallas_call x1, Pallas kernels, gather(): pl.pallas_call(partial(gather_kernel, kinds, order), out_shape=shapes, in...  68.6 us
    pallas_call x1, Pallas kernels, reduce_and_move(): pl.pallas_call(reduce_kernel, in_specs=[hbm, hbm], out_specs=[pl.BlockSpe...  68.5 us
    pallas_call x1, Pallas kernels, middle(): pl.pallas_call(middle_kernel, in_specs=[v] * 11 + [pl.BlockSpec(memory_sp...  58.2 us
    pallas_call x1, Pallas kernels, attend_bwd_and_spread(): pl.pallas_call(attend_bwd_kernel_hosting, grid=(pairs,), in_specs=[block(...  56.8 us
    pallas_call x1, Pallas kernels, attend_fwd_and_gather(): pl.pallas_call(attend_fwd_kernel_hosting, grid=(pairs,), in_specs=[block(...  48.1 us
    pallas_call x1, Pallas kernels, mlp_bwd(): pl.pallas_call(mlp_bwd_kernel, grid=(fold,), in_specs=[whole, whole, tile...  39.7 us
    pallas_call x1, Pallas kernels, mlp_fwd(): pl.pallas_call(mlp_fwd_kernel, grid=(fold,), in_specs=[whole, whole, at(l...  39.1 us
    unnamed x86, local copies, waits for them, and re-layouts  19 us
  transfers between devices with their start and end apart: 2, of which 0 were waited for; matrix products, arithmetic and copies ran while one was open for 8% of the time, Pallas kernels for 55%

profile of v4, /device:TPU:8, one launch (start us, length us, event | category | flops | bytes accessed | tf_op | source)
XLA Modules:
  0.0 476.9 jit_solution(14030361372470193903)
XLA Ops:
  7.3 1.3 copy.72
  10.0 1.0 reshape.297
  12.8 68.6 %shard_map.398 = (bf16[2,2,2,4,24,2304]{5,4,3,2,1,0:T(8,128)(2,1)}, bf16[2,2,2,4,16,128]{5,4,3,2,1,0:T(8,128)(2,1)}, bf16[4,256,768]{2,1,0:T(8,128)(2,1)}) custom-call(bf16[24,2304]{1,0:T(8,128)(2,1)} %refs_0_.1, bf16[16,128]{1,0:T(8,128)(2,1)} %pad_bitcast_fusion.refs_1_, bf16[4,256,768]{2,1,0:T(8,128)(2,1)} %refs_2_.1), custom_call_target="tpu_custom_call" | custom-call | tf_op jit(solution)/shard_map/pallas_call | solution.py:611
  81.4 0.9 copy.114
  83.6 1.2 reshape.286
  90.7 5.4 %convolution_convert_fusion.q_ref.k_ref.v_ref = bf16[1024,2304]{1,0:T(8,128)(2,1)} fusion(bf16[1024,768]{1,0:T(8,128)(2,1)S(1)} %bitcast.128, bf16[768,2304]{1,0:T(8,128)(2,1)S(1)} %bitcast.126), kind=kOutput, calls=%fused_computation | convolution fusion | flops 3626237952 | bytes 9830400 | tf_op jit(solution)/shard_map/dot_general | solution.py:18
  96.1 48.1 %shard_map.399 = (bf16[1024,768]{1,0:T(8,128)(2,1)S(1)}, f32[6,2,1024]{2,1,0:T(2,128)S(1)}, bf16[2,2,2,4,24,3328]{5,4,3,2,1,0:T(8,128)(2,1)}, bf16[2,2,2,96,1536...) custom-call(bf16[1024,2304]{1,0:T(8,128)(2,1)} %convolution_convert_fusion.q_ref.k_ref.v_ref, ...), custom_call_target="tpu_custom_call" | custom-call | tf_op jit(solution)/shard_map/pallas_call | solution.py:1168
  144.3 1.4 copy-done.1
  145.7 1.2 copy-done.2
  147.5 1.7 slice-done
  149.2 39.1 %shard_map.400 = (f32[1024,768]{1,0:T(8,128)}, bf16[1024,768]{1,0:T(8,128)(2,1)}, bf16[1024,3072]{1,0:T(8,128)(2,1)}, bf16[1024,3072]{1,0:T(8,128)(2,1)}, f32[10...) custom-call(bf16[1024,768]{1,0:T(8,128)(2,1)} %bitcast.120, ...), custom_call_target="tpu_custom_call", output_to_operand_aliasing={{6}: (7, {}), {7}: (8, {})} | custom-call | tf_op jit(solution)/shard_map/pallas_call | solution.py:1235
  188.3 58.2 %shard_map.401 = (f32[1024,768]{1,0:T(8,128)}, bf16[1024,768]{1,0:T(8,128)(2,1)S(1)}, bf16[80,768]{1,0:T(8,128)(2,1)S(1)}, f32[24,768]{1,0:T(8,128)S(1)}, f32[64...) custom-call(bf16[1024,768]{1,0:T(8,128)(2,1)} %get-tuple-element.79.final_ref, ...), custom_call_target="tpu_custom_call" | custom-call | tf_op jit(solution)/shard_map/pallas_call | solution.py:963
  246.6 1.2 copy-done.5
  247.8 39.7 %shard_map.402 = (bf16[768,6912]{1,0:T(8,128)(2,1)}, f32[1024,768]{1,0:T(8,128)}, bf16[1024,768]{1,0:T(8,128)(2,1)}, f32[6,2,1024]{2,1,0:T(2,128)}, f32[4,1,768]{2,1,0:T(1,128)}, /*index=5*/f32[8,768]{1,0:T(8,128)}) custom-call(f32[1024,768]{1,0:T(8,128)} %get-tuple-element.85.dy_ref, bf16[1024,768]{1,0:T(8,128)(2,1)} %copy-done.5, ...), custom_call_target="tpu_custom_call" | custom-call | tf_op jit(solution)/shard_map/pallas_call | solution.py:1300
  287.8 1.1 copy-done.12
  288.9 1.8 add_convert_fusion.normed_ref
  290.7 56.8 %shard_map.403 = (bf16[1024,768]{1,0:T(8,128)(2,1)}, bf16[1024,768]{1,0:T(8,128)(2,1)}, bf16[1024,768]{1,0:T(8,128)(2,1)}, bf16[2,2,2,4,80,768]{5,4,3,2,1,0:T(8,128)(2,1)}) custom-call(bf16[1024,2304]{1,0:T(8,128)(2,1)} %convolution_convert_fusion.q_ref.k_ref.v_ref, bf16[1024,2304]{1,0:T(8,128)(2,1)} %convolution_convert_fusion.q_ref.k_ref.v_ref, ...), custom_call_target="tpu_custom_call" | custom-call | tf_op jit(solution)/shard_map/pallas_call | solution.py:1102
  347.5 5.3 %copy.111 = bf16[32,80,768]{2,0,1:T(8,128)(2,1)} copy(bf16[32,80,768]{2,1,0:T(8,128)(2,1)} %bitcast.124) | data formatting | bytes 7864320 | tf_op jit(solution)/shard_map/reshape | solution.py:1535
  353.0 2.1 copy-done
  355.1 4.4 shard_map.406
  359.6 0.9 reshape.326
  361.0 1.1 reshape.325
  362.5 1.1 reshape.328
  365.1 0.8 broadcast_multiply_fusion.1
  367.5 17.1 %shard_map.404 = (bf16[768,2560]{1,0:T(8,128)(2,1)}, bf16[1024,768]{1,0:T(8,128)(2,1)}) custom-call(bf16[1024,768]{1,0:T(8,128)(2,1)} %get-tuple-element.95.dq_ref, bf16[1024,768]{1,0:T(8,128)(2,1)} %get-tuple-element.96.dk_ref, bf16[1024,768]{1,0:T(8,128)(2,1)} %get-tuple-element.97.dv_ref, bf16[1024,768]{1,0:T(8,128)(2,1)} %add_convert_fusion.normed_ref, ...), custom_call_target="tpu_custom_call" | custom-call | tf_op jit(solution)/shard_map/pallas_call | solution.py:1335
  384.6 2.1 copy-done.3
  386.7 1.4 copy-done.4
  388.1 68.5 %shard_map.405 = (f32[24,2560]{1,0:T(8,128)S(1)}, bf16[4,256,768]{2,1,0:T(8,128)(2,1)S(1)}) custom-call(bf16[2,2,2,4,24,2560]{5,4,3,2,1,0:T(8,128)(2,1)S(1)} %bitcast.111, bf16[4,256,768]{2,1,0:T(8,128)(2,1)S(1)} %bitcast.112), custom_call_target="tpu_custom_call" | custom-call | tf_op jit(solution)/shard_map/pallas_call | solution.py:694
  458.3 1.9 convert_element_type.66
  463.9 1.0 fusion.10
  465.8 1.2 copy.87
  467.8 1.4 slice.152
  (184 shorter events, 22.6 us)
Async XLA Ops:
  7.2 3.9 copy-start.21
  7.2 3.9 copy-start.22
  7.2 4.7 copy-start.26
  7.2 4.8 %copy-start.27 = (bf16[7,24]{1,0:T(8,128)(2,1)S(1)}, bf16[7,24]{1,0:T(8,128)(2,1)}, u32[]{:S(2)}) copy-start(bf16[7,24]{1,0:T(8,128)(2,1)} %param.43) | copy-start | bytes 1012
  7.2 4.9 %copy-start.28 = (bf16[96]{0:T(256)(128)(2,1)S(1)}, bf16[96]{0:T(256)(128)(2,1)}, u32[]{:S(2)}) copy-start(bf16[96]{0:T(256)(128)(2,1)} %param.29) | copy-start | bytes 580
  7.2 4.9 %copy-start.29 = (bf16[96]{0:T(256)(128)(2,1)S(1)}, bf16[96]{0:T(256)(128)(2,1)}, u32[]{:S(2)}) copy-start(bf16[96]{0:T(256)(128)(2,1)} %param.36) | copy-start | bytes 580
  7.3 4.9 %copy-start.30 = (bf16[96]{0:T(256)(128)(2,1)S(1)}, bf16[96]{0:T(256)(128)(2,1)}, u32[]{:S(2)}) copy-start(bf16[96]{0:T(256)(128)(2,1)} %param.41) | copy-start | bytes 580
  7.3 75.7 %copy-start.19 = (bf16[24,2304]{1,0:T(8,128)(2,1)S(1)}, bf16[24,2304]{1,0:T(8,128)(2,1)}, u32[]{:S(2)}) copy-start(bf16[24,2304]{1,0:T(8,128)(2,1)} %param.38) | copy-start | bytes 331780
  7.3 140.2 %all-gather.2.cloned.1.call-start = ((), (), s32[]{:S(2)}) async-start(), calls=%async_computation.1 | async-start | bytes 13381632 | tf_op jit(solution)/shard_map/all_gather | solution.py:1494
  8.7 74.5 %copy-start.16 = (bf16[24,3072]{1,0:T(8,128)(2,1)S(1)}, bf16[24,3072]{1,0:T(8,128)(2,1)}, u32[]{:S(2)}) copy-start(bf16[24,3072]{1,0:T(8,128)(2,1)} %param.35) | copy-start | bytes 442372
  11.1 74.2 %copy-start.23 = (bf16[24,768]{1,0:T(8,128)(2,1)S(1)}, bf16[24,768]{1,0:T(8,128)(2,1)}, u32[]{:S(2)}) copy-start(bf16[24,768]{1,0:T(8,128)(2,1)} %param.44) | copy-start | bytes 110596
  11.1 74.3 %copy-start.15 = (bf16[24,768]{1,0:T(8,128)(2,1)S(1)}, bf16[24,768]{1,0:T(8,128)(2,1)}, u32[]{:S(2)}) copy-start(bf16[24,768]{1,0:T(8,128)(2,1)} %param.32) | copy-start | bytes 110596
  11.9 73.7 %copy-start.20 = (bf16[24,1536]{1,0:T(8,128)(2,1)S(1)}, bf16[24,1536]{1,0:T(8,128)(2,1)}, u32[]{:S(2)}) copy-start(bf16[24,1536]{1,0:T(8,128)(2,1)} %param.33) | copy-start | bytes 221188
  11.9 452.0 %reduce-scatter.2.cloned.1.call-start = ((), (), s32[]{:S(2)}) async-start(), calls=%async_computation.2 | async-start | bytes 10948608 | tf_op jit(solution)/shard_map/reduce_scatter | solution.py:1529
  82.5 5.7 %copy-start.24 = (s32[32,32]{1,0:T(8,128)S(1)}, s32[32,32]{1,0:T(8,128)}, u32[]{:S(2)}) copy-start(s32[32,32]{1,0:T(8,128)} %param.25) | copy-start | bytes 12292
  83.6 5.1 %copy-start.11 = (bf16[4,256,768]{2,1,0:T(8,128)(2,1)S(1)}, bf16[4,256,768]{2,1,0:T(8,128)(2,1)}, u32[]{:S(2)}) copy-start(bf16[4,256,768]{2,1,0:T(8,128)(2,1)} %get-tuple-element.73) | copy-start | bytes 4718596
  86.9 2.8 copy-start.17
  86.9 2.8 copy-start.18
  88.7 2.0 copy-start.13
  90.7 5.4 %copy-start.8 = (bf16[4,16,768]{2,1,0:T(8,128)(2,1)S(1)}, bf16[4,16,768]{2,1,0:T(8,128)(2,1)}, u32[]{:S(2)}) copy-start(bf16[4,16,768]{2,1,0:T(8,128)(2,1)} %tokens_ref.1) | copy-start | bytes 294916
  144.3 1.4 copy-start.1
  145.7 1.2 copy-start.2
  147.5 1.7 slice-start
  149.2 39.1 %copy-start.6 = (f32[11,768]{1,0:T(8,128)S(1)}, f32[11,768]{1,0:T(8,128)}, u32[]{:S(2)}) copy-start(f32[11,768]{1,0:T(8,128)} %reshape.299.vec_ref.ivec_ref) | copy-start | bytes 101380
  149.2 39.1 %copy-start.10 = (f32[2]{0:T(128)S(1)}, f32[2]{0:T(128)}, u32[]{:S(2)}) copy-start(f32[2]{0:T(128)} %temp_ref.1) | copy-start | bytes 28
  246.6 1.2 copy-start.5
  247.8 39.7 %copy-start.7 = (bf16[80,768]{1,0:T(8,128)(2,1)}, bf16[80,768]{1,0:T(8,128)(2,1)S(1)}, u32[]{:S(2)}) copy-start(bf16[80,768]{1,0:T(8,128)(2,1)S(1)} %get-tuple-element.94.rows_ref) | copy-start | bytes 368644
  287.5 1.4 copy-start.12
  353.0 2.2 copy-start
  359.6 6.4 %copy-start.25 = (f32[4,1,768]{2,1,0:T(1,128)S(1)}, f32[4,1,768]{2,1,0:T(1,128)}, u32[]{:S(2)}) copy-start(f32[4,1,768]{2,1,0:T(1,128)} %get-tuple-element.101) | copy-start | bytes 36868
  384.6 2.1 copy-start.3
  386.7 1.4 copy-start.4
  (2 other events, 1.4 us)
Sparse Core Ops, SparseCore 0:
  12.0 135.1 all-gather.1
  287.7 170.1 reduce-scatter.1

commit v5 on v4

--- a/solution.py
+++ b/solution.py
@@ -1060,54 +1060,183 @@
             self.each(s, "sent")
 
 
-def attend_bwd_kernel_hosting(q_ref, k_ref, v_ref, do_ref, lse_ref, d_ref, rows_ref, dq_ref, dk_ref, dv_ref, all_ref, send, recv, local):
+class Reduce:
+    def __init__(self, me, g, own, acc, from_c, from_1, from_2, from_z, send, recv, local):
+        self.me, self.g, self.own, self.acc = me, g, own, acc
+        self.from_c, self.from_1, self.from_2, self.from_z = from_c, from_1, from_2, from_z
+        self.send, self.recv, self.local = send, recv, local
+        self.size = acc.shape[-1]
+        self.left, self.right = slice(0, self.size // 2), slice(self.size // 2, self.size)
+
+    def moves(self, n, stage):
+        me, acc = self.me, self.acc.at[n]
+        y, x, z = me.y, me.x, me.z
+        if stage == "core":
+            src = self.g.at[:, :, 1 - me.c, :, :, n * self.size : (n + 1) * self.size]
+            yield 0, src, self.from_c.at[n], me.at_c, None, self.from_c.at[n], None
+        elif stage == "one":
+            a, b = self.from_1.at[n, 0], self.from_1.at[n, 1]
+            yield 1, acc.at[1 - y, :, :, :, self.left], a, me.at_y, None, a, None
+            yield 2, acc.at[:, 1 - x, :, :, self.right], b, me.at_x, None, b, None
+        elif stage == "two":
+            a, b = self.from_2.at[n, 0], self.from_2.at[n, 1]
+            yield 3, acc.at[y, 1 - x, :, :, self.left], a, me.at_x, None, a, None
+            yield 4, acc.at[1 - y, x, :, :, self.right], b, me.at_y, None, b, None
+        else:
+            for k in (3, 2, 1):
+                got = self.from_z.at[n, k - 1]
+                yield 4 + k, acc.at[y, x, (z + k) % 4], got, me.at_z(k), None, got, None
+
+    def act(self, n, stage, what):
+        run_moves(self.moves(n, stage), what, self.send.at[n], self.recv.at[n])
+
+    def keep(self, n):
+        src = self.g.at[:, :, self.me.c, :, :, n * self.size : (n + 1) * self.size]
+        return pltpu.make_async_copy(src, self.acc.at[n], self.local.at[n])
+
+    def start(self, n, stage):
+        if stage == "core":
+            self.keep(n).start()
+        self.act(n, stage, "start")
+
+    def done(self, n, stage):
+        me, acc = self.me, self.acc
+        y, x = me.y, me.x
+        f32 = lambda v: v.astype(F32)
+
+        def each(count, body):
+            lax.fori_loop(0, count, lambda q, carry: body(q) or carry, 0)
+
+        if stage == "core":
+            self.keep(n).wait()
+        self.act(n, stage, "arrived")
+        if stage == "core":
+
+            def add(q):
+                for a in range(2):
+                    for b in range(2):
+                        acc[n, a, b, q] = (f32(acc[n, a, b, q]) + f32(self.from_c[n, a, b, q])).astype(BF)
+
+            each(4, add)
+        elif stage == "one":
+
+            def add(q):
+                for b in range(2):
+                    at = (n, y, b, q, slice(None), self.left)
+                    acc[at] = (f32(acc[at]) + f32(self.from_1[n, 0, b, q])).astype(BF)
+                    at = (n, b, x, q, slice(None), self.right)
+                    acc[at] = (f32(acc[at]) + f32(self.from_1[n, 1, b, q])).astype(BF)
+
+            each(4, add)
+        elif stage == "two":
+
+            def add(q):
+                for half, cut in enumerate((self.left, self.right)):
+                    at = (n, y, x, q, slice(None), cut)
+                    acc[at] = (f32(acc[at]) + f32(self.from_2[n, half, q])).astype(BF)
+
+            each(4, add)
+        else:
+            total = f32(acc[n, y, x, me.z])
+            for k in range(3):
+                total += f32(self.from_z[n, k])
+            self.own[:, n * self.size : (n + 1) * self.size] = total
+
+    def finish(self, n):
+        for stage in ("core", "one", "two", "z"):
+            self.act(n, stage, "sent")
+
+
+REDUCE_STEPS = {
+    0: [("start", 0, "core"), ("start", 1, "core")],
+    1: [("done", 0, "core"), ("start", 0, "one")],
+    2: [("done", 1, "core")],
+    3: [("start", 1, "one")],
+    5: [("done", 0, "one"), ("start", 0, "two")],
+    7: [("done", 1, "one"), ("done", 0, "two"), ("start", 0, "z"), ("start", 1, "two")],
+    9: [("done", 1, "two"), ("start", 1, "z")],
+    12: [("done", 0, "z"), ("done", 1, "z")],
+}
+CHUNKS = 2
+
+
+def attend_bwd_kernel_hosting(q_ref, k_ref, v_ref, do_ref, lse_ref, d_ref, g_ref, rows_ref, dq_ref, dk_ref, dv_ref, own_ref, all_ref,
+                              acc, from_c, from_1, from_2, from_z, send, recv, local, rows_send, rows_recv, rows_local):
     h_at = pl.program_id(0)
     me = Place()
-    spread = Spread(me, rows_ref, all_ref, send, recv, local)
-
-    def first():
-        greet([me.at_z(1), me.at_z(2), me.at_z(3), me.at_x, me.at_y, me.at_c])
-        spread.begin(0)
-
-    pl.when(h_at == 0)(first)
-    for s in range(1, 6):
+    spread = Spread(me, rows_ref, all_ref, rows_send, rows_recv, rows_local)
+    reduce = Reduce(me, g_ref, own_ref, acc, from_c, from_1, from_2, from_z, send, recv, local)
+
+    def tick(step):
+        if step not in REDUCE_STEPS:
+            return
+
+        def go():
+            if step == 0:
+                greet([me.at_z(1), me.at_z(2), me.at_z(3), me.at_x, me.at_y, me.at_c])
+            for what, n, stage in REDUCE_STEPS[step]:
+                getattr(reduce, what)(n, stage)
+
+        pl.when(h_at == step // 2)(go)
+
+    for step in range(0, 12, 2):
+        tick(step)
+    for s in range(6):
         pl.when(h_at == s)(partial(spread.begin, s))
     q = q_ref[...] * 0.125
     k, v, do = k_ref[...], v_ref[...], do_ref[...]
     lane = lax.broadcasted_iota(jnp.int32, k.shape, 1)
-    dqs, dks, dvs = [], [], []
+    low = lane < 64
     for h in range(2):
-        keep = (lane < 64) if h == 0 else (lane >= 64)
+        if h == 1:
+            for step in range(1, 12, 2):
+                tick(step)
+        keep = low if h == 0 else ~low
         s = mm(jnp.where(keep, k, jnp.zeros_like(k)), q, 1, 1)
         p = jnp.exp(s - lse_ref[0, h : h + 1, :])
         dp = mm(jnp.where(keep, v, jnp.zeros_like(v)), do, 1, 1)
         ds = (p * (dp - d_ref[0, h : h + 1, :])).astype(BF)
-        dvs.append(mm(p.astype(BF), do))
-        dks.append(mm(ds, q))
-        dqs.append(mm(ds, k, 0, 0))
-    low = lane < 64
-    dq_ref[...] = (jnp.where(low, dqs[0], dqs[1]) * 0.125).astype(BF)
-    dk_ref[...] = jnp.where(low, dks[0], dks[1]).astype(BF)
-    dv_ref[...] = jnp.where(low, dvs[0], dvs[1]).astype(BF)
-    pl.when(h_at == 5)(spread.finish)
-
-
-def attend_bwd_and_spread(proj, d_out, lse, inner, rows, cid):
+        d_v = mm(p.astype(BF), do).astype(BF)
+        d_k = mm(ds, q).astype(BF)
+        d_q = (mm(ds, k, 0, 0) * 0.125).astype(BF)
+        for ref, value in ((dq_ref, d_q), (dk_ref, d_k), (dv_ref, d_v)):
+            ref[...] = value if h == 0 else jnp.where(low, ref[...], value)
+
+    def last():
+        for what, n, stage in REDUCE_STEPS[12]:
+            getattr(reduce, what)(n, stage)
+        for n in range(CHUNKS):
+            reduce.finish(n)
+        spread.finish()
+
+    pl.when(h_at == pl.num_programs(0) - 1)(last)
+
+
+def attend_bwd_and_reduce(proj, d_out, lse, inner, g, own_rows, cid):
     length, width = proj.shape[0], proj.shape[1] // 3
     pairs = width // 128
+    rows, n = g.shape[0] // 32, g.shape[1]
+    size = n // CHUNKS
     block = lambda part: pl.BlockSpec((length, 128), lambda h: (0, part * pairs + h))
     row = pl.BlockSpec((1, 2, length), lambda h: (h, 0, 0))
     hbm = pl.BlockSpec(memory_space=pl.ANY)
     result = jax.ShapeDtypeStruct((length, width), BF)
+    v = lambda *s: pltpu.VMEM(s, BF)
     return pl.pallas_call(
         attend_bwd_kernel_hosting,
         grid=(pairs,),
-        in_specs=[block(0), block(1), block(2), block(0), row, row, hbm],
-        out_specs=[block(0)] * 3 + [hbm],
-        out_shape=[result] * 3 + [jax.ShapeDtypeStruct((2, 2, 2, 4) + rows.shape, rows.dtype)],
-        scratch_shapes=[pltpu.SemaphoreType.DMA((11,)), pltpu.SemaphoreType.DMA((11,)), pltpu.SemaphoreType.DMA],
-        compiler_params=pltpu.CompilerParams(collective_id=cid, has_side_effects=True, vmem_limit_bytes=56 << 20),
-    )(proj, proj, proj, d_out, lse, inner, rows)
+        in_specs=[block(0), block(1), block(2), block(0), row, row, hbm, hbm],
+        out_specs=[block(0)] * 3 + [pl.BlockSpec((rows, n), lambda h: (0, 0)), hbm],
+        out_shape=[result] * 3
+        + [jax.ShapeDtypeStruct((rows, n), F32), jax.ShapeDtypeStruct((2, 2, 2, 4) + own_rows.shape, BF)],
+        scratch_shapes=[
+            v(CHUNKS, 2, 2, 4, rows, size), v(CHUNKS, 2, 2, 4, rows, size), v(CHUNKS, 2, 2, 4, rows, size // 2),
+            v(CHUNKS, 2, 4, rows, size // 2), v(CHUNKS, 3, rows, size),
+            pltpu.SemaphoreType.DMA((CHUNKS, 8)), pltpu.SemaphoreType.DMA((CHUNKS, 8)), pltpu.SemaphoreType.DMA((CHUNKS,)),
+            pltpu.SemaphoreType.DMA((11,)), pltpu.SemaphoreType.DMA((11,)), pltpu.SemaphoreType.DMA,
+        ],
+        compiler_params=pltpu.CompilerParams(collective_id=cid, has_side_effects=True, vmem_limit_bytes=60 << 20),
+    )(proj, proj, proj, d_out, lse, inner, g.reshape(2, 2, 2, 4, rows, n), own_rows)
 
 
 def attend_fwd_kernel_hosting(q_ref, k_ref, v_ref, split_ref, downs_ref, tokens_ref,
@@ -1248,17 +1377,17 @@
 
 def mlp_bwd_kernel(dy_ref, branch_ref, active_ref, slope_ref, second_ref, hidden_ref, mixed_ref,
                    wo_ref, wu_ref, wd_ref, vec_ref,
-                   g_ref, dhid_ref, dmix_ref, inner_ref, bias_ref, dvec_ref, total):
+                   g_ref, gs_ref, dhid_ref, dmix_ref, inner_ref, bias_ref, dvec_ref, total):
     k = pl.program_id(0)
     fold = pl.num_programs(0)
     width = mixed_ref.shape[1]
     branch = branch_ref[...]
     columns = lambda n: pl.ds(pl.multiple_of(n * width, width), width)
-    g_ref[:, columns(1 + fold + k)] = mm(active_ref[...], branch, 0, 0).astype(BF)
+    gs_ref[:, columns(1 + k)] = mm(active_ref[...], branch, 0, 0).astype(BF)
     d_upper_f = mm(branch, wd_ref[...], 1, 1) * slope_ref[...].astype(F32)
     bias_ref[0] = jnp.sum(d_upper_f, 0, keepdims=True)
     d_upper = d_upper_f.astype(BF)
-    g_ref[:, columns(1 + k)] = mm(second_ref[...], d_upper, 0, 0).astype(BF)
+    g_ref[:, columns(k)] = mm(second_ref[...], d_upper, 0, 0).astype(BF)
     back = mm(d_upper, wu_ref[...], 1, 1)
 
     @pl.when(k == 0)
@@ -1279,7 +1408,7 @@
         dhid_ref[...] = d_hidden
         d_attend = d_hidden.astype(BF)
         mixed = mixed_ref[...]
-        g_ref[:, 0:width] = mm(mixed, d_attend, 0, 0).astype(BF)
+        gs_ref[:, 0:width] = mm(mixed, d_attend, 0, 0).astype(BF)
         d_mixed = mm(d_attend, wo_ref[...], 1, 1).astype(BF)
         dmix_ref[...] = d_mixed
         head = lax.broadcasted_iota(jnp.int32, (16, width), 0)
@@ -1302,10 +1431,10 @@
         grid=(fold,),
         in_specs=[whole, whole, tile, tile, whole, whole, whole,
                   at(lambda k: 0), at(lambda k: 1 + k), at(lambda k: 1 + fold + k), pl.BlockSpec(vec.shape, lambda k: (0, 0))],
-        out_specs=[pl.BlockSpec((width, (1 + 2 * fold) * width), lambda k: (0, 0)), whole, whole,
+        out_specs=[pl.BlockSpec((width, fold * width), lambda k: (0, 0)), pl.BlockSpec((width, (1 + fold) * width), lambda k: (0, 0)), whole, whole,
                    pl.BlockSpec((HEADS // 2, 2, rows), lambda k: (0, 0, 0)),
                    pl.BlockSpec((1, 1, width), lambda k: (k, 0, 0)), pl.BlockSpec((8, width), lambda k: (0, 0))],
-        out_shape=[jax.ShapeDtypeStruct((width, (1 + 2 * fold) * width), BF), f(rows, width),
+        out_shape=[jax.ShapeDtypeStruct((width, fold * width), BF), jax.ShapeDtypeStruct((width, (1 + fold) * width), BF), f(rows, width),
                    jax.ShapeDtypeStruct((rows, width), BF), f(HEADS // 2, 2, rows), f(fold, 1, width), f(8, width)],
         scratch_shapes=[pltpu.VMEM((rows, width), F32)],
         compiler_params=pltpu.CompilerParams(vmem_limit_bytes=60 << 20),
@@ -1523,15 +1652,14 @@
     loss, grad_temp = loss_row[0, 0], loss_row[0, 1:3]
     grad_captions = d_captions.reshape(captions.shape)
 
-    g_main, d_hidden, d_mixed, inner, g_bias, dvec = mlp_bwd(
+    g_up, g_rest, d_hidden, d_mixed, inner, g_bias, dvec = mlp_bwd(
         dy, d_branch, active, slope, second, hidden, mixed, main, ivec, fold
     )
-    g_main = lax.psum_scatter(g_main, ALL, scatter_dimension=0, tiled=True).astype(F32)
-    own_out = g_main[:, :width]
-    own_up = g_main[:, width : width + hidden_width].reshape(part, fold, width)
-    own_up = own_up.transpose(0, 2, 1).reshape(part, hidden_width)
-    own_down = g_main[:, width + hidden_width :].reshape(wide_part, width)
-    d_q, d_k, d_v, rows = attend_bwd_and_spread(proj, d_mixed, lse, inner, rows, 4)
+    g_rest = lax.psum_scatter(g_rest, ALL, scatter_dimension=0, tiled=True).astype(F32)
+    own_out = g_rest[:, :width]
+    own_down = g_rest[:, width:].reshape(wide_part, width)
+    d_q, d_k, d_v, own_up, rows = attend_bwd_and_reduce(proj, d_mixed, lse, inner, g_up, rows, 4)
+    own_up = own_up.reshape(part, fold, width).transpose(0, 2, 1).reshape(part, hidden_width)
     rows = rows.reshape(world, ROWS, width).transpose(1, 0, 2)
     sums = jnp.concatenate([dvec[0:2], dvec[0:2], sums[4:], g_bias.reshape(fold, width)], 0)
     g_in, d_x = project_bwd(d_q, d_k, d_v, normed, w_in, x, d_hidden, sums, ivec)

time: 485 us -> 464 us (0.957)
  the two profiles are of different devices: /device:TPU:8 before, /device:TPU:0 now
where the time goes in v5:
time: 464 us; the launch traced here: 456 us
  Pallas kernels  379 us (82%)
  local copies, waits for them, and re-layouts  47 us (10%)
  between operations  15.3 us (3%)
  other arithmetic  8.64 us (2%)
  matrix products  5.48 us (1%)
    pallas_call x1, Pallas kernels, attend_fwd_and_gather(): pl.pallas_call(attend_fwd_kernel_hosting, grid=(pairs,), in_specs=[block(...  62 us
    pallas_call x1, Pallas kernels, gather(): pl.pallas_call(partial(gather_kernel, kinds, order), out_shape=shapes, in...  60.5 us
    pallas_call x1, Pallas kernels, middle(): pl.pallas_call(middle_kernel, in_specs=[v] * 11 + [pl.BlockSpec(memory_sp...  52.9 us
    pallas_call x1, Pallas kernels, attend_bwd_and_reduce(): pl.pallas_call(attend_bwd_kernel_hosting, grid=(pairs,), in_specs=[block(...  52.8 us
    pallas_call x1, Pallas kernels, reduce_and_move(): pl.pallas_call(reduce_kernel, in_specs=[hbm, hbm], out_specs=[pl.BlockSpe...  49.9 us
    pallas_call x1, Pallas kernels, mlp_fwd(): pl.pallas_call(mlp_fwd_kernel, grid=(fold,), in_specs=[whole, whole, at(l...  39.7 us
    pallas_call x1, Pallas kernels, mlp_bwd(): pl.pallas_call(mlp_bwd_kernel, grid=(fold,), in_specs=[whole, whole, tile...  39.4 us
    unnamed x88, local copies, waits for them, and re-layouts  19 us
  transfers between devices with their start and end apart: 2, of which 1 were waited for; matrix products, arithmetic and copies ran while one was open for 9% of the time, Pallas kernels for 54%

profile of v5, /device:TPU:0, one launch (start us, length us, event | category | flops | bytes accessed | tf_op | source)
XLA Modules:
  0.0 455.7 jit_solution(12363747109783963674)
XLA Ops:
  7.3 1.3 copy.72
  10.0 1.0 reshape.300
  12.8 60.5 %shard_map.398 = (bf16[2,2,2,4,24,2304]{5,4,3,2,1,0:T(8,128)(2,1)}, bf16[2,2,2,4,16,128]{5,4,3,2,1,0:T(8,128)(2,1)}, bf16[4,256,768]{2,1,0:T(8,128)(2,1)}) custom-call(bf16[24,2304]{1,0:T(8,128)(2,1)} %refs_0_.1, bf16[16,128]{1,0:T(8,128)(2,1)} %pad_bitcast_fusion.refs_1_, bf16[4,256,768]{2,1,0:T(8,128)(2,1)} %refs_2_.1), custom_call_target="tpu_custom_call" | custom-call | tf_op jit(solution)/shard_map/pallas_call | solution.py:611
  73.3 0.9 copy.114
  75.5 1.2 reshape.289
  82.6 5.5 %convolution_convert_fusion.q_ref.k_ref.v_ref = bf16[1024,2304]{1,0:T(8,128)(2,1)} fusion(bf16[1024,768]{1,0:T(8,128)(2,1)S(1)} %bitcast.130, bf16[768,2304]{1,0:T(8,128)(2,1)S(1)} %bitcast.128), kind=kOutput, calls=%fused_computation | convolution fusion | flops 3626237952 | bytes 9830400 | tf_op jit(solution)/shard_map/dot_general | solution.py:18
  88.1 62.0 %shard_map.399 = (bf16[1024,768]{1,0:T(8,128)(2,1)S(1)}, f32[6,2,1024]{2,1,0:T(2,128)S(1)}, bf16[2,2,2,4,24,3328]{5,4,3,2,1,0:T(8,128)(2,1)}, bf16[2,2,2,96,1536...) custom-call(bf16[1024,2304]{1,0:T(8,128)(2,1)} %convolution_convert_fusion.q_ref.k_ref.v_ref, ...), custom_call_target="tpu_custom_call" | custom-call | tf_op jit(solution)/shard_map/pallas_call | solution.py:1297
  150.2 1.4 copy-done.1
  151.5 1.2 copy-done.2
  154.0 1.7 slice-done
  155.7 39.7 %shard_map.400 = (f32[1024,768]{1,0:T(8,128)}, bf16[1024,768]{1,0:T(8,128)(2,1)}, bf16[1024,3072]{1,0:T(8,128)(2,1)}, bf16[1024,3072]{1,0:T(8,128)(2,1)}, f32[10...) custom-call(bf16[1024,768]{1,0:T(8,128)(2,1)} %bitcast.121, ...), custom_call_target="tpu_custom_call", output_to_operand_aliasing={{6}: (7, {}), {7}: (8, {})} | custom-call | tf_op jit(solution)/shard_map/pallas_call | solution.py:1364
  195.4 52.9 %shard_map.401 = (f32[1024,768]{1,0:T(8,128)}, bf16[1024,768]{1,0:T(8,128)(2,1)S(1)}, bf16[80,768]{1,0:T(8,128)(2,1)S(1)}, f32[24,768]{1,0:T(8,128)S(1)}, f32[64...) custom-call(bf16[1024,768]{1,0:T(8,128)(2,1)} %get-tuple-element.81.final_ref, ...), custom_call_target="tpu_custom_call" | custom-call | tf_op jit(solution)/shard_map/pallas_call | solution.py:963
  248.3 1.2 copy-done.5
  249.5 39.4 %shard_map.402 = (bf16[768,3072]{1,0:T(8,128)(2,1)}, bf16[768,3840]{1,0:T(8,128)(2,1)}, f32[1024,768]{1,0:T(8,128)}, bf16[1024,768]{1,0:T(8,128)(2,1)}, f32[6,2,...) custom-call(f32[1024,768]{1,0:T(8,128)} %get-tuple-element.87.dy_ref, bf16[1024,768]{1,0:T(8,128)(2,1)} %copy-done.5, ...), custom_call_target="tpu_custom_call" | custom-call | tf_op jit(solution)/shard_map/pallas_call | solution.py:1429
  289.2 1.1 copy-done.12
  290.3 1.8 add_convert_fusion.normed_ref
  292.1 52.8 %shard_map.403 = (bf16[1024,768]{1,0:T(8,128)(2,1)}, bf16[1024,768]{1,0:T(8,128)(2,1)}, bf16[1024,768]{1,0:T(8,128)(2,1)}, f32[24,3072]{1,0:T(8,128)}, bf16[2,2,2,4,80,768]{5,4,3,2,1,0:T(8,128)(2,1)}) custom-call(bf16[1024,2304]{1,0:T(8,128)(2,1)} %convolution_convert_fusion.q_ref.k_ref.v_ref, bf16[1024,2304]{1,0:T(8,128)(2,1)} %convolution_convert_fusion.q_ref.k_ref.v_ref, ...), custom_call_target="tpu_custom_call" | custom-call | tf_op jit(solution)/shard_map/pallas_call | solution.py:1225
  344.9 5.3 %copy.111 = bf16[32,80,768]{2,0,1:T(8,128)(2,1)} copy(bf16[32,80,768]{2,1,0:T(8,128)(2,1)} %bitcast.126) | data formatting | bytes 7864320 | tf_op jit(solution)/shard_map/reshape | solution.py:1663
  350.4 2.1 copy-done
  352.5 4.4 shard_map.406
  357.0 0.9 reshape.330
  358.3 1.1 reshape.329
  359.9 1.1 reshape.332
  362.5 0.8 broadcast_multiply_fusion.1
  364.8 17.2 %shard_map.404 = (bf16[768,2560]{1,0:T(8,128)(2,1)}, bf16[1024,768]{1,0:T(8,128)(2,1)}) custom-call(bf16[1024,768]{1,0:T(8,128)(2,1)} %get-tuple-element.98.dq_ref, bf16[1024,768]{1,0:T(8,128)(2,1)} %get-tuple-element.99.dk_ref, bf16[1024,768]{1,0:T(8,128)(2,1)} %get-tuple-element.100.dv_ref, bf16[1024,768]{1,0:T(8,128)(2,1)} %add_convert_fusion.normed_ref, ...), custom_call_target="tpu_custom_call" | custom-call | tf_op jit(solution)/shard_map/pallas_call | solution.py:1464
  382.0 2.1 copy-done.3
  384.1 1.4 copy-done.4
  385.5 49.9 %shard_map.405 = (f32[24,2560]{1,0:T(8,128)S(1)}, bf16[4,256,768]{2,1,0:T(8,128)(2,1)S(1)}) custom-call(bf16[2,2,2,4,24,2560]{5,4,3,2,1,0:T(8,128)(2,1)S(1)} %bitcast.112, bf16[4,256,768]{2,1,0:T(8,128)(2,1)S(1)} %bitcast.113), custom_call_target="tpu_custom_call" | custom-call | tf_op jit(solution)/shard_map/pallas_call | solution.py:694
  437.1 1.9 convert_element_type.66
  441.3 1.2 copy.87
  444.8 0.9 slice.150
  446.6 1.4 slice.148
  (186 shorter events, 23.1 us)
Async XLA Ops:
  7.2 3.9 copy-start.22
  7.2 3.9 copy-start.23
  7.2 4.7 %copy-start.27 = (bf16[11,24]{1,0:T(8,128)(2,1)S(1)}, bf16[11,24]{1,0:T(8,128)(2,1)}, u32[]{:S(2)}) copy-start(bf16[11,24]{1,0:T(8,128)(2,1)} %param.31) | copy-start | bytes 1588
  7.2 4.8 %copy-start.28 = (bf16[7,24]{1,0:T(8,128)(2,1)S(1)}, bf16[7,24]{1,0:T(8,128)(2,1)}, u32[]{:S(2)}) copy-start(bf16[7,24]{1,0:T(8,128)(2,1)} %param.43) | copy-start | bytes 1012
  7.2 4.9 %copy-start.29 = (bf16[96]{0:T(256)(128)(2,1)S(1)}, bf16[96]{0:T(256)(128)(2,1)}, u32[]{:S(2)}) copy-start(bf16[96]{0:T(256)(128)(2,1)} %param.29) | copy-start | bytes 580
  7.2 4.9 %copy-start.30 = (bf16[96]{0:T(256)(128)(2,1)S(1)}, bf16[96]{0:T(256)(128)(2,1)}, u32[]{:S(2)}) copy-start(bf16[96]{0:T(256)(128)(2,1)} %param.36) | copy-start | bytes 580
  7.3 4.9 %copy-start.31 = (bf16[96]{0:T(256)(128)(2,1)S(1)}, bf16[96]{0:T(256)(128)(2,1)}, u32[]{:S(2)}) copy-start(bf16[96]{0:T(256)(128)(2,1)} %param.41) | copy-start | bytes 580
  7.3 67.6 %copy-start.20 = (bf16[24,2304]{1,0:T(8,128)(2,1)S(1)}, bf16[24,2304]{1,0:T(8,128)(2,1)}, u32[]{:S(2)}) copy-start(bf16[24,2304]{1,0:T(8,128)(2,1)} %param.38) | copy-start | bytes 331780
  7.3 146.7 %all-gather.2.cloned.1.call-start = ((), (), s32[]{:S(2)}) async-start(), calls=%async_computation.1 | async-start | bytes 13381632 | tf_op jit(solution)/shard_map/all_gather | solution.py:1623
  8.7 66.4 %copy-start.17 = (bf16[24,3072]{1,0:T(8,128)(2,1)S(1)}, bf16[24,3072]{1,0:T(8,128)(2,1)}, u32[]{:S(2)}) copy-start(bf16[24,3072]{1,0:T(8,128)(2,1)} %param.35) | copy-start | bytes 442372
  11.1 66.1 %copy-start.24 = (bf16[24,768]{1,0:T(8,128)(2,1)S(1)}, bf16[24,768]{1,0:T(8,128)(2,1)}, u32[]{:S(2)}) copy-start(bf16[24,768]{1,0:T(8,128)(2,1)} %param.44) | copy-start | bytes 110596
  11.1 66.2 %copy-start.16 = (bf16[24,768]{1,0:T(8,128)(2,1)S(1)}, bf16[24,768]{1,0:T(8,128)(2,1)}, u32[]{:S(2)}) copy-start(bf16[24,768]{1,0:T(8,128)(2,1)} %param.32) | copy-start | bytes 110596
  11.9 65.6 %copy-start.21 = (bf16[24,1536]{1,0:T(8,128)(2,1)S(1)}, bf16[24,1536]{1,0:T(8,128)(2,1)}, u32[]{:S(2)}) copy-start(bf16[24,1536]{1,0:T(8,128)(2,1)} %param.33) | copy-start | bytes 221188
  11.9 432.9 %reduce-scatter.2.cloned.1.call-start = ((), (), s32[]{:S(2)}) async-start(), calls=%async_computation.2 | async-start | bytes 6082560 | tf_op jit(solution)/shard_map/reduce_scatter | solution.py:1658
  74.4 5.7 %copy-start.25 = (s32[32,32]{1,0:T(8,128)S(1)}, s32[32,32]{1,0:T(8,128)}, u32[]{:S(2)}) copy-start(s32[32,32]{1,0:T(8,128)} %param.25) | copy-start | bytes 12292
  75.4 5.1 %copy-start.11 = (bf16[4,256,768]{2,1,0:T(8,128)(2,1)S(1)}, bf16[4,256,768]{2,1,0:T(8,128)(2,1)}, u32[]{:S(2)}) copy-start(bf16[4,256,768]{2,1,0:T(8,128)(2,1)} %get-tuple-element.75) | copy-start | bytes 4718596
  78.7 2.8 copy-start.18
  78.8 2.8 copy-start.19
  80.6 2.0 copy-start.13
  82.6 5.5 %copy-start.8 = (bf16[4,16,768]{2,1,0:T(8,128)(2,1)S(1)}, bf16[4,16,768]{2,1,0:T(8,128)(2,1)}, u32[]{:S(2)}) copy-start(bf16[4,16,768]{2,1,0:T(8,128)(2,1)} %tokens_ref.1) | copy-start | bytes 294916
  150.1 1.4 copy-start.1
  151.5 1.2 copy-start.2
  154.0 1.7 slice-start
  155.7 39.7 %copy-start.6 = (f32[11,768]{1,0:T(8,128)S(1)}, f32[11,768]{1,0:T(8,128)}, u32[]{:S(2)}) copy-start(f32[11,768]{1,0:T(8,128)} %reshape.302.vec_ref.ivec_ref) | copy-start | bytes 101380
  155.7 39.7 %copy-start.10 = (f32[2]{0:T(128)S(1)}, f32[2]{0:T(128)}, u32[]{:S(2)}) copy-start(f32[2]{0:T(128)} %temp_ref.1) | copy-start | bytes 28
  249.5 39.4 %copy-start.7 = (bf16[80,768]{1,0:T(8,128)(2,1)}, bf16[80,768]{1,0:T(8,128)(2,1)S(1)}, u32[]{:S(2)}) copy-start(bf16[80,768]{1,0:T(8,128)(2,1)S(1)} %get-tuple-element.97.rows_ref) | copy-start | bytes 368644
  288.9 1.4 copy-start.12
  350.4 2.1 copy-start
  357.0 6.4 %copy-start.26 = (f32[4,1,768]{2,1,0:T(1,128)S(1)}, f32[4,1,768]{2,1,0:T(1,128)}, u32[]{:S(2)}) copy-start(f32[4,1,768]{2,1,0:T(1,128)} %get-tuple-element.104) | copy-start | bytes 36868
  382.0 2.2 copy-start.3
  384.1 1.4 copy-start.4
  435.5 4.9 %copy-start.15 = (f32[24,3072]{1,0:T(8,128)S(1)}, f32[24,3072]{1,0:T(8,128)}, u32[]{:S(2)}) copy-start(f32[24,3072]{1,0:T(8,128)} %get-tuple-element.111) | copy-start | bytes 884740
  (3 other events, 2.6 us)
Sparse Core Ops, SparseCore 0:
  12.0 141.9 all-gather.1
  289.0 124.6 reduce-scatter.1

commit v6 on v5

--- a/solution.py
+++ b/solution.py
@@ -622,100 +622,27 @@
     )(*ops)
 
 
-def reduce_kernel(g_ref, dx_ref, own_ref, moved_ref, from_c, acc_c, from_1, acc_1, from_2, acc_2, from_z, send, recv, local):
-    me = Place()
-    y, x, c, z = me.y, me.x, me.c, me.z
-    greet([me.at_z(1), me.at_z(2), me.at_z(3), me.at_x, me.at_y, me.at_c])
-    half = g_ref.shape[-1] // 2
-    started = []
-
-    def push(slot, src, dst, dev, arriving):
-        copy = pltpu.make_async_remote_copy(src, dst, send.at[slot], recv.at[slot], device_id=dev, device_id_type=MESH)
-        copy.start()
-        started.append(copy)
-        return pltpu.make_async_remote_copy(src, arriving, send.at[slot], recv.at[slot], device_id=dev, device_id_type=MESH)
-
-    a_c = push(0, g_ref.at[:, :, 1 - c], from_c, me.at_c, from_c)
-    home = pltpu.make_async_copy(g_ref.at[:, :, c], acc_c, local.at[0])
-    home.start()
-    rest = []
-    for k in (1, 2, 3):
-        to, fro = (z + k) % 4, (z + 4 - k) % 4
-        rest.append(push(k, dx_ref.at[to], moved_ref.at[z], me.at_z(k), moved_ref.at[fro]))
-    keep = pltpu.make_async_copy(dx_ref.at[z], moved_ref.at[z], local.at[1])
-    keep.start()
-    home.wait()
-    a_c.wait_recv()
-    f32 = lambda v: v.astype(jnp.float32)
-    for a in range(2):
-        for b in range(2):
-            for q in range(4):
-                acc_c[a, b, q] = (f32(acc_c[a, b, q]) + f32(from_c[a, b, q])).astype(acc_c.dtype)
-    left, right = slice(0, half), slice(half, 2 * half)
-    a_y = push(4, acc_c.at[1 - y, :, :, :, left], from_1.at[0], me.at_y, from_1.at[0])
-    a_x = push(5, acc_c.at[:, 1 - x, :, :, right], from_1.at[1], me.at_x, from_1.at[1])
-    a_y.wait_recv()
-    for b in range(2):
-        for q in range(4):
-            acc_1[0, b, q] = (f32(acc_c[y, b, q, :, left]) + f32(from_1[0, b, q])).astype(acc_1.dtype)
-    b_x = push(6, acc_1.at[0, 1 - x], from_2.at[0], me.at_x, from_2.at[0])
-    a_x.wait_recv()
-    for b in range(2):
-        for q in range(4):
-            acc_1[1, b, q] = (f32(acc_c[b, x, q, :, right]) + f32(from_1[1, b, q])).astype(acc_1.dtype)
-    b_y = push(7, acc_1.at[1, 1 - y], from_2.at[1], me.at_y, from_2.at[1])
-    b_x.wait_recv()
-    for q in range(4):
-        acc_2[q, :, left] = (f32(acc_1[0, x, q]) + f32(from_2[0, q])).astype(acc_2.dtype)
-    b_y.wait_recv()
-    for q in range(4):
-        acc_2[q, :, right] = (f32(acc_1[1, y, q]) + f32(from_2[1, q])).astype(acc_2.dtype)
-    last = []
-    for k in (1, 2, 3):
-        to, fro = (z + k) % 4, (z + 4 - k) % 4
-        last.append(push(7 + k, acc_2.at[to], from_z.at[k - 1], me.at_z(k), from_z.at[k - 1]))
-    total = f32(acc_2[z])
-    for k in (1, 2, 3):
-        last[k - 1].wait_recv()
-        total += f32(from_z[k - 1])
-    own_ref[...] = total
-    keep.wait()
-    for r in rest:
-        r.wait_recv()
-    for copy in started:
-        copy.wait_send()
-
-def reduce_and_move(g, dx, cid):
-    rows, n = g.shape[0] // 32, g.shape[1]
-    g = g.reshape(2, 2, 2, 4, rows, n)
-    dx = dx.reshape(4, dx.shape[0] // 4, dx.shape[1])
-    hbm = pl.BlockSpec(memory_space=pl.ANY)
-    v = lambda *s: pltpu.VMEM(s, g.dtype)
-    return pl.pallas_call(
-        reduce_kernel,
-        in_specs=[hbm, hbm],
-        out_specs=[pl.BlockSpec(memory_space=pltpu.VMEM), hbm],
-        out_shape=[jax.ShapeDtypeStruct((rows, n), jnp.float32), jax.ShapeDtypeStruct(dx.shape, dx.dtype)],
-        scratch_shapes=[
-            v(2, 2, 4, rows, n), v(2, 2, 4, rows, n), v(2, 2, 4, rows, n // 2), v(2, 2, 4, rows, n // 2),
-            v(2, 4, rows, n // 2), v(4, rows, n), v(3, rows, n),
-            pltpu.SemaphoreType.DMA((11,)), pltpu.SemaphoreType.DMA((11,)), pltpu.SemaphoreType.DMA((2,)),
-        ],
-        compiler_params=pltpu.CompilerParams(collective_id=cid, has_side_effects=True, vmem_limit_bytes=40 << 20),
-    )(g, dx)
-
 ROWS = 80
 
-def middle_kernel(final_ref, block_ref, tokens_ref, tp_ref, downs_ref, outs_ref, ivec_ref, tvec_ref, pbias_ref, tbias_ref,
+def middle_kernel(final_in, block_in, tokens_ref, tp_in, downs_in, outs_ref, ivec_ref, tvec_ref, pbias_ref, tbias_ref,
                   label_ref, temp_ref,
                   dy_ref, branch_ref, rows_ref, sums_ref, dcap_ref, loss_ref, dz_ref,
-                  tn_ref, dn_ref, send_a, recv_a, send_l, recv_l, send_t, recv_t, send_sem, recv_sem):
+                  tn_ref, dn_ref, send_a, recv_a, send_l, recv_l, send_t, recv_t,
+                  final_ref, block_ref, tp_ref, downs_ref, send_sem, recv_sem, fetch):
     me = Place()
+    cut = 2 * final_in.shape[1]
+    pairs = {
+        "small": (tp_in.at[:, cut:], tp_ref.at[:, cut:]), "final": (final_in, final_ref),
+        "up": (tp_in.at[:, 0:cut], tp_ref.at[:, 0:cut]), "down": (downs_in, downs_ref), "block": (block_in, block_ref),
+    }
+    loads = {name: pltpu.make_async_copy(*pair, fetch.at[n]) for n, (name, pair) in enumerate(pairs.items())}
+    for load in loads.values():
+        load.start()
     z, i = me.z, me.i
     n_dp = recv_l.shape[0]
     plane = [((i + k) % n_dp, z) for k in range(1, n_dp)]
     greet([me.at_z(1), me.at_z(2), me.at_z(3)] + plane)
-    width = final_ref.shape[1]
+    width = final_in.shape[1]
     part = width // 4
     started = []
 
@@ -767,6 +694,7 @@
         n = a.shape[0] // 3
         return sum(a[h * n:(h + 1) * n] * own[h] for h in range(3))
 
+    loads["small"].wait()
     p_q = mm(iv(7).astype(BF), small("pq"))
     get_keys = exchange(0, mm_two(spread(p_q), small("pk"), 1) * 0.125, 3)
     t_x = tokens_ref[...].astype(F32)
@@ -787,6 +715,7 @@
     t_used = mm_two(t_probs, tn)
     t_mixed = fold(mm(t_used.astype(BF), small("tv"))).astype(BF)
     get_t = exchange(1, mm(t_mixed[:, 0:part], t_out_w()), 4)
+    loads["final"].wait()
     final = final_ref[...]
     p_keys = jnp.concatenate(get_keys(), 0)
     p_scores = mm_two(p_keys, final, 1)
@@ -796,6 +725,8 @@
     get_p = exchange(2, [used[3 * q:3 * q + 3] for q in range(4)], 3)
     t_hidden = x_last + total(get_t())
     t_second = layer_norm(t_hidden, tv(2), tv(3)).astype(BF)
+    loads["up"].wait()
+    loads["down"].wait()
     t_value, t_slope = gelu_pair(mm(t_second, t_up()) + tbias_ref[...])
     t_active = t_value.astype(BF)
     get_t = exchange(3, mm(t_active, t_down()), 4)
@@ -916,6 +847,7 @@
         sums_ref[4:5] += jnp.sum(d_y, 0, keepdims=True)
         return carry
 
+    loads["block"].wait()
     lax.fori_loop(0, final_ref.shape[0] // tile, step, 0)
     w_got = by_head(get_p())
     dq_rows = fold(mm_two(w_got, small("pk")))
@@ -958,11 +890,11 @@
 
 def middle(final, block_out, tokens, tp, downs, outs, ivec, tvec, pbias, tbias, label, temp, cid, n_dp):
     length, width = final.shape
-    v = pl.BlockSpec(memory_space=pltpu.VMEM)
+    v, hbm = pl.BlockSpec(memory_space=pltpu.VMEM), pl.BlockSpec(memory_space=pl.ANY)
     f = lambda *s: jax.ShapeDtypeStruct(s, F32)
     return pl.pallas_call(
         middle_kernel,
-        in_specs=[v] * 11 + [pl.BlockSpec(memory_space=pltpu.SMEM)],
+        in_specs=[hbm, hbm, v, hbm, hbm] + [v] * 6 + [pl.BlockSpec(memory_space=pltpu.SMEM)],
         out_specs=[v] * 7,
         out_shape=[f(length, width), jax.ShapeDtypeStruct((length, width), BF), jax.ShapeDtypeStruct((ROWS, width), BF), f(24, width), f(64, width), f(8, 128), f(8 * n_dp, width)],
         scratch_shapes=[
@@ -970,7 +902,8 @@
             pltpu.VMEM((12, 4, 4, width), F32), pltpu.VMEM((12, 4, 4, width), F32),
             pltpu.VMEM((8, width), F32), pltpu.VMEM((n_dp, 8, width), F32),
             pltpu.VMEM((length, 128), F32), pltpu.VMEM((4, 64, width), BF),
-            pltpu.SemaphoreType.DMA((16, 8)), pltpu.SemaphoreType.DMA((16, 8)),
+            pltpu.VMEM((length, width), BF), pltpu.VMEM((length, width), F32), pltpu.VMEM(tp.shape, BF), pltpu.VMEM(downs.shape, BF),
+            pltpu.SemaphoreType.DMA((16, 8)), pltpu.SemaphoreType.DMA((16, 8)), pltpu.SemaphoreType.DMA((5,)),
         ],
         compiler_params=pltpu.CompilerParams(collective_id=cid, has_side_effects=True, vmem_limit_bytes=50 << 20),
     )(final, block_out, tokens, tp, downs, outs, ivec, tvec, pbias, tbias, label, temp)
@@ -1254,7 +1187,9 @@
         "split": (lambda: turn_moves(me, split_ref, home, True), 0),
         "tokens": (lambda: turn_moves(me, tokens_ref, token_ref, False), 2),
         "split_xy": (lambda: plane_moves(me, tp_ref, 3), 0),
-        "down_xy": (lambda: plane_moves(me, down_ref, 3), 1),
+        "down_one": (lambda: plane_moves(me, down_ref, 3), 1),
+        "down_two": (lambda: plane_moves(me, down_ref, 4), 1),
+        "down_core": (lambda: plane_moves(me, down_ref, 5), 1),
     }
 
     def act(name, what):
@@ -1262,12 +1197,16 @@
         run_moves(moves(), what, send.at[a], recv.at[a])
 
     def first():
-        greet([me.at_z(1), me.at_z(2), me.at_z(3), me.at_x, me.at_y])
+        greet([me.at_z(1), me.at_z(2), me.at_z(3), me.at_x, me.at_y, me.at_c])
         for keep in keeps:
             keep.start()
         act("split", "start")
         keeps[1].wait()
-        act("down_xy", "start")
+        act("down_one", "start")
+
+    def second_step():
+        act("down_one", "arrived")
+        act("down_two", "start")
 
     def middle_step():
         act("split", "arrived")
@@ -1275,15 +1214,21 @@
         act("split_xy", "start")
         act("tokens", "start")
 
+    def fifth_step():
+        act("down_two", "arrived")
+        act("down_core", "start")
+
     def last():
-        for name in ("split_xy", "down_xy", "tokens"):
+        for name in ("split_xy", "down_core", "tokens"):
             act(name, "arrived")
         keeps[2].wait()
         for name in groups:
             act(name, "sent")
 
     pl.when(h_at == 0)(first)
+    pl.when(h_at == 2)(second_step)
     pl.when(h_at == 3)(middle_step)
+    pl.when(h_at == 5)(fifth_step)
     attend_fwd_kernel(q_ref, k_ref, v_ref, o_ref, lse_ref)
     pl.when(h_at == pl.num_programs(0) - 1)(last)
 
@@ -1311,14 +1256,13 @@
     )(proj, proj, proj, split, downs, tokens)
 
 
-def mlp_fwd_kernel(x_ref, mixed_ref, wo_ref, wu_ref, wd_ref, bias_ref, vec_ref, tp_in, down_in,
-                   hidden_ref, second_ref, active_ref, slope_ref, block_ref, final_ref, tp_ref, down_ref, total, send, recv):
+def mlp_fwd_kernel(x_ref, mixed_ref, wo_ref, wu_ref, wd_ref, bias_ref, vec_ref, tp_in,
+                   hidden_ref, second_ref, active_ref, slope_ref, block_ref, final_ref, tp_ref, total, send, recv):
     k = pl.program_id(0)
     me = Place()
 
     def act(s, what):
-        for a, ref in enumerate((tp_ref, down_ref)):
-            run_moves(plane_moves(me, ref, s), what, send.at[a], recv.at[a])
+        run_moves(plane_moves(me, tp_ref, s), what, send, recv)
 
     def first():
         greet([me.at_x, me.at_y, me.at_c])
@@ -1354,7 +1298,7 @@
         act(5, "sent")
 
 
-def mlp_fwd(x, mixed, main, bias, vec, fold, tp, downs, cid):
+def mlp_fwd(x, mixed, main, bias, vec, fold, tp, cid):
     rows, width = mixed.shape
     whole = pl.BlockSpec((rows, width), lambda k: (0, 0))
     tile = pl.BlockSpec((rows, width), lambda k: (0, k))
@@ -1365,29 +1309,44 @@
         mlp_fwd_kernel,
         grid=(fold,),
         in_specs=[whole, whole, at(lambda k: 0), at(lambda k: 1 + k), at(lambda k: 1 + fold + k),
-                  pl.BlockSpec((1, 1, width), lambda k: (k, 0, 0)), pl.BlockSpec(vec.shape, lambda k: (0, 0)), hbm, hbm],
-        out_specs=[whole, whole, tile, tile, whole, whole, hbm, hbm],
+                  pl.BlockSpec((1, 1, width), lambda k: (k, 0, 0)), pl.BlockSpec(vec.shape, lambda k: (0, 0)), hbm],
+        out_specs=[whole, whole, tile, tile, whole, whole, hbm],
         out_shape=[s(1, F32), s(1, BF), s(fold, BF), s(fold, BF), s(1, F32), s(1, BF),
-                   jax.ShapeDtypeStruct(tp.shape, BF), jax.ShapeDtypeStruct(downs.shape, BF)],
-        scratch_shapes=[pltpu.VMEM((rows, width), F32), pltpu.SemaphoreType.DMA((2, 11)), pltpu.SemaphoreType.DMA((2, 11))],
-        input_output_aliases={7: 6, 8: 7},
+                   jax.ShapeDtypeStruct(tp.shape, BF)],
+        scratch_shapes=[pltpu.VMEM((rows, width), F32), pltpu.SemaphoreType.DMA((11,)), pltpu.SemaphoreType.DMA((11,))],
+        input_output_aliases={7: 6},
         compiler_params=pltpu.CompilerParams(collective_id=cid, has_side_effects=True, vmem_limit_bytes=56 << 20),
-    )(x, mixed, main, main, main, bias.reshape(fold, 1, width), vec, tp, downs)
+    )(x, mixed, main, main, main, bias.reshape(fold, 1, width), vec, tp)
 
 
 def mlp_bwd_kernel(dy_ref, branch_ref, active_ref, slope_ref, second_ref, hidden_ref, mixed_ref,
                    wo_ref, wu_ref, wd_ref, vec_ref,
-                   g_ref, gs_ref, dhid_ref, dmix_ref, inner_ref, bias_ref, dvec_ref, total):
+                   g_ref, gs_ref, dhid_ref, dmix_ref, inner_ref, bias_ref, dvec_ref, total, dy_in, hid_in, mix_in, slots, fetch, leave):
     k = pl.program_id(0)
     fold = pl.num_programs(0)
+    pairs = ((dy_ref, dy_in), (hidden_ref, hid_in), (mixed_ref, mix_in))
+    loads = [pltpu.make_async_copy(src, dst, fetch.at[n]) for n, (src, dst) in enumerate(pairs)]
+
+    @pl.when(k == 0)
+    def _():
+        for load in loads:
+            load.start()
+
     width = mixed_ref.shape[1]
+
+    def leaves(n):
+        at = pl.ds(pl.multiple_of((n + 1) * width, width), width)
+        return pltpu.make_async_copy(slots.at[n % 2], gs_ref.at[:, at], leave.at[n % 2])
+
+    pl.when(k >= 2)(lambda: leaves(k - 2).wait())
     branch = branch_ref[...]
     columns = lambda n: pl.ds(pl.multiple_of(n * width, width), width)
-    gs_ref[:, columns(1 + k)] = mm(active_ref[...], branch, 0, 0).astype(BF)
+    slots[k % 2] = mm(active_ref[...], branch, 0, 0).astype(BF)
+    leaves(k).start()
     d_upper_f = mm(branch, wd_ref[...], 1, 1) * slope_ref[...].astype(F32)
     bias_ref[0] = jnp.sum(d_upper_f, 0, keepdims=True)
     d_upper = d_upper_f.astype(BF)
-    g_ref[:, columns(k)] = mm(second_ref[...], d_upper, 0, 0).astype(BF)
+    g_ref[...] = mm(second_ref[...], d_upper, 0, 0).astype(BF)
     back = mm(d_upper, wu_ref[...], 1, 1)
 
     @pl.when(k == 0)
@@ -1401,14 +1360,19 @@
     @pl.when(k == fold - 1)
     def _():
         vec = vec_ref[...]
-        d_hidden, gain, shift = norm_back_rows(hidden_ref[...], vec[2:3], total[...])
+        for load in loads:
+            load.wait()
+        d_hidden, gain, shift = norm_back_rows(hid_in[...], vec[2:3], total[...])
         dvec_ref[0:1] = gain
         dvec_ref[1:2] = shift
-        d_hidden = dy_ref[...] + d_hidden
+        d_hidden = dy_in[...] + d_hidden
         dhid_ref[...] = d_hidden
         d_attend = d_hidden.astype(BF)
-        mixed = mixed_ref[...]
-        gs_ref[:, 0:width] = mm(mixed, d_attend, 0, 0).astype(BF)
+        mixed = mix_in[...]
+        leaves(fold - 2).wait()
+        slots[fold % 2] = mm(mixed, d_attend, 0, 0).astype(BF)
+        out = pltpu.make_async_copy(slots.at[fold % 2], gs_ref.at[:, 0:width], leave.at[2])
+        out.start()
         d_mixed = mm(d_attend, wo_ref[...], 1, 1).astype(BF)
         dmix_ref[...] = d_mixed
         head = lax.broadcasted_iota(jnp.int32, (16, width), 0)
@@ -1418,6 +1382,8 @@
         sums = mm(own, high, 1, 1) + mm(own, low, 1, 1)
         for h in range(HEADS // 2):
             inner_ref[h] = sums[2 * h : 2 * h + 2]
+        leaves(fold - 1).wait()
+        out.wait()
 
 
 def mlp_bwd(dy, branch, active, slope, second, hidden, mixed, main, vec, fold):
@@ -1426,47 +1392,167 @@
     tile = pl.BlockSpec((rows, width), lambda k: (0, k))
     at = lambda f: pl.BlockSpec((width, width), lambda k: (0, f(k)))
     f = lambda *s: jax.ShapeDtypeStruct(s, F32)
+    hbm = pl.BlockSpec(memory_space=pl.ANY)
     return pl.pallas_call(
         mlp_bwd_kernel,
         grid=(fold,),
-        in_specs=[whole, whole, tile, tile, whole, whole, whole,
+        in_specs=[hbm, whole, tile, tile, whole, hbm, hbm,
                   at(lambda k: 0), at(lambda k: 1 + k), at(lambda k: 1 + fold + k), pl.BlockSpec(vec.shape, lambda k: (0, 0))],
-        out_specs=[pl.BlockSpec((width, fold * width), lambda k: (0, 0)), pl.BlockSpec((width, (1 + fold) * width), lambda k: (0, 0)), whole, whole,
+        out_specs=[at(lambda k: k), hbm, whole, whole,
                    pl.BlockSpec((HEADS // 2, 2, rows), lambda k: (0, 0, 0)),
                    pl.BlockSpec((1, 1, width), lambda k: (k, 0, 0)), pl.BlockSpec((8, width), lambda k: (0, 0))],
         out_shape=[jax.ShapeDtypeStruct((width, fold * width), BF), jax.ShapeDtypeStruct((width, (1 + fold) * width), BF), f(rows, width),
                    jax.ShapeDtypeStruct((rows, width), BF), f(HEADS // 2, 2, rows), f(fold, 1, width), f(8, width)],
-        scratch_shapes=[pltpu.VMEM((rows, width), F32)],
+        scratch_shapes=[pltpu.VMEM((rows, width), F32), pltpu.VMEM((rows, width), F32), pltpu.VMEM((rows, width), F32),
+                        pltpu.VMEM((rows, width), BF), pltpu.VMEM((2, width, width), BF),
+                        pltpu.SemaphoreType.DMA((3,)), pltpu.SemaphoreType.DMA((3,))],
         compiler_params=pltpu.CompilerParams(vmem_limit_bytes=60 << 20),
     )(dy, branch, active, slope, second, hidden, mixed, main, main, main, vec)
 
 
-def project_bwd_kernel(dq_ref, dk_ref, dv_ref, normed_ref, w_ref, x_ref, dhid_ref, sums_ref, vec_ref, g_ref, dx_ref):
+def finish_kernel(dq_ref, dk_ref, dv_ref, normed_ref, w_ref, x_ref, dhid_ref, sums_ref, vec_ref, own_ref, moved_ref,
+                  g, dx, from_c, acc_c, from_1, from_2, from_z, q_in, k_in, v_in, n_in, w_in, x_in, h_in,
+                  send, recv, local, fetch):
+    me = Place()
+    pairs = ((dq_ref, q_in), (normed_ref, n_in), (dk_ref, k_in), (dv_ref, v_in), (w_ref, w_in), (x_ref, x_in), (dhid_ref, h_in))
+    loads = [pltpu.make_async_copy(src, dst, fetch.at[n]) for n, (src, dst) in enumerate(pairs)]
+    for load in loads:
+        load.start()
+    dq_ref, dk_ref, dv_ref, normed_ref, w_ref, x_ref, dhid_ref = q_in, k_in, v_in, n_in, w_in, x_in, h_in
+    y, x, c, z = me.y, me.x, me.c, me.z
     width = dq_ref.shape[1]
-    normed = normed_ref[...]
-    back = None
-    for n, ref in enumerate((dq_ref, dk_ref, dv_ref)):
-        d = ref[...]
-        g_ref[:, n * width : (n + 1) * width] = mm(normed, d, 0, 0).astype(BF)
-        part = mm(d, w_ref[:, n * width : (n + 1) * width], 1, 1)
-        back = part if back is None else back + part
-    d_x, gain, shift = norm_back_rows(x_ref[...].astype(F32), vec_ref[0:1], back)
-    dx_ref[...] = (dhid_ref[...] + d_x).astype(BF)
-    sums = jnp.concatenate([gain, shift, sums_ref[2:, :]], 0)
+    part = g.shape[4]
+    tile = dx.shape[1]
+    half = g.shape[-1] // 2
+    left, right = slice(0, half), slice(half, 2 * half)
+    f32 = lambda v: v.astype(F32)
+    started = []
+    greet([me.at_z(1), me.at_z(2), me.at_z(3), me.at_x, me.at_y, me.at_c])
+
+    def push(slot, src, dst, dev, arriving):
+        copy = pltpu.make_async_remote_copy(src, dst, send.at[slot], recv.at[slot], device_id=dev, device_id_type=MESH)
+        copy.start()
+        started.append(copy)
+        return pltpu.make_async_remote_copy(src, arriving, send.at[slot], recv.at[slot], device_id=dev, device_id_type=MESH)
+
+    def put(value, first):
+        for p in range(32):
+            i, q = p // 4, p % 4
+            g[i // 4, (i // 2) % 2, i % 2, q, :, first : first + value.shape[1]] = value[part * p : part * (p + 1)].astype(BF)
+
+    gain, shift, moves = [], [], []
+
+    def d_x_rows(k):
+        to, fro = (z + k) % 4, (z + 4 - k) % 4
+        at = pl.ds(pl.multiple_of(to * tile, tile), tile)
+        back = None
+        for n, ref in enumerate((dq_ref, dk_ref, dv_ref)):
+            term = mm(ref[at, :], w_ref[:, n * width : (n + 1) * width], 1, 1)
+            back = term if back is None else back + term
+        d_x, a, b = norm_back_rows(x_ref[at, :].astype(F32), vec_ref[0:1], back)
+        gain.append(a)
+        shift.append(b)
+        dx[to] = (dhid_ref[at, :] + d_x).astype(BF)
+        if k:
+            moves.append(push(k, dx.at[to], moved_ref.at[z], me.at_z(k), moved_ref.at[fro]))
+        else:
+            keep.start()
+
+    keep = pltpu.make_async_copy(dx.at[z], moved_ref.at[z], local)
+
+    def add(at, value):
+        acc_c[at] = (f32(acc_c[at]) + f32(value)).astype(BF)
+
+    def core(cut, slot):
+        to = from_c.at[:, :, :, :, cut]
+        return push(slot, g.at[:, :, 1 - c, :, :, cut], to, me.at_c, to)
+
+    def core_done(arrive, cut):
+        arrive.wait_recv()
+        for a in range(2):
+            for b in range(2):
+                for q in range(4):
+                    at = (a, b, q, slice(None), cut)
+                    acc_c[at] = (f32(g[a, b, c, q, :, cut]) + f32(from_c[at])).astype(BF)
+
+    def one_done(arrive, n, cut):
+        arrive.wait_recv()
+        for b in range(2):
+            for q in range(4):
+                add((b, x, q, slice(None), cut) if n else (y, b, q, slice(None), cut), from_1[n, b, q])
+
+    def two_done(arrive, n, cut):
+        arrive.wait_recv()
+        for q in range(4):
+            add((y, x, q, slice(None), cut), from_2[n, q])
+
+    def along(cut, slot):
+        arrives = []
+        for k in (3, 2, 1):
+            got = from_z.at[k - 1, :, cut]
+            arrives.append(push(slot + k, acc_c.at[y, x, (z + k) % 4, :, cut], got, me.at_z(k), got))
+        return arrives
+
+    part_of = lambda n, ref: put(mm(normed_ref[...], ref[...], 0, 0), n * width)
+    loads[0].wait()
+    loads[1].wait()
+    part_of(0, dq_ref)
+    loads[2].wait()
+    part_of(1, dk_ref)
+    for load in loads[3:]:
+        load.wait()
+    core_left = core(left, 0)
+    d_x_rows(2)
+    part_of(2, dv_ref)
+    core_done(core_left, left)
+    one_left = push(4, acc_c.at[1 - y, :, :, :, left], from_1.at[0], me.at_y, from_1.at[0])
+    d_x_rows(3)
+    d_x_rows(1)
+    d_x_rows(0)
+    sums = jnp.concatenate([sum(gain), sum(shift), sums_ref[2:, :]], 0)
     sums = jnp.concatenate([sums, jnp.zeros((128 - sums.shape[0], width), F32)], 0)
-    g_ref[:, 3 * width : 3 * width + 128] = jnp.transpose(sums).astype(BF)
-    g_ref[:, 3 * width + 128 : 3 * width + 256] = jnp.zeros((width, 128), BF)
-
-
-def project_bwd(dq, dk, dv, normed, w_in, x, d_hidden, sums, vec):
+    put(jnp.transpose(sums), 3 * width)
+    put(jnp.zeros((width, 128), F32), 3 * width + 128)
+    core_right = core(right, 8)
+    one_done(one_left, 0, left)
+    two_left = push(6, acc_c.at[y, 1 - x, :, :, left], from_2.at[0], me.at_x, from_2.at[0])
+    core_done(core_right, right)
+    one_right = push(5, acc_c.at[:, 1 - x, :, :, right], from_1.at[1], me.at_x, from_1.at[1])
+    two_done(two_left, 0, left)
+    z_left = along(left, 8)
+    one_done(one_right, 1, right)
+    two_right = push(7, acc_c.at[1 - y, x, :, :, right], from_2.at[1], me.at_y, from_2.at[1])
+    two_done(two_right, 1, right)
+    z_right = along(right, 11)
+    for arrive in z_left + z_right:
+        arrive.wait_recv()
+    total = f32(acc_c[y, x, z]) + f32(from_z[0]) + f32(from_z[1]) + f32(from_z[2])
+    own_ref[...] = total
+    keep.wait()
+    for arrive in moves:
+        arrive.wait_recv()
+    for copy in started:
+        copy.wait_send()
+
+
+def finish_image(dq, dk, dv, normed, w_in, x, d_hidden, sums, vec, cid):
     rows, width = dq.shape
-    v = pl.BlockSpec(memory_space=pltpu.VMEM)
+    part, n = width // 32, 3 * width + 256
+    v, hbm = pl.BlockSpec(memory_space=pltpu.VMEM), pl.BlockSpec(memory_space=pl.ANY)
+    s = lambda *shape: pltpu.VMEM(shape, BF)
     return pl.pallas_call(
-        project_bwd_kernel,
-        in_specs=[v] * 9,
-        out_specs=[v] * 2,
-        out_shape=[jax.ShapeDtypeStruct((width, 3 * width + 256), BF), jax.ShapeDtypeStruct((rows, width), BF)],
-        compiler_params=pltpu.CompilerParams(vmem_limit_bytes=56 << 20),
+        finish_kernel,
+        in_specs=[hbm] * 7 + [v] * 2,
+        out_specs=[v, hbm],
+        out_shape=[jax.ShapeDtypeStruct((part, n), F32), jax.ShapeDtypeStruct((4, rows // 4, width), BF)],
+        scratch_shapes=[
+            s(2, 2, 2, 4, part, n), s(4, rows // 4, width), s(2, 2, 4, part, n), s(2, 2, 4, part, n),
+            s(2, 2, 4, part, n // 2), s(2, 4, part, n // 2), s(3, part, n),
+            s(rows, width), s(rows, width), s(rows, width), s(rows, width), s(width, 3 * width), s(rows, width),
+            pltpu.VMEM((rows, width), F32),
+            pltpu.SemaphoreType.DMA((15,)), pltpu.SemaphoreType.DMA((15,)), pltpu.SemaphoreType.DMA, pltpu.SemaphoreType.DMA((7,)),
+        ],
+        compiler_params=pltpu.CompilerParams(collective_id=cid, has_side_effects=True, vmem_limit_bytes=56 << 20),
     )(dq, dk, dv, normed, w_in, x, d_hidden, sums, vec)
 
 
@@ -1639,9 +1725,7 @@
     normed = layer_norm(x.astype(F32), ivec[0], ivec[1]).astype(BF)
     proj = mm(normed, w_in).astype(BF)
     mixed, lse, tp, downs, tokens = attend_fwd_and_gather(proj, split, downs, captions, 5)
-    hidden, second, active, slope, block_out, final, tp, downs = mlp_fwd(
-        x, mixed, main, i_bias, ivec, fold, tp, downs, 6
-    )
+    hidden, second, active, slope, block_out, final, tp = mlp_fwd(x, mixed, main, i_bias, ivec, fold, tp, 6)
     tp, downs = tp.reshape(width, -1), downs.reshape(width, -1)
 
     labels = (2 * pairs - 1).astype(F32).reshape(n_dp, n_z, n_dp, n_z)
@@ -1662,8 +1746,7 @@
     own_up = own_up.reshape(part, fold, width).transpose(0, 2, 1).reshape(part, hidden_width)
     rows = rows.reshape(world, ROWS, width).transpose(1, 0, 2)
     sums = jnp.concatenate([dvec[0:2], dvec[0:2], sums[4:], g_bias.reshape(fold, width)], 0)
-    g_in, d_x = project_bwd(d_q, d_k, d_v, normed, w_in, x, d_hidden, sums, ivec)
-    own_in, moved = reduce_and_move(g_in, d_x, 3)
+    own_in, moved = finish_image(d_q, d_k, d_v, normed, w_in, x, d_hidden, sums, ivec, 3)
     grad_patches = moved.astype(F32)
     own_sums = own_in[:, 3 * width : 3 * width + 128].T
     own_in = own_in[:, : 3 * width]

time: 464 us -> 445 us (0.959)
  Pallas kernels: 379 us -> 361 us
    pallas_call x4 -> x3, Pallas kernels: 159 us -> 148 us  [the longest x1 64.5 us: finish_image(): pl.pallas_call(finish_kernel, in_specs=[hbm] * 7 + [v] * 2, out_specs=[v,...]
    pallas_call x1, Pallas kernels: 39.7 us -> 32.1 us  [mlp_fwd(): pl.pallas_call(mlp_fwd_kernel, grid=(fold,), in_specs=[whole, whole, at(l...]
  transfers between devices with their start and end apart: 2 -> 2, of which waited for: 1 -> 1; matrix products, arithmetic and copies ran while one was open for 9% -> 9% of each run, Pallas kernels for 54% -> 56%
where the time goes in v6:
time: 445 us; the launch traced here: 437 us
  Pallas kernels  361 us (81%)
  local copies, waits for them, and re-layouts  44.6 us (10%)
  between operations  15.3 us (3%)
  other arithmetic  10.1 us (2%)
  matrix products  5.41 us (1%)
    pallas_call x1, Pallas kernels, finish_image(): pl.pallas_call(finish_kernel, in_specs=[hbm] * 7 + [v] * 2, out_specs=[v,...  64.5 us
    pallas_call x1, Pallas kernels, attend_fwd_and_gather(): pl.pallas_call(attend_fwd_kernel_hosting, grid=(pairs,), in_specs=[block(...  63.1 us
    pallas_call x1, Pallas kernels, gather(): pl.pallas_call(partial(gather_kernel, kinds, order), out_shape=shapes, in...  60.5 us
    pallas_call x1, Pallas kernels, attend_bwd_and_reduce(): pl.pallas_call(attend_bwd_kernel_hosting, grid=(pairs,), in_specs=[block(...  52.8 us
    pallas_call x1, Pallas kernels, middle(): pl.pallas_call(middle_kernel, in_specs=[hbm, hbm, v, hbm, hbm] + [v] * 6...  48.6 us
    pallas_call x1, Pallas kernels, mlp_bwd(): pl.pallas_call(mlp_bwd_kernel, grid=(fold,), in_specs=[hbm, whole, tile,...  34.8 us
    pallas_call x1, Pallas kernels, mlp_fwd(): pl.pallas_call(mlp_fwd_kernel, grid=(fold,), in_specs=[whole, whole, at(l...  32.1 us
    unnamed x88, local copies, waits for them, and re-layouts  16.1 us
  transfers between devices with their start and end apart: 2, of which 1 were waited for; matrix products, arithmetic and copies ran while one was open for 9% of the time, Pallas kernels for 56%

profile of v6, /device:TPU:0, one launch (start us, length us, event | category | flops | bytes accessed | tf_op | source)
XLA Modules:
  0.0 437.0 jit_solution(14058329552353197545)
XLA Ops:
  7.3 1.3 copy.71
  9.2 0.8 constant_dynamic-update-slice_fusion.6
  10.0 1.0 reshape.294
  12.9 60.5 %shard_map.398 = (bf16[2,2,2,4,24,2304]{5,4,3,2,1,0:T(8,128)(2,1)}, bf16[2,2,2,4,16,128]{5,4,3,2,1,0:T(8,128)(2,1)}, bf16[4,256,768]{2,1,0:T(8,128)(2,1)}) custom-call(bf16[24,2304]{1,0:T(8,128)(2,1)} %refs_0_.1, bf16[16,128]{1,0:T(8,128)(2,1)} %pad_bitcast_fusion.refs_1_, bf16[4,256,768]{2,1,0:T(8,128)(2,1)} %refs_2_.1), custom_call_target="tpu_custom_call" | custom-call | tf_op jit(solution)/shard_map/pallas_call | solution.py:611
  73.4 0.9 copy.113
  81.6 5.4 %convolution_convert_fusion.q_ref.k_ref.v_ref = bf16[1024,2304]{1,0:T(8,128)(2,1)} fusion(bf16[1024,768]{1,0:T(8,128)(2,1)S(1)} %bitcast.126, bf16[768,2304]{1,0:T(8,128)(2,1)S(1)} %bitcast.124), kind=kOutput, calls=%fused_computation | convolution fusion | flops 3626237952 | bytes 9830400 | tf_op jit(solution)/shard_map/dot_general | solution.py:18
  87.0 63.1 %shard_map.399 = (bf16[1024,768]{1,0:T(8,128)(2,1)S(1)}, f32[6,2,1024]{2,1,0:T(2,128)S(1)}, bf16[2,2,2,4,24,3328]{5,4,3,2,1,0:T(8,128)(2,1)}, bf16[2,2,2,96,1536...) custom-call(bf16[1024,2304]{1,0:T(8,128)(2,1)} %convolution_convert_fusion.q_ref.k_ref.v_ref, ...), custom_call_target="tpu_custom_call" | custom-call | tf_op jit(solution)/shard_map/pallas_call | solution.py:1242
  150.2 1.2 copy-done.1
  151.3 1.4 copy-done.2
  154.1 1.7 slice-done
  155.8 32.1 %shard_map.400 = (f32[1024,768]{1,0:T(8,128)}, bf16[1024,768]{1,0:T(8,128)(2,1)}, bf16[1024,3072]{1,0:T(8,128)(2,1)}, bf16[1024,3072]{1,0:T(8,128)(2,1)}, f32[10...) custom-call(bf16[1024,768]{1,0:T(8,128)(2,1)} %bitcast.117, ...), custom_call_target="tpu_custom_call", output_to_operand_aliasing={{6}: (7, {})} | custom-call | tf_op jit(solution)/shard_map/pallas_call | solution.py:1308
  187.9 48.6 %shard_map.401 = (f32[1024,768]{1,0:T(8,128)}, bf16[1024,768]{1,0:T(8,128)(2,1)S(1)}, bf16[80,768]{1,0:T(8,128)(2,1)S(1)}, f32[24,768]{1,0:T(8,128)S(1)}, f32[64...) custom-call(bf16[1024,768]{1,0:T(8,128)(2,1)} %get-tuple-element.77.final_in, ...), custom_call_target="tpu_custom_call" | custom-call | tf_op jit(solution)/shard_map/pallas_call | solution.py:895
  236.6 1.2 copy-done.3
  238.4 34.8 %shard_map.402 = (bf16[768,3072]{1,0:T(8,128)(2,1)}, bf16[768,3840]{1,0:T(8,128)(2,1)}, f32[1024,768]{1,0:T(8,128)}, bf16[1024,768]{1,0:T(8,128)(2,1)}, f32[6,2,...) custom-call(f32[1024,768]{1,0:T(8,128)} %get-tuple-element.83.dy_ref, bf16[1024,768]{1,0:T(8,128)(2,1)} %copy-done.3, ...), custom_call_target="tpu_custom_call" | custom-call | tf_op jit(solution)/shard_map/pallas_call | solution.py:1396
  273.5 1.1 copy-done.10
  274.6 1.8 add_convert_fusion.normed_ref
  276.5 52.8 %shard_map.403 = (bf16[1024,768]{1,0:T(8,128)(2,1)}, bf16[1024,768]{1,0:T(8,128)(2,1)}, bf16[1024,768]{1,0:T(8,128)(2,1)}, f32[24,3072]{1,0:T(8,128)}, bf16[2,2,2,4,80,768]{5,4,3,2,1,0:T(8,128)(2,1)}) custom-call(bf16[1024,2304]{1,0:T(8,128)(2,1)} %convolution_convert_fusion.q_ref.k_ref.v_ref, bf16[1024,2304]{1,0:T(8,128)(2,1)} %convolution_convert_fusion.q_ref.k_ref.v_ref, ...), custom_call_target="tpu_custom_call" | custom-call | tf_op jit(solution)/shard_map/pallas_call | solution.py:1158
  329.3 5.3 %copy.110 = bf16[32,80,768]{2,0,1:T(8,128)(2,1)} copy(bf16[32,80,768]{2,1,0:T(8,128)(2,1)} %bitcast.122) | data formatting | bytes 7864320 | tf_op jit(solution)/shard_map/reshape | solution.py:1747
  334.7 2.1 copy-done
  336.8 4.4 shard_map.405
  341.3 0.9 reshape.322
  342.7 1.1 reshape.321
  344.2 1.1 reshape.324
  345.5 0.8 slice_convert_fusion
  346.8 0.8 broadcast_multiply_fusion.1
  349.1 64.5 %shard_map.404 = (f32[24,2560]{1,0:T(8,128)}, bf16[4,256,768]{2,1,0:T(8,128)(2,1)}) custom-call(bf16[1024,768]{1,0:T(8,128)(2,1)} %get-tuple-element.94.dq_ref, bf16[1024,768]{1,0:T(8,128)(2,1)} %get-tuple-element.95.dk_ref, bf16[1024,768]{1,0:T(8,128)(2,1)} %get-tuple-element.96.dv_ref, bf16[1024,768]{1,0:T(8,128)(2,1)} %add_convert_fusion.normed_ref, ...), custom_call_target="tpu_custom_call" | custom-call | tf_op jit(solution)/shard_map/pallas_call | solution.py:1543
  413.7 1.7 slice.122
  417.0 3.3 convert_element_type.66
  422.6 1.2 copy.86
  426.1 0.9 slice.150
  427.1 0.8 reshape.317
  427.9 1.4 slice.148
  (185 shorter events, 21.7 us)
Async XLA Ops:
  7.2 3.9 copy-start.22
  7.2 3.9 copy-start.23
  7.2 4.8 %copy-start.27 = (bf16[11,24]{1,0:T(8,128)(2,1)S(1)}, bf16[11,24]{1,0:T(8,128)(2,1)}, u32[]{:S(2)}) copy-start(bf16[11,24]{1,0:T(8,128)(2,1)} %param.31) | copy-start | bytes 1588
  7.2 4.9 %copy-start.28 = (bf16[7,24]{1,0:T(8,128)(2,1)S(1)}, bf16[7,24]{1,0:T(8,128)(2,1)}, u32[]{:S(2)}) copy-start(bf16[7,24]{1,0:T(8,128)(2,1)} %param.43) | copy-start | bytes 1012
  7.2 4.9 %copy-start.29 = (bf16[96]{0:T(256)(128)(2,1)S(1)}, bf16[96]{0:T(256)(128)(2,1)}, u32[]{:S(2)}) copy-start(bf16[96]{0:T(256)(128)(2,1)} %param.29) | copy-start | bytes 580
  7.2 4.9 %copy-start.30 = (bf16[96]{0:T(256)(128)(2,1)S(1)}, bf16[96]{0:T(256)(128)(2,1)}, u32[]{:S(2)}) copy-start(bf16[96]{0:T(256)(128)(2,1)} %param.36) | copy-start | bytes 580
  7.3 4.9 %copy-start.31 = (bf16[96]{0:T(256)(128)(2,1)S(1)}, bf16[96]{0:T(256)(128)(2,1)}, u32[]{:S(2)}) copy-start(bf16[96]{0:T(256)(128)(2,1)} %param.41) | copy-start | bytes 580
  7.3 67.7 %copy-start.20 = (bf16[24,2304]{1,0:T(8,128)(2,1)S(1)}, bf16[24,2304]{1,0:T(8,128)(2,1)}, u32[]{:S(2)}) copy-start(bf16[24,2304]{1,0:T(8,128)(2,1)} %param.38) | copy-start | bytes 331780
  7.3 146.8 %all-gather.2.cloned.1.call-start = ((), (), s32[]{:S(2)}) async-start(), calls=%async_computation.1 | async-start | bytes 13381632 | tf_op jit(solution)/shard_map/all_gather | solution.py:1709
  8.7 66.4 %copy-start.16 = (bf16[24,3072]{1,0:T(8,128)(2,1)S(1)}, bf16[24,3072]{1,0:T(8,128)(2,1)}, u32[]{:S(2)}) copy-start(bf16[24,3072]{1,0:T(8,128)(2,1)} %param.35) | copy-start | bytes 442372
  9.2 66.3 %copy-start.17 = (bf16[24,3072]{1,0:T(8,128)(2,1)S(1)}, bf16[24,3072]{1,0:T(8,128)(2,1)}, u32[]{:S(2)}) copy-start(bf16[24,3072]{1,0:T(8,128)(2,1)} %param.40) | copy-start | bytes 442372
  11.1 65.1 %copy-start.24 = (bf16[24,768]{1,0:T(8,128)(2,1)S(1)}, bf16[24,768]{1,0:T(8,128)(2,1)}, u32[]{:S(2)}) copy-start(bf16[24,768]{1,0:T(8,128)(2,1)} %param.44) | copy-start | bytes 110596
  11.2 65.2 %copy-start.14 = (bf16[24,768]{1,0:T(8,128)(2,1)S(1)}, bf16[24,768]{1,0:T(8,128)(2,1)}, u32[]{:S(2)}) copy-start(bf16[24,768]{1,0:T(8,128)(2,1)} %param.32) | copy-start | bytes 110596
  11.9 64.5 %copy-start.21 = (bf16[24,1536]{1,0:T(8,128)(2,1)S(1)}, bf16[24,1536]{1,0:T(8,128)(2,1)}, u32[]{:S(2)}) copy-start(bf16[24,1536]{1,0:T(8,128)(2,1)} %param.33) | copy-start | bytes 221188
  11.9 414.2 %reduce-scatter.2.cloned.1.call-start = ((), (), s32[]{:S(2)}) async-start(), calls=%async_computation.2 | async-start | bytes 6082560 | tf_op jit(solution)/shard_map/reduce_scatter | solution.py:1742
  74.4 4.6 %copy-start.25 = (s32[32,32]{1,0:T(8,128)S(1)}, s32[32,32]{1,0:T(8,128)}, u32[]{:S(2)}) copy-start(s32[32,32]{1,0:T(8,128)} %param.25) | copy-start | bytes 12292
  75.5 4.1 copy-start.9
  77.8 2.8 copy-start.18
  77.8 2.8 copy-start.19
  79.6 2.0 copy-start.11
  81.6 5.4 %copy-start.6 = (bf16[4,16,768]{2,1,0:T(8,128)(2,1)S(1)}, bf16[4,16,768]{2,1,0:T(8,128)(2,1)}, u32[]{:S(2)}) copy-start(bf16[4,16,768]{2,1,0:T(8,128)(2,1)} %tokens_ref.1) | copy-start | bytes 294916
  150.2 1.2 copy-start.1
  151.3 1.4 copy-start.2
  154.1 1.7 slice-start
  155.8 32.1 %copy-start.4 = (f32[11,768]{1,0:T(8,128)S(1)}, f32[11,768]{1,0:T(8,128)}, u32[]{:S(2)}) copy-start(f32[11,768]{1,0:T(8,128)} %reshape.296.vec_ref.ivec_ref) | copy-start | bytes 101380
  155.8 32.1 %copy-start.8 = (f32[2]{0:T(128)S(1)}, f32[2]{0:T(128)}, u32[]{:S(2)}) copy-start(f32[2]{0:T(128)} %temp_ref.1) | copy-start | bytes 28
  236.6 1.2 copy-start.3
  273.2 1.4 copy-start.10
  334.7 2.1 copy-start
  341.3 5.5 %copy-start.15 = (bf16[24,768]{1,0:T(8,128)(2,1)S(1)}, bf16[24,768]{1,0:T(8,128)(2,1)}, u32[]{:S(2)}) copy-start(bf16[24,768]{1,0:T(8,128)(2,1)} %param.32) | copy-start | bytes 110596
  341.3 6.4 %copy-start.26 = (f32[4,1,768]{2,1,0:T(1,128)S(1)}, f32[4,1,768]{2,1,0:T(1,128)}, u32[]{:S(2)}) copy-start(f32[4,1,768]{2,1,0:T(1,128)} %get-tuple-element.100) | copy-start | bytes 36868
  413.7 8.0 %copy-start.13 = (f32[24,3072]{1,0:T(8,128)S(1)}, f32[24,3072]{1,0:T(8,128)}, u32[]{:S(2)}) copy-start(f32[24,3072]{1,0:T(8,128)} %get-tuple-element.105) | copy-start | bytes 884740
  (3 other events, 2.0 us)
Sparse Core Ops, SparseCore 0:
  12.0 141.9 all-gather.1
  273.4 134.7 reduce-scatter.1

commit v7 on v6

--- a/solution.py
+++ b/solution.py
@@ -1410,11 +1410,12 @@
     )(dy, branch, active, slope, second, hidden, mixed, main, main, main, vec)
 
 
-def finish_kernel(dq_ref, dk_ref, dv_ref, normed_ref, w_ref, x_ref, dhid_ref, sums_ref, vec_ref, own_ref, moved_ref,
-                  g, dx, from_c, acc_c, from_1, from_2, from_z, q_in, k_in, v_in, n_in, w_in, x_in, h_in,
-                  send, recv, local, fetch):
+def finish_kernel(dq_ref, dk_ref, dv_ref, normed_ref, w_ref, x_ref, dhid_ref, rows_ref, sums_ref, vec_ref, dimage_ref, dtext_ref, own_ref, moved_ref, *rest):
+    outer_refs, rest = rest[:13], rest[13:]
+    (g, dx, from_c, acc_c, from_1, from_2, from_z, q_in, k_in, v_in, n_in, w_in, x_in, h_in, r_in, turned,
+     send, recv, local, fetch) = rest
     me = Place()
-    pairs = ((dq_ref, q_in), (normed_ref, n_in), (dk_ref, k_in), (dv_ref, v_in), (w_ref, w_in), (x_ref, x_in), (dhid_ref, h_in))
+    pairs = ((dq_ref, q_in), (normed_ref, n_in), (dk_ref, k_in), (dv_ref, v_in), (w_ref, w_in), (x_ref, x_in), (dhid_ref, h_in), (rows_ref, r_in))
     loads = [pltpu.make_async_copy(src, dst, fetch.at[n]) for n, (src, dst) in enumerate(pairs)]
     for load in loads:
         load.start()
@@ -1499,7 +1500,7 @@
     part_of(0, dq_ref)
     loads[2].wait()
     part_of(1, dk_ref)
-    for load in loads[3:]:
+    for load in loads[3:7]:
         load.wait()
     core_left = core(left, 0)
     d_x_rows(2)
@@ -1518,10 +1519,19 @@
     two_left = push(6, acc_c.at[y, 1 - x, :, :, left], from_2.at[0], me.at_x, from_2.at[0])
     core_done(core_right, right)
     one_right = push(5, acc_c.at[:, 1 - x, :, :, right], from_1.at[1], me.at_x, from_1.at[1])
+    loads[7].wait()
+    group = 16
+    count = 32 * group
+    to, fro = lax.broadcasted_iota(jnp.int32, (count, count), 0), lax.broadcasted_iota(jnp.int32, (count, count), 1)
+    turn = ((to % 32 == fro // group) & (to // 32 == fro % group)).astype(BF)
+    for n in range(r_in.shape[1] // group):
+        value = mm(turn, r_in[:, n * group : (n + 1) * group, :].reshape(count, width)).astype(BF)
+        turned[n * group : (n + 1) * group] = value.reshape(group, 32, width)
     two_done(two_left, 0, left)
     z_left = along(left, 8)
     one_done(one_right, 1, right)
     two_right = push(7, acc_c.at[1 - y, x, :, :, right], from_2.at[1], me.at_y, from_2.at[1])
+    outer_kernel(turned, dimage_ref, dtext_ref, *outer_refs)
     two_done(two_right, 1, right)
     z_right = along(right, 11)
     for arrive in z_left + z_right:
@@ -1535,25 +1545,29 @@
         copy.wait_send()
 
 
-def finish_image(dq, dk, dv, normed, w_in, x, d_hidden, sums, vec, cid):
+def finish_image(dq, dk, dv, normed, w_in, x, d_hidden, own_rows, sums, vec, d_image, d_text, cid):
     rows, width = dq.shape
-    part, n = width // 32, 3 * width + 256
+    part, n, quarter = width // 32, 3 * width + 256, width // 4
+    f = lambda *s: jax.ShapeDtypeStruct(s, F32)
     v, hbm = pl.BlockSpec(memory_space=pltpu.VMEM), pl.BlockSpec(memory_space=pl.ANY)
     s = lambda *shape: pltpu.VMEM(shape, BF)
     return pl.pallas_call(
         finish_kernel,
-        in_specs=[hbm] * 7 + [v] * 2,
-        out_specs=[v, hbm],
-        out_shape=[jax.ShapeDtypeStruct((part, n), F32), jax.ShapeDtypeStruct((4, rows // 4, width), BF)],
+        in_specs=[hbm] * 8 + [v] * 4,
+        out_specs=[v, hbm] + [v] * 13,
+        out_shape=[jax.ShapeDtypeStruct((part, n), F32), jax.ShapeDtypeStruct((4, rows // 4, width), BF),
+                   f(4, part, width), f(4, part, width), f(4 * part, width), f(4 * part, width), f(part, width), f(part, width),
+                   f(part, width), f(4, part, quarter), f(4, part, quarter), f(4, part, quarter), f(4, part, quarter),
+                   f(part, 128), f(2, 4 * part, 128)],
         scratch_shapes=[
             s(2, 2, 2, 4, part, n), s(4, rows // 4, width), s(2, 2, 4, part, n), s(2, 2, 4, part, n),
             s(2, 2, 4, part, n // 2), s(2, 4, part, n // 2), s(3, part, n),
             s(rows, width), s(rows, width), s(rows, width), s(rows, width), s(width, 3 * width), s(rows, width),
-            pltpu.VMEM((rows, width), F32),
-            pltpu.SemaphoreType.DMA((15,)), pltpu.SemaphoreType.DMA((15,)), pltpu.SemaphoreType.DMA, pltpu.SemaphoreType.DMA((7,)),
+            pltpu.VMEM((rows, width), F32), s(32, ROWS, width), s(ROWS, 32, width),
+            pltpu.SemaphoreType.DMA((15,)), pltpu.SemaphoreType.DMA((15,)), pltpu.SemaphoreType.DMA, pltpu.SemaphoreType.DMA((8,)),
         ],
-        compiler_params=pltpu.CompilerParams(collective_id=cid, has_side_effects=True, vmem_limit_bytes=56 << 20),
-    )(dq, dk, dv, normed, w_in, x, d_hidden, sums, vec)
+        compiler_params=pltpu.CompilerParams(collective_id=cid, has_side_effects=True, vmem_limit_bytes=60 << 20),
+    )(dq, dk, dv, normed, w_in, x, d_hidden, own_rows, sums, vec, d_image, d_text)
 
 
 def outer_kernel(rows_ref, dimage_ref, dtext_ref,
@@ -1634,22 +1648,6 @@
     pk_ref[...] = mm(get(68, HEADS), (a // n == b).astype(BF))
 
 
-def outer_grads(rows, d_image, d_text):
-    width = rows.shape[2]
-    part, quarter = width // 32, width // 4
-    v = pl.BlockSpec(memory_space=pltpu.VMEM)
-    f = lambda *s: jax.ShapeDtypeStruct(s, F32)
-    return pl.pallas_call(
-        outer_kernel,
-        in_specs=[v] * 3,
-        out_specs=[v] * 13,
-        out_shape=[f(4, part, width), f(4, part, width), f(4 * part, width), f(4 * part, width), f(part, width), f(part, width),
-                   f(part, width), f(4, part, quarter), f(4, part, quarter), f(4, part, quarter), f(4, part, quarter),
-                   f(part, 128), f(2, 4 * part, 128)],
-        compiler_params=pltpu.CompilerParams(vmem_limit_bytes=48 << 20),
-    )(rows, d_image, d_text)
-
-
 def fast_program(
     patches, captions, pairs,
     image_attend_in, image_attend_out, image_up_weight, image_up_bias, image_down_weight,
@@ -1744,24 +1742,24 @@
     own_down = g_rest[:, width:].reshape(wide_part, width)
     d_q, d_k, d_v, own_up, rows = attend_bwd_and_reduce(proj, d_mixed, lse, inner, g_up, rows, 4)
     own_up = own_up.reshape(part, fold, width).transpose(0, 2, 1).reshape(part, hidden_width)
-    rows = rows.reshape(world, ROWS, width).transpose(1, 0, 2)
+    rows = rows.reshape(world, ROWS, width)
     sums = jnp.concatenate([dvec[0:2], dvec[0:2], sums[4:], g_bias.reshape(fold, width)], 0)
-    own_in, moved = finish_image(d_q, d_k, d_v, normed, w_in, x, d_hidden, sums, ivec, 3)
+    d_embeds = d_embeds.reshape(n_dp, 2, n_z, width).astype(BF)
+    own_in, moved, *outer = finish_image(
+        d_q, d_k, d_v, normed, w_in, x, d_hidden, rows, sums, ivec,
+        d_embeds[:, 0].reshape(world, width), d_embeds[:, 1].reshape(world, width), 3
+    )
+    pup, tup, own_p_down, own_t_down, own_p_out, own_t_out, own_t_head, tq, tk, tv, pv, pk, biases = outer
     grad_patches = moved.astype(F32)
     own_sums = own_in[:, 3 * width : 3 * width + 128].T
     own_in = own_in[:, : 3 * width]
 
-    d_embeds = d_embeds.reshape(n_dp, 2, n_z, width).astype(BF)
-    pup, tup, own_p_down, own_t_down, own_p_out, own_t_out, own_t_head, tq, tk, tv, pv, pk, biases = outer_grads(
-        rows, d_embeds[:, 0].reshape(world, width), d_embeds[:, 1].reshape(world, width)
-    )
-
     def wide(g):
         return g.reshape(n_z, part, n_dp, wide_part).transpose(1, 2, 0, 3).reshape(part, hidden_width)
 
     own_p_up, own_t_up = wide(pup), wide(tup)
     own_t_in = jnp.stack([tq, tk, tv]).transpose(2, 0, 1, 3).reshape(part, 3 * width)
-    row20 = rows[20].reshape(n_dp, n_z, n_z, quarter).astype(F32)
+    row20 = rows[:, 20].reshape(n_dp, n_z, n_z, quarter).astype(F32)
     probe_query = row20[0, :, 3].reshape(HEADS, head_width)
     own_p_k = (pk[:, :HEADS, None] * probe_query[None]).reshape(part, width)
     own_p_pair = jnp.concatenate([own_p_k, pv.transpose(1, 0, 2).reshape(part, width)], 1)

time: 445 us -> 443 us (level)
    reshape x1 -> x0, local copies, waits for them, and re-layouts: 5.29 us -> none  [fast_program(): rows = rows.reshape(world, ROWS, width).transpose(1, 0, 2)]
    unnamed x88 -> x109, local copies, waits for them, and re-layouts: 16.1 us -> 17.3 us
    pallas_call x2 -> x1, Pallas kernels: 68.9 us -> 70 us  [finish_image(): pl.pallas_call(finish_kernel, in_specs=[hbm] * 8 + [v] * 4, out_specs=[v,...]
  transfers between devices with their start and end apart: 2 -> 2, of which waited for: 1 -> 1; matrix products, arithmetic and copies ran while one was open for 9% -> 9% of each run, Pallas kernels for 56% -> 57%
where the time goes in v7:
time: 443 us; the launch traced here: 435 us
  Pallas kernels  361 us (81%)
  local copies, waits for them, and re-layouts  41.7 us (9%)
  between operations  15.4 us (3%)
  other arithmetic  10.3 us (2%)
  matrix products  5.39 us (1%)
    pallas_call x1, Pallas kernels, finish_image(): pl.pallas_call(finish_kernel, in_specs=[hbm] * 8 + [v] * 4, out_specs=[v,...  70 us
    pallas_call x1, Pallas kernels, attend_fwd_and_gather(): pl.pallas_call(attend_fwd_kernel_hosting, grid=(pairs,), in_specs=[block(...  63.1 us
    pallas_call x1, Pallas kernels, gather(): pl.pallas_call(partial(gather_kernel, kinds, order), out_shape=shapes, in...  60.5 us
    pallas_call x1, Pallas kernels, attend_bwd_and_reduce(): pl.pallas_call(attend_bwd_kernel_hosting, grid=(pairs,), in_specs=[block(...  52.5 us
    pallas_call x1, Pallas kernels, middle(): pl.pallas_call(middle_kernel, in_specs=[hbm, hbm, v, hbm, hbm] + [v] * 6...  48.6 us
    pallas_call x1, Pallas kernels, mlp_bwd(): pl.pallas_call(mlp_bwd_kernel, grid=(fold,), in_specs=[hbm, whole, tile,...  34.9 us
    pallas_call x1, Pallas kernels, mlp_fwd(): pl.pallas_call(mlp_fwd_kernel, grid=(fold,), in_specs=[whole, whole, at(l...  31.6 us
    unnamed x109, local copies, waits for them, and re-layouts  17.3 us
  transfers between devices with their start and end apart: 2, of which 1 were waited for; matrix products, arithmetic and copies ran while one was open for 9% of the time, Pallas kernels for 57%

profile of v7, /device:TPU:0, one launch (start us, length us, event | category | flops | bytes accessed | tf_op | source)
XLA Modules:
  0.0 434.7 jit_solution(17661160594070146870)
XLA Ops:
  7.3 1.3 copy.70
  9.2 0.8 constant_dynamic-update-slice_fusion.6
  10.0 1.0 reshape.294
  12.9 60.5 %shard_map.398 = (bf16[2,2,2,4,24,2304]{5,4,3,2,1,0:T(8,128)(2,1)}, bf16[2,2,2,4,16,128]{5,4,3,2,1,0:T(8,128)(2,1)}, bf16[4,256,768]{2,1,0:T(8,128)(2,1)}) custom-call(bf16[24,2304]{1,0:T(8,128)(2,1)} %refs_0_.1, bf16[16,128]{1,0:T(8,128)(2,1)} %pad_bitcast_fusion.refs_1_, bf16[4,256,768]{2,1,0:T(8,128)(2,1)} %refs_2_.1), custom_call_target="tpu_custom_call" | custom-call | tf_op jit(solution)/shard_map/pallas_call | solution.py:611
  73.4 0.9 copy.108
  76.7 0.8 reshape.296.vec_ref.ivec_ref
  81.6 5.4 %convolution_convert_fusion.q_ref.k_ref.v_ref = bf16[1024,2304]{1,0:T(8,128)(2,1)} fusion(bf16[1024,768]{1,0:T(8,128)(2,1)S(1)} %bitcast.117, bf16[768,2304]{1,0:T(8,128)(2,1)S(1)} %bitcast.115), kind=kOutput, calls=%fused_computation | convolution fusion | flops 3626237952 | bytes 9830400 | tf_op jit(solution)/shard_map/dot_general | solution.py:18
  87.0 63.1 %shard_map.399 = (bf16[1024,768]{1,0:T(8,128)(2,1)S(1)}, f32[6,2,1024]{2,1,0:T(2,128)S(1)}, bf16[2,2,2,4,24,3328]{5,4,3,2,1,0:T(8,128)(2,1)}, bf16[2,2,2,96,1536...) custom-call(bf16[1024,2304]{1,0:T(8,128)(2,1)} %convolution_convert_fusion.q_ref.k_ref.v_ref, ...), custom_call_target="tpu_custom_call" | custom-call | tf_op jit(solution)/shard_map/pallas_call | solution.py:1242
  150.1 1.2 copy-done
  151.3 1.4 copy-done.1
  154.1 1.7 slice-done
  155.8 31.6 %shard_map.400 = (f32[1024,768]{1,0:T(8,128)}, bf16[1024,768]{1,0:T(8,128)(2,1)}, bf16[1024,3072]{1,0:T(8,128)(2,1)}, bf16[1024,3072]{1,0:T(8,128)(2,1)}, f32[10...) custom-call(bf16[1024,768]{1,0:T(8,128)(2,1)} %bitcast.107, ...), custom_call_target="tpu_custom_call", output_to_operand_aliasing={{6}: (7, {})} | custom-call | tf_op jit(solution)/shard_map/pallas_call | solution.py:1308
  187.4 48.6 %shard_map.401 = (f32[1024,768]{1,0:T(8,128)}, bf16[1024,768]{1,0:T(8,128)(2,1)S(1)}, bf16[80,768]{1,0:T(8,128)(2,1)S(1)}, f32[24,768]{1,0:T(8,128)S(1)}, f32[64...) custom-call(bf16[1024,768]{1,0:T(8,128)(2,1)} %get-tuple-element.77.final_in, ...), custom_call_target="tpu_custom_call" | custom-call | tf_op jit(solution)/shard_map/pallas_call | solution.py:895
  236.0 1.2 copy-done.2
  237.9 34.9 %shard_map.402 = (bf16[768,3072]{1,0:T(8,128)(2,1)}, bf16[768,3840]{1,0:T(8,128)(2,1)}, f32[1024,768]{1,0:T(8,128)}, bf16[1024,768]{1,0:T(8,128)(2,1)}, f32[6,2,...) custom-call(f32[1024,768]{1,0:T(8,128)} %get-tuple-element.83.dy_ref, bf16[1024,768]{1,0:T(8,128)(2,1)} %copy-done.2, ...), custom_call_target="tpu_custom_call" | custom-call | tf_op jit(solution)/shard_map/pallas_call | solution.py:1396
  273.1 1.1 copy-done.9
  274.2 1.8 add_convert_fusion.normed_ref
  278.1 52.5 %shard_map.403 = (bf16[1024,768]{1,0:T(8,128)(2,1)}, bf16[1024,768]{1,0:T(8,128)(2,1)}, bf16[1024,768]{1,0:T(8,128)(2,1)}, f32[24,3072]{1,0:T(8,128)}, bf16[2,2,2,4,80,768]{5,4,3,2,1,0:T(8,128)(2,1)}) custom-call(bf16[1024,2304]{1,0:T(8,128)(2,1)} %convolution_convert_fusion.q_ref.k_ref.v_ref, bf16[1024,2304]{1,0:T(8,128)(2,1)} %convolution_convert_fusion.q_ref.k_ref.v_ref, ...), custom_call_target="tpu_custom_call" | custom-call | tf_op jit(solution)/shard_map/pallas_call | solution.py:1158
  331.3 70.0 %shard_map.404 = (f32[24,2560]{1,0:T(8,128)}, bf16[4,256,768]{2,1,0:T(8,128)(2,1)}, f32[4,24,768]{2,1,0:T(8,128)}, f32[4,24,768]{2,1,0:T(8,128)}, f32[96,768]{1,...) custom-call(bf16[1024,768]{1,0:T(8,128)(2,1)} %get-tuple-element.94., ...), custom_call_target="tpu_custom_call" | custom-call | tf_op jit(solution)/shard_map/pallas_call | solution.py:1554
  401.3 1.1 maximum_bitcast_fusion
  402.5 0.9 reshape.322
  403.4 0.8 mul.106
  404.4 1.3 fusion.6
  405.9 0.9 copy.80
  407.1 0.8 broadcast_multiply_fusion.1
  409.6 1.9 convert_element_type.68
  412.0 1.1 reshape.321
  413.6 1.1 reshape.324
  416.9 1.2 copy.84
  420.5 0.9 slice.152
  421.4 0.8 reshape.318
  422.2 1.4 slice.150
  (204 shorter events, 25.4 us)
Async XLA Ops:
  7.2 3.9 copy-start.30
  7.2 3.9 copy-start.31
  7.2 4.8 %copy-start.35 = (bf16[11,24]{1,0:T(8,128)(2,1)S(1)}, bf16[11,24]{1,0:T(8,128)(2,1)}, u32[]{:S(2)}) copy-start(bf16[11,24]{1,0:T(8,128)(2,1)} %param.31) | copy-start | bytes 1588
  7.2 4.9 %copy-start.36 = (bf16[7,24]{1,0:T(8,128)(2,1)S(1)}, bf16[7,24]{1,0:T(8,128)(2,1)}, u32[]{:S(2)}) copy-start(bf16[7,24]{1,0:T(8,128)(2,1)} %param.43) | copy-start | bytes 1012
  7.2 4.9 %copy-start.37 = (bf16[96]{0:T(256)(128)(2,1)S(1)}, bf16[96]{0:T(256)(128)(2,1)}, u32[]{:S(2)}) copy-start(bf16[96]{0:T(256)(128)(2,1)} %param.29) | copy-start | bytes 580
  7.2 4.9 %copy-start.38 = (bf16[96]{0:T(256)(128)(2,1)S(1)}, bf16[96]{0:T(256)(128)(2,1)}, u32[]{:S(2)}) copy-start(bf16[96]{0:T(256)(128)(2,1)} %param.36) | copy-start | bytes 580
  7.3 4.9 %copy-start.39 = (bf16[96]{0:T(256)(128)(2,1)S(1)}, bf16[96]{0:T(256)(128)(2,1)}, u32[]{:S(2)}) copy-start(bf16[96]{0:T(256)(128)(2,1)} %param.41) | copy-start | bytes 580
  7.3 67.7 %copy-start.24 = (bf16[24,2304]{1,0:T(8,128)(2,1)S(1)}, bf16[24,2304]{1,0:T(8,128)(2,1)}, u32[]{:S(2)}) copy-start(bf16[24,2304]{1,0:T(8,128)(2,1)} %param.38) | copy-start | bytes 331780
  7.3 146.8 %all-gather.2.cloned.1.call-start = ((), (), s32[]{:S(2)}) async-start(), calls=%async_computation.1 | async-start | bytes 13381632 | tf_op jit(solution)/shard_map/all_gather | solution.py:1707
  8.7 66.4 %copy-start.20 = (bf16[24,3072]{1,0:T(8,128)(2,1)S(1)}, bf16[24,3072]{1,0:T(8,128)(2,1)}, u32[]{:S(2)}) copy-start(bf16[24,3072]{1,0:T(8,128)(2,1)} %param.35) | copy-start | bytes 442372
  9.2 66.3 %copy-start.21 = (bf16[24,3072]{1,0:T(8,128)(2,1)S(1)}, bf16[24,3072]{1,0:T(8,128)(2,1)}, u32[]{:S(2)}) copy-start(bf16[24,3072]{1,0:T(8,128)(2,1)} %param.40) | copy-start | bytes 442372
  11.1 65.1 %copy-start.32 = (bf16[24,768]{1,0:T(8,128)(2,1)S(1)}, bf16[24,768]{1,0:T(8,128)(2,1)}, u32[]{:S(2)}) copy-start(bf16[24,768]{1,0:T(8,128)(2,1)} %param.44) | copy-start | bytes 110596
  11.2 65.2 %copy-start.19 = (bf16[24,768]{1,0:T(8,128)(2,1)S(1)}, bf16[24,768]{1,0:T(8,128)(2,1)}, u32[]{:S(2)}) copy-start(bf16[24,768]{1,0:T(8,128)(2,1)} %param.32) | copy-start | bytes 110596
  11.9 64.5 %copy-start.26 = (bf16[24,1536]{1,0:T(8,128)(2,1)S(1)}, bf16[24,1536]{1,0:T(8,128)(2,1)}, u32[]{:S(2)}) copy-start(bf16[24,1536]{1,0:T(8,128)(2,1)} %param.33) | copy-start | bytes 221188
  11.9 408.5 %reduce-scatter.2.cloned.1.call-start = ((), (), s32[]{:S(2)}) async-start(), calls=%async_computation.2 | async-start | bytes 6082560 | tf_op jit(solution)/shard_map/reduce_scatter | solution.py:1740
  74.4 4.6 %copy-start.33 = (s32[32,32]{1,0:T(8,128)S(1)}, s32[32,32]{1,0:T(8,128)}, u32[]{:S(2)}) copy-start(s32[32,32]{1,0:T(8,128)} %param.25) | copy-start | bytes 12292
  75.5 4.1 copy-start.8
  81.6 5.4 %copy-start.5 = (bf16[4,16,768]{2,1,0:T(8,128)(2,1)S(1)}, bf16[4,16,768]{2,1,0:T(8,128)(2,1)}, u32[]{:S(2)}) copy-start(bf16[4,16,768]{2,1,0:T(8,128)(2,1)} %tokens_ref.1) | copy-start | bytes 294916
  155.8 31.6 %copy-start.3 = (f32[11,768]{1,0:T(8,128)S(1)}, f32[11,768]{1,0:T(8,128)}, u32[]{:S(2)}) copy-start(f32[11,768]{1,0:T(8,128)} %reshape.296.vec_ref.ivec_ref) | copy-start | bytes 101380
  155.8 31.6 %copy-start.7 = (f32[2]{0:T(128)S(1)}, f32[2]{0:T(128)}, u32[]{:S(2)}) copy-start(f32[2]{0:T(128)} %temp_ref.1) | copy-start | bytes 28
  272.8 3.2 copy-start.34
  401.3 6.8 %copy-start.18 = (f32[24,2560]{1,0:T(8,128)S(1)}, f32[24,2560]{1,0:T(8,128)}, u32[]{:S(2)}) copy-start(f32[24,2560]{1,0:T(8,128)} %get-tuple-element.105) | copy-start | bytes 737284
  401.3 8.4 %copy-start.11 = (bf16[4,256,768]{2,1,0:T(8,128)(2,1)S(1)}, bf16[4,256,768]{2,1,0:T(8,128)(2,1)}, u32[]{:S(2)}) copy-start(bf16[4,256,768]{2,1,0:T(8,128)(2,1)} %get-tuple-element.103) | copy-start | bytes 4718596
  404.3 7.2 %copy-start.17 = (f32[4,24,768]{2,1,0:T(8,128)S(1)}, f32[4,24,768]{2,1,0:T(8,128)}, u32[]{:S(2)}) copy-start(f32[4,24,768]{2,1,0:T(8,128)} %get-tuple-element.111) | copy-start | bytes 884740
  409.6 3.5 copy-start.16
  411.6 4.4 %copy-start.15 = (f32[24,3072]{1,0:T(8,128)S(1)}, f32[24,3072]{1,0:T(8,128)}, u32[]{:S(2)}) copy-start(f32[24,3072]{1,0:T(8,128)} %get-tuple-element.107) | copy-start | bytes 884740
  413.1 5.5 %copy-start.25 = (f32[2,96,128]{2,1,0:T(8,128)S(1)}, f32[2,96,128]{2,1,0:T(8,128)}, u32[]{:S(2)}) copy-start(f32[2,96,128]{2,1,0:T(8,128)} %get-tuple-element.112) | copy-start | bytes 294916
  416.1 8.1 %copy-start.29 = (f32[24,768]{1,0:T(8,128)S(1)}, f32[24,768]{1,0:T(8,128)}, u32[]{:S(2)}) copy-start(f32[24,768]{1,0:T(8,128)} %get-tuple-element.226) | copy-start | bytes 221188
  416.2 8.8 %copy-start.14 = (f32[96,768]{1,0:T(8,128)S(1)}, f32[96,768]{1,0:T(8,128)}, u32[]{:S(2)}) copy-start(f32[96,768]{1,0:T(8,128)} %get-tuple-element.229) | copy-start | bytes 884740
  416.2 9.5 %copy-start.28 = (f32[24,768]{1,0:T(8,128)S(1)}, f32[24,768]{1,0:T(8,128)}, u32[]{:S(2)}) copy-start(f32[24,768]{1,0:T(8,128)} %get-tuple-element.231) | copy-start | bytes 221188
  416.2 10.1 %copy-start.13 = (f32[96,768]{1,0:T(8,128)S(1)}, f32[96,768]{1,0:T(8,128)}, u32[]{:S(2)}) copy-start(f32[96,768]{1,0:T(8,128)} %get-tuple-element.234) | copy-start | bytes 884740
  416.9 10.1 %copy-start.27 = (f32[24,768]{1,0:T(8,128)S(1)}, f32[24,768]{1,0:T(8,128)}, u32[]{:S(2)}) copy-start(f32[24,768]{1,0:T(8,128)} %get-tuple-element.236) | copy-start | bytes 221188
  (11 other events, 16.4 us)
Sparse Core Ops, SparseCore 0:
  12.0 141.9 all-gather.1
  272.9 137.9 reduce-scatter.1

commit v8 on v7

--- a/solution.py
+++ b/solution.py
@@ -1298,7 +1298,7 @@
         act(5, "sent")
 
 
-def mlp_fwd(x, mixed, main, bias, vec, fold, tp, cid):
+def mlp_fwd(x, mixed, w_outs, main, bias, vec, fold, tp, cid):
     rows, width = mixed.shape
     whole = pl.BlockSpec((rows, width), lambda k: (0, 0))
     tile = pl.BlockSpec((rows, width), lambda k: (0, k))
@@ -1308,7 +1308,7 @@
     return pl.pallas_call(
         mlp_fwd_kernel,
         grid=(fold,),
-        in_specs=[whole, whole, at(lambda k: 0), at(lambda k: 1 + k), at(lambda k: 1 + fold + k),
+        in_specs=[whole, whole, at(lambda k: 0), at(lambda k: k), at(lambda k: fold + k),
                   pl.BlockSpec((1, 1, width), lambda k: (k, 0, 0)), pl.BlockSpec(vec.shape, lambda k: (0, 0)), hbm],
         out_specs=[whole, whole, tile, tile, whole, whole, hbm],
         out_shape=[s(1, F32), s(1, BF), s(fold, BF), s(fold, BF), s(1, F32), s(1, BF),
@@ -1316,7 +1316,7 @@
         scratch_shapes=[pltpu.VMEM((rows, width), F32), pltpu.SemaphoreType.DMA((11,)), pltpu.SemaphoreType.DMA((11,))],
         input_output_aliases={7: 6},
         compiler_params=pltpu.CompilerParams(collective_id=cid, has_side_effects=True, vmem_limit_bytes=56 << 20),
-    )(x, mixed, main, main, main, bias.reshape(fold, 1, width), vec, tp)
+    )(x, mixed, w_outs, main, main, bias.reshape(fold, 1, width), vec, tp)
 
 
 def mlp_bwd_kernel(dy_ref, branch_ref, active_ref, slope_ref, second_ref, hidden_ref, mixed_ref,
@@ -1386,7 +1386,7 @@
         out.wait()
 
 
-def mlp_bwd(dy, branch, active, slope, second, hidden, mixed, main, vec, fold):
+def mlp_bwd(dy, branch, active, slope, second, hidden, mixed, w_outs, main, vec, fold):
     rows, width = mixed.shape
     whole = pl.BlockSpec((rows, width), lambda k: (0, 0))
     tile = pl.BlockSpec((rows, width), lambda k: (0, k))
@@ -1397,7 +1397,7 @@
         mlp_bwd_kernel,
         grid=(fold,),
         in_specs=[hbm, whole, tile, tile, whole, hbm, hbm,
-                  at(lambda k: 0), at(lambda k: 1 + k), at(lambda k: 1 + fold + k), pl.BlockSpec(vec.shape, lambda k: (0, 0))],
+                  at(lambda k: 0), at(lambda k: k), at(lambda k: fold + k), pl.BlockSpec(vec.shape, lambda k: (0, 0))],
         out_specs=[at(lambda k: k), hbm, whole, whole,
                    pl.BlockSpec((HEADS // 2, 2, rows), lambda k: (0, 0, 0)),
                    pl.BlockSpec((1, 1, width), lambda k: (k, 0, 0)), pl.BlockSpec((8, width), lambda k: (0, 0))],
@@ -1407,7 +1407,7 @@
                         pltpu.VMEM((rows, width), BF), pltpu.VMEM((2, width, width), BF),
                         pltpu.SemaphoreType.DMA((3,)), pltpu.SemaphoreType.DMA((3,))],
         compiler_params=pltpu.CompilerParams(vmem_limit_bytes=60 << 20),
-    )(dy, branch, active, slope, second, hidden, mixed, main, main, main, vec)
+    )(dy, branch, active, slope, second, hidden, mixed, w_outs, main, main, vec)
 
 
 def finish_kernel(dq_ref, dk_ref, dv_ref, normed_ref, w_ref, x_ref, dhid_ref, rows_ref, sums_ref, vec_ref, dimage_ref, dtext_ref, own_ref, moved_ref, *rest):
@@ -1686,26 +1686,25 @@
     split += [by_heads(probe_pair_weight[:, k * width : (k + 1) * width]) for k in range(2)]
     split = jnp.concatenate(split, 2)
     downs = jnp.concatenate([text_down_weight, probe_down_weight], 1)
-    w_in, small_all, x = gather(
-        [image_attend_in, small, patches],
-        [("full", "S"), ("full", "C"), ("za", None)],
-        [(0, 0), (1, 0), (0, 1), (1, 1), (0, 2), (1, 2), (0, 3), (2, 0), (1, 3), (0, 4), (1, 4), (0, 5), (1, 5)],
+    w_in, small_all, w_outs, x = gather(
+        [image_attend_in, small, jnp.concatenate([image_attend_out, text_attend_out, probe_out_weight], 1), patches],
+        [("full", "S"), ("full", "C"), ("full", "S"), ("za", None)],
+        [(0, 0), (1, 0), (0, 1), (1, 1), (0, 2), (1, 2), (2, 0), (0, 3), (2, 1), (1, 3), (2, 2), (3, 0)]
+        + [(0, 4), (1, 4), (2, 3), (0, 5), (1, 5), (2, 4), (2, 5)],
         1,
     )
+    w_outs = w_outs.reshape(width, 3 * width)
+    outs = lax.dynamic_slice_in_dim(w_outs[:, width:], at_z * quarter, quarter, 0)
     w_in = w_in.reshape(width, 3 * width)
     x = x.reshape(length, width)
     main = jnp.concatenate(
         [
-            image_attend_out,
             image_up_weight.reshape(part, width, fold).transpose(0, 2, 1).reshape(part, hidden_width),
             image_down_weight.reshape(part, hidden_width),
-            text_attend_out,
-            probe_out_weight,
         ],
         1,
     )
     main = lax.all_gather(main, ALL, axis=0, tiled=True)
-    outs = lax.dynamic_slice_in_dim(main[:, width + 2 * hidden_width :], at_z * quarter, quarter, 0)
 
     small_all = small_all.reshape(world, -1)
     cuts = [sum(sizes[:i]) for i in range(len(sizes) + 1)]
@@ -1723,7 +1722,7 @@
     normed = layer_norm(x.astype(F32), ivec[0], ivec[1]).astype(BF)
     proj = mm(normed, w_in).astype(BF)
     mixed, lse, tp, downs, tokens = attend_fwd_and_gather(proj, split, downs, captions, 5)
-    hidden, second, active, slope, block_out, final, tp = mlp_fwd(x, mixed, main, i_bias, ivec, fold, tp, 6)
+    hidden, second, active, slope, block_out, final, tp = mlp_fwd(x, mixed, w_outs, main, i_bias, ivec, fold, tp, 6)
     tp, downs = tp.reshape(width, -1), downs.reshape(width, -1)
 
     labels = (2 * pairs - 1).astype(F32).reshape(n_dp, n_z, n_dp, n_z)
@@ -1735,7 +1734,7 @@
     grad_captions = d_captions.reshape(captions.shape)
 
     g_up, g_rest, d_hidden, d_mixed, inner, g_bias, dvec = mlp_bwd(
-        dy, d_branch, active, slope, second, hidden, mixed, main, ivec, fold
+        dy, d_branch, active, slope, second, hidden, mixed, w_outs, main, ivec, fold
     )
     g_rest = lax.psum_scatter(g_rest, ALL, scatter_dimension=0, tiled=True).astype(F32)
     own_out = g_rest[:, :width]

time: 443 us -> 432 us (0.975)
  Pallas kernels: 361 us -> 348 us
    pallas_call x1, Pallas kernels: 63.1 us -> 41.5 us  [attend_fwd_and_gather(): pl.pallas_call(attend_fwd_kernel_hosting, grid=(pairs,), in_specs=[block(...]
    pallas_call x1, Pallas kernels: 60.5 us -> 69.9 us  [gather(): pl.pallas_call(partial(gather_kernel, kinds, order), out_shape=shapes, in...]
    unnamed x109 -> x105, local copies, waits for them, and re-layouts: 17.3 us -> 15.8 us
  transfers between devices with their start and end apart: 2 -> 2, of which waited for: 1 -> 0; matrix products, arithmetic and copies ran while one was open for 9% -> 10% of each run, Pallas kernels for 57% -> 55%
where the time goes in v8:
time: 432 us; the launch traced here: 423 us
  Pallas kernels  348 us (81%)
  local copies, waits for them, and re-layouts  43 us (10%)
  between operations  15.3 us (4%)
  other arithmetic  11.7 us (3%)
  matrix products  5.4 us (1%)
    pallas_call x1, Pallas kernels, gather(): pl.pallas_call(partial(gather_kernel, kinds, order), out_shape=shapes, in...  69.9 us
    pallas_call x1, Pallas kernels, finish_image(): pl.pallas_call(finish_kernel, in_specs=[hbm] * 8 + [v] * 4, out_specs=[v,...  69.7 us
    pallas_call x1, Pallas kernels, attend_bwd_and_reduce(): pl.pallas_call(attend_bwd_kernel_hosting, grid=(pairs,), in_specs=[block(...  52.9 us
    pallas_call x1, Pallas kernels, middle(): pl.pallas_call(middle_kernel, in_specs=[hbm, hbm, v, hbm, hbm] + [v] * 6...  49 us
    pallas_call x1, Pallas kernels, attend_fwd_and_gather(): pl.pallas_call(attend_fwd_kernel_hosting, grid=(pairs,), in_specs=[block(...  41.5 us
    pallas_call x1, Pallas kernels, mlp_bwd(): pl.pallas_call(mlp_bwd_kernel, grid=(fold,), in_specs=[hbm, whole, tile,...  34.8 us
    pallas_call x1, Pallas kernels, mlp_fwd(): pl.pallas_call(mlp_fwd_kernel, grid=(fold,), in_specs=[whole, whole, at(l...  29.9 us
    unnamed x105, local copies, waits for them, and re-layouts  15.8 us
  transfers between devices with their start and end apart: 2, of which 0 were waited for; matrix products, arithmetic and copies ran while one was open for 10% of the time, Pallas kernels for 55%

profile of v8, /device:TPU:0, one launch (start us, length us, event | category | flops | bytes accessed | tf_op | source)
XLA Modules:
  0.0 423.1 jit_solution(13567929354005352253)
XLA Ops:
  7.3 1.3 copy.70
  9.2 1.0 reshape.298
  12.7 69.9 %shard_map.398 = (bf16[2,2,2,4,24,2304]{5,4,3,2,1,0:T(8,128)(2,1)}, bf16[2,2,2,4,16,128]{5,4,3,2,1,0:T(8,128)(2,1)}, bf16[2,2,2,4,24,2304]{5,4,3,2,1,0:T(8,128)(2,1)}, bf16[4,256,768]{2,1,0:T(8,128)(2,1)}) custom-call(bf16[24,2304]{1,0:T(8,128)(2,1)} %refs_0_.1, bf16[16,128]{1,0:T(8,128)(2,1)} %pad_bitcast_fusion.refs_1_, ...), custom_call_target="tpu_custom_call" | custom-call | tf_op jit(solution)/shard_map/pallas_call | solution.py:611
  82.6 0.9 copy.108
  86.0 0.8 reshape.300.vec_ref.ivec_ref
  88.0 3.3 slice.144
  94.2 5.4 %convolution_convert_fusion.q_ref.k_ref.v_ref = bf16[1024,2304]{1,0:T(8,128)(2,1)} fusion(bf16[1024,768]{1,0:T(8,128)(2,1)S(1)} %bitcast.121, bf16[768,2304]{1,0:T(8,128)(2,1)S(1)} %bitcast.119), kind=kOutput, calls=%fused_computation | convolution fusion | flops 3626237952 | bytes 9830400 | tf_op jit(solution)/shard_map/dot_general | solution.py:18
  99.6 41.5 %shard_map.399 = (bf16[1024,768]{1,0:T(8,128)(2,1)S(1)}, f32[6,2,1024]{2,1,0:T(2,128)S(1)}, bf16[2,2,2,4,24,3328]{5,4,3,2,1,0:T(8,128)(2,1)}, bf16[2,2,2,96,1536...) custom-call(bf16[1024,2304]{1,0:T(8,128)(2,1)} %convolution_convert_fusion.q_ref.k_ref.v_ref, ...), custom_call_target="tpu_custom_call" | custom-call | tf_op jit(solution)/shard_map/pallas_call | solution.py:1242
  141.1 1.2 copy-done
  142.3 1.4 copy-done.1
  144.3 1.1 constant_dynamic-slice_fusion.outs_ref
  145.5 29.9 %shard_map.400 = (f32[1024,768]{1,0:T(8,128)}, bf16[1024,768]{1,0:T(8,128)(2,1)}, bf16[1024,3072]{1,0:T(8,128)(2,1)}, bf16[1024,3072]{1,0:T(8,128)(2,1)}, f32[10...) custom-call(bf16[1024,768]{1,0:T(8,128)(2,1)} %bitcast.108, ...), custom_call_target="tpu_custom_call", output_to_operand_aliasing={{6}: (7, {})} | custom-call | tf_op jit(solution)/shard_map/pallas_call | solution.py:1308
  175.4 49.0 %shard_map.401 = (f32[1024,768]{1,0:T(8,128)}, bf16[1024,768]{1,0:T(8,128)(2,1)S(1)}, bf16[80,768]{1,0:T(8,128)(2,1)S(1)}, f32[24,768]{1,0:T(8,128)S(1)}, f32[64...) custom-call(bf16[1024,768]{1,0:T(8,128)(2,1)} %get-tuple-element.79.final_in, ...), custom_call_target="tpu_custom_call" | custom-call | tf_op jit(solution)/shard_map/pallas_call | solution.py:895
  224.4 1.2 copy-done.2
  226.3 34.8 %shard_map.402 = (bf16[768,3072]{1,0:T(8,128)(2,1)}, bf16[768,3840]{1,0:T(8,128)(2,1)}, f32[1024,768]{1,0:T(8,128)}, bf16[1024,768]{1,0:T(8,128)(2,1)}, f32[6,2,...) custom-call(f32[1024,768]{1,0:T(8,128)} %get-tuple-element.85.dy_ref, bf16[1024,768]{1,0:T(8,128)(2,1)} %copy-done.2, ...), custom_call_target="tpu_custom_call" | custom-call | tf_op jit(solution)/shard_map/pallas_call | solution.py:1396
  261.4 1.1 copy-done.9
  262.5 1.8 add_convert_fusion.normed_ref
  266.4 52.9 %shard_map.403 = (bf16[1024,768]{1,0:T(8,128)(2,1)}, bf16[1024,768]{1,0:T(8,128)(2,1)}, bf16[1024,768]{1,0:T(8,128)(2,1)}, f32[24,3072]{1,0:T(8,128)}, bf16[2,2,2,4,80,768]{5,4,3,2,1,0:T(8,128)(2,1)}) custom-call(bf16[1024,2304]{1,0:T(8,128)(2,1)} %convolution_convert_fusion.q_ref.k_ref.v_ref, bf16[1024,2304]{1,0:T(8,128)(2,1)} %convolution_convert_fusion.q_ref.k_ref.v_ref, ...), custom_call_target="tpu_custom_call" | custom-call | tf_op jit(solution)/shard_map/pallas_call | solution.py:1158
  320.0 69.7 %shard_map.404 = (f32[24,2560]{1,0:T(8,128)}, bf16[4,256,768]{2,1,0:T(8,128)(2,1)}, f32[4,24,768]{2,1,0:T(8,128)}, f32[4,24,768]{2,1,0:T(8,128)}, f32[96,768]{1,...) custom-call(bf16[1024,768]{1,0:T(8,128)(2,1)} %get-tuple-element.96., ...), custom_call_target="tpu_custom_call" | custom-call | tf_op jit(solution)/shard_map/pallas_call | solution.py:1554
  389.7 1.1 maximum_bitcast_fusion
  391.0 0.9 reshape.326
  391.8 0.8 mul.106
  392.8 1.3 fusion.6
  394.4 0.9 copy.80
  395.5 0.8 broadcast_multiply_fusion.1
  398.1 1.9 convert_element_type.68
  400.5 1.1 reshape.325
  402.0 1.1 reshape.328
  405.3 1.2 copy.84
  408.9 0.9 slice.152
  409.8 0.8 reshape.322
  410.6 1.4 slice.150
  (200 shorter events, 25.3 us)
Async XLA Ops:
  7.2 3.9 copy-start.35
  7.2 4.0 copy-start.36
  7.2 4.1 copy-start.37
  7.2 4.1 copy-start.38
  7.2 4.1 copy-start.39
  7.2 4.8 %copy-start.31 = (bf16[24,768]{1,0:T(8,128)(2,1)S(1)}, bf16[24,768]{1,0:T(8,128)(2,1)}, u32[]{:S(2)}) copy-start(bf16[24,768]{1,0:T(8,128)(2,1)} %param.27) | copy-start | bytes 110596
  7.3 4.8 %copy-start.29 = (bf16[24,768]{1,0:T(8,128)(2,1)S(1)}, bf16[24,768]{1,0:T(8,128)(2,1)}, u32[]{:S(2)}) copy-start(bf16[24,768]{1,0:T(8,128)(2,1)} %param.34) | copy-start | bytes 110596
  7.3 4.8 %copy-start.30 = (bf16[24,768]{1,0:T(8,128)(2,1)S(1)}, bf16[24,768]{1,0:T(8,128)(2,1)}, u32[]{:S(2)}) copy-start(bf16[24,768]{1,0:T(8,128)(2,1)} %param.39) | copy-start | bytes 110596
  7.3 76.9 %copy-start.23 = (bf16[24,2304]{1,0:T(8,128)(2,1)S(1)}, bf16[24,2304]{1,0:T(8,128)(2,1)}, u32[]{:S(2)}) copy-start(bf16[24,2304]{1,0:T(8,128)(2,1)} %param.38) | copy-start | bytes 331780
  7.3 138.2 %all-gather.2.cloned.1.call-start = ((), (), s32[]{:S(2)}) async-start(), calls=%async_computation.1 | async-start | bytes 9732096 | tf_op jit(solution)/shard_map/all_gather | solution.py:1707
  8.7 75.7 %copy-start.19 = (bf16[24,3072]{1,0:T(8,128)(2,1)S(1)}, bf16[24,3072]{1,0:T(8,128)(2,1)}, u32[]{:S(2)}) copy-start(bf16[24,3072]{1,0:T(8,128)(2,1)} %param.35) | copy-start | bytes 442372
  9.2 75.6 %copy-start.20 = (bf16[24,3072]{1,0:T(8,128)(2,1)S(1)}, bf16[24,3072]{1,0:T(8,128)(2,1)}, u32[]{:S(2)}) copy-start(bf16[24,3072]{1,0:T(8,128)(2,1)} %param.40) | copy-start | bytes 442372
  11.0 74.4 %copy-start.32 = (bf16[24,768]{1,0:T(8,128)(2,1)S(1)}, bf16[24,768]{1,0:T(8,128)(2,1)}, u32[]{:S(2)}) copy-start(bf16[24,768]{1,0:T(8,128)(2,1)} %param.44) | copy-start | bytes 110596
  11.1 74.5 %copy-start.18 = (bf16[24,768]{1,0:T(8,128)(2,1)S(1)}, bf16[24,768]{1,0:T(8,128)(2,1)}, u32[]{:S(2)}) copy-start(bf16[24,768]{1,0:T(8,128)(2,1)} %param.32) | copy-start | bytes 110596
  11.1 397.8 %reduce-scatter.2.cloned.1.call-start = ((), (), s32[]{:S(2)}) async-start(), calls=%async_computation.2 | async-start | bytes 6082560 | tf_op jit(solution)/shard_map/reduce_scatter | solution.py:1739
  12.7 73.0 %copy-start.25 = (bf16[24,1536]{1,0:T(8,128)(2,1)S(1)}, bf16[24,1536]{1,0:T(8,128)(2,1)}, u32[]{:S(2)}) copy-start(bf16[24,1536]{1,0:T(8,128)(2,1)} %param.33) | copy-start | bytes 221188
  86.8 4.9 %copy-start.33 = (s32[32,32]{1,0:T(8,128)S(1)}, s32[32,32]{1,0:T(8,128)}, u32[]{:S(2)}) copy-start(s32[32,32]{1,0:T(8,128)} %param.25) | copy-start | bytes 12292
  88.0 4.2 copy-start.8
  94.2 5.4 %copy-start.5 = (bf16[4,16,768]{2,1,0:T(8,128)(2,1)S(1)}, bf16[4,16,768]{2,1,0:T(8,128)(2,1)}, u32[]{:S(2)}) copy-start(bf16[4,16,768]{2,1,0:T(8,128)(2,1)} %tokens_ref.1) | copy-start | bytes 294916
  145.5 29.9 %copy-start.3 = (f32[11,768]{1,0:T(8,128)S(1)}, f32[11,768]{1,0:T(8,128)}, u32[]{:S(2)}) copy-start(f32[11,768]{1,0:T(8,128)} %reshape.300.vec_ref.ivec_ref) | copy-start | bytes 101380
  145.5 29.9 %copy-start.7 = (f32[2]{0:T(128)S(1)}, f32[2]{0:T(128)}, u32[]{:S(2)}) copy-start(f32[2]{0:T(128)} %temp_ref.1) | copy-start | bytes 28
  389.7 6.8 %copy-start.17 = (f32[24,2560]{1,0:T(8,128)S(1)}, f32[24,2560]{1,0:T(8,128)}, u32[]{:S(2)}) copy-start(f32[24,2560]{1,0:T(8,128)} %get-tuple-element.107) | copy-start | bytes 737284
  389.7 8.4 %copy-start.11 = (bf16[4,256,768]{2,1,0:T(8,128)(2,1)S(1)}, bf16[4,256,768]{2,1,0:T(8,128)(2,1)}, u32[]{:S(2)}) copy-start(bf16[4,256,768]{2,1,0:T(8,128)(2,1)} %get-tuple-element.105) | copy-start | bytes 4718596
  392.8 7.2 %copy-start.16 = (f32[4,24,768]{2,1,0:T(8,128)S(1)}, f32[4,24,768]{2,1,0:T(8,128)}, u32[]{:S(2)}) copy-start(f32[4,24,768]{2,1,0:T(8,128)} %get-tuple-element.113) | copy-start | bytes 884740
  398.1 3.5 copy-start.15
  400.0 4.4 %copy-start.14 = (f32[24,3072]{1,0:T(8,128)S(1)}, f32[24,3072]{1,0:T(8,128)}, u32[]{:S(2)}) copy-start(f32[24,3072]{1,0:T(8,128)} %get-tuple-element.109) | copy-start | bytes 884740
  401.5 5.5 %copy-start.24 = (f32[2,96,128]{2,1,0:T(8,128)S(1)}, f32[2,96,128]{2,1,0:T(8,128)}, u32[]{:S(2)}) copy-start(f32[2,96,128]{2,1,0:T(8,128)} %get-tuple-element.114) | copy-start | bytes 294916
  404.6 8.2 %copy-start.28 = (f32[24,768]{1,0:T(8,128)S(1)}, f32[24,768]{1,0:T(8,128)}, u32[]{:S(2)}) copy-start(f32[24,768]{1,0:T(8,128)} %get-tuple-element.228) | copy-start | bytes 221188
  404.6 8.8 %copy-start.13 = (f32[96,768]{1,0:T(8,128)S(1)}, f32[96,768]{1,0:T(8,128)}, u32[]{:S(2)}) copy-start(f32[96,768]{1,0:T(8,128)} %get-tuple-element.231) | copy-start | bytes 884740
  404.6 9.5 %copy-start.27 = (f32[24,768]{1,0:T(8,128)S(1)}, f32[24,768]{1,0:T(8,128)}, u32[]{:S(2)}) copy-start(f32[24,768]{1,0:T(8,128)} %get-tuple-element.233) | copy-start | bytes 221188
  404.6 10.1 %copy-start.12 = (f32[96,768]{1,0:T(8,128)S(1)}, f32[96,768]{1,0:T(8,128)}, u32[]{:S(2)}) copy-start(f32[96,768]{1,0:T(8,128)} %get-tuple-element.236) | copy-start | bytes 884740
  405.3 10.1 %copy-start.26 = (f32[24,768]{1,0:T(8,128)S(1)}, f32[24,768]{1,0:T(8,128)}, u32[]{:S(2)}) copy-start(f32[24,768]{1,0:T(8,128)} %get-tuple-element.238) | copy-start | bytes 221188
  (10 other events, 15.3 us)
Sparse Core Ops, SparseCore 0:
  11.5 113.3 all-gather.1
  261.2 137.8 reduce-scatter.1
